TPU v7x, 256 devices: a whole 4x4x8 slice. The times are simulated.
256 devices in a mesh: ia: 4 (over x), ja: 8 (over y, core), ka: 8 (over z).
Axes of the slice: x: 4, y: 4, z: 8, core: 2. Of those that a mesh axis runs over, the one named last changes fastest.
Arguments:
- tensor: bfloat16 [64, 2048, 4096], P('ka', 'ia', 'ja'), may hold values from -6 to 6
- factor_b: float32 [32, 4096], P('ia', ('ja', 'ka')), may hold values from -0.09375 to 0.09375
- factor_c: float32 [32, 64], P(('ia', 'ja'), 'ka'), may hold values from -0.75 to 0.75
Outputs:
- factor_a_new: float32 [32, 2048], P('ja', ('ia', 'ka'))
- factor_b_new: float32 [32, 4096], P('ia', ('ja', 'ka'))
All inputs are finite; a program needn't handle non-finite values.
Results may differ from a plain program's by a relative error of at most 0.0033.
Values sent between devices are 32-bit elements; how exact they have to be, the bound alone decides.
No kernel may reach another device: no remote copies, remote signals or barrier semaphores. Data moves between devices by JAX's collectives and lax.ppermute only.
A program may use at most 64 MiB of HBM per device.

v0:
```python
import jax
import jax.numpy as jnp
from jax import lax
from jax.sharding import PartitionSpec as P

EPS = 1e-06
HIGH = lax.Precision.HIGHEST


def gram_of(block):
    return jnp.dot(block, block.T, precision=HIGH, preferred_element_type=jnp.float32)


def solve_with(normal, rhs):
    lower = jnp.linalg.cholesky(normal)
    return jax.scipy.linalg.cho_solve((lower, True), rhs)


def arrange(partial_rows, rows_split, cols_split):
    rank, width = partial_rows.shape
    grid = partial_rows.reshape(rows_split, rank // rows_split, cols_split, width // cols_split)
    return grid.transpose(0, 2, 1, 3).reshape(rank * cols_split, width // cols_split)


def assemble(pieces, rows_split, cols_split):
    count, height, width = pieces.shape
    grid = pieces.reshape(rows_split, cols_split, height, width)
    return grid.transpose(0, 2, 1, 3).reshape(rows_split * height, cols_split * width)


def scaled(raw, squares, total):
    return raw / jnp.sqrt(squares / total + EPS)[:, None]


def body(tensor, factor_b, factor_c):
    n_ia = lax.axis_size("ia")
    n_ja = lax.axis_size("ja")
    n_ka = lax.axis_size("ka")
    total_i = tensor.shape[1] * n_ia
    total_j = tensor.shape[2] * n_ja
    c_block = lax.all_gather(factor_c, ("ia", "ja"), axis=0, tiled=True)
    pieces = lax.all_gather(factor_b[None], ("ia", "ka"), axis=0, tiled=True)
    b_block = assemble(pieces, n_ia, n_ka)
    gram_b = lax.psum(gram_of(b_block), "ja")
    gram_c = lax.psum(gram_of(c_block), "ka")
    normal_a = gram_b * gram_c
    kr_a = (c_block[:, :, None] * b_block[:, None, :]).astype(jnp.bfloat16)
    partial_a = jnp.einsum("rkj,kij->ri", kr_a, tensor, preferred_element_type=jnp.float32)
    solved_a = solve_with(normal_a, partial_a)
    raw_a = lax.psum_scatter(
        arrange(solved_a, n_ja, n_ka), ("ja", "ka"), scatter_dimension=0, tiled=True
    )
    squares_a = lax.psum(jnp.sum(raw_a * raw_a, axis=1), ("ia", "ka"))
    local_a = scaled(raw_a, squares_a, total_i)
    pieces_a = lax.all_gather(local_a[None], ("ja", "ka"), axis=0, tiled=True)
    gathered_a = assemble(pieces_a, n_ja, n_ka)
    gram_a = lax.psum(gram_of(gathered_a), "ia")
    normal_b = gram_a * gram_c
    kr_b = (c_block[:, :, None] * gathered_a[:, None, :]).astype(jnp.bfloat16)
    partial_b = jnp.einsum("rki,kij->rj", kr_b, tensor, preferred_element_type=jnp.float32)
    solved_b = solve_with(normal_b, partial_b)
    raw_b = lax.psum_scatter(
        arrange(solved_b, n_ia, n_ka), ("ia", "ka"), scatter_dimension=0, tiled=True
    )
    squares_b = lax.psum(jnp.sum(raw_b * raw_b, axis=1), ("ja", "ka"))
    share_b = scaled(raw_b, squares_b, total_j)
    return (local_a, share_b)


def solution(mesh):
    return jax.shard_map(
        body,
        mesh=mesh,
        in_specs=(P("ka", "ia", "ja"), P("ia", ("ja", "ka")), P(("ia", "ja"), "ka")),
        out_specs=(P("ja", ("ia", "ka")), P("ia", ("ja", "ka"))),
        check_vma=False,
    )
```

profile of v0, /device:TPU:1, one launch (start us, length us, event | category | flops | bytes accessed | tf_op | source)
XLA Modules:
  0.0 714.9 jit_solution(10917909202712670892)
XLA Ops:
  7.2 23.1 %all-gather.2 = f32[32,1,8]{2,1,0:T(1,128)S(1)} all-gather(f32[1,1,8]{2,1,0:T(1,128)} %bitcast.70), channel_id=1, replica_groups=mesh['ia'=4,'ja'=8,'ka'=8] {'ia','ja'}, dimensions={0}, use_global_device_ids=true | all-gather | bytes 1056 | tf_op jit(solution)/shard_map/all_gather | solution.py:41
  30.6 25.8 %psum.36 = f32[32,32]{0,1:T(8,128)S(1)} all-reduce(f32[32,32]{0,1:T(8,128)S(1)} %fusion.17), channel_id=1, replica_groups=mesh['ia'=4,'ja'=8,'ka'=8] {'ka'}, use_global_device_ids=true, to_apply=%region_1.0 | all-reduce | flops 1024 | bytes 8192 | tf_op jit(solution)/shard_map/psum | solution.py:45
  56.3 31.6 %all-gather = f32[256,64]{1,0:T(8,128)S(1)} all-gather(f32[8,64]{1,0:T(8,128)} %param.7), channel_id=2, replica_groups=mesh['ia'=4,'ja'=8,'ka'=8] {'ia','ka'}, dimensions={0}, use_global_device_ids=true | all-gather | bytes 67584 | tf_op jit(solution)/shard_map/all_gather | solution.py:42
  88.3 37.3 %psum.35 = f32[32,32]{0,1:T(8,128)S(1)} all-reduce(f32[32,32]{0,1:T(8,128)S(1)} %fusion.16), channel_id=1, replica_groups=mesh['ia'=4,'ja'=8,'ka'=8] {'ja'}, use_global_device_ids=true, to_apply=%region_0.0 | all-reduce | flops 1024 | bytes 8192 | tf_op jit(solution)/shard_map/psum | solution.py:44
  125.7 2.9 cholesky.44
  129.3 0.7 fusion.4
  129.9 2.4 custom-call.8
  132.4 3.5 convolution_bitcast_fusion.1
  136.5 0.7 copy.26
  138.5 168.9 %all-reduce.5.cloned.1.call-done = f32[256,64]{1,0:T(8,128)} async-done(((f32[256,64]{1,0:T(8,128)}), f32[256,64]{1,0:T(8,128)}) %all-reduce.5.cloned.1.call-update) | async-done | bytes 65552
  307.4 0.8 multiply_reduce_fusion.1
  308.2 57.6 %psum.37 = f32[4]{0:T(128)S(1)} all-reduce(f32[4]{0:T(128)S(1)} %multiply_reduce_fusion.1), channel_id=1, replica_groups=mesh['ia'=4,'ja'=8,'ka'=8] {'ia','ka'}, use_global_device_ids=true, to_apply=%region_6.0 | all-reduce | flops 4 | bytes 32 | tf_op jit(solution)/shard_map/psum | solution.py:53
  365.9 0.7 fusion.31
  366.6 59.8 %all-gather.3 = f32[64,4,64]{2,1,0:T(4,128)S(1)} all-gather(f32[1,4,64]{2,1,0:T(4,128)S(1)} %fusion.31), channel_id=3, replica_groups=mesh['ia'=4,'ja'=8,'ka'=8] {'ja','ka'}, dimensions={0}, use_global_device_ids=true | all-gather | bytes 66560 | tf_op jit(solution)/shard_map/all_gather | solution.py:55
  426.7 3.1 convolution_bitcast_fusion
  429.8 10.8 %psum.38 = f32[32,32]{0,1:T(8,128)S(1)} all-reduce(f32[32,32]{0,1:T(8,128)S(1)} %fusion.18), channel_id=1, replica_groups=mesh['ia'=4,'ja'=8,'ka'=8] {'ia'}, use_global_device_ids=true, to_apply=%region_7.0 | all-reduce | flops 1024 | bytes 8192 | tf_op jit(solution)/shard_map/psum | solution.py:57
  440.7 2.9 cholesky.55
  444.9 2.4 custom-call.9
  447.9 0.7 copy.30
  449.9 134.0 %all-reduce.7.cloned.1.call-done = f32[256,64]{1,0:T(8,128)} async-done(((f32[256,64]{1,0:T(8,128)}), f32[256,64]{1,0:T(8,128)}) %all-reduce.7.cloned.1.call-update) | async-done | bytes 65552
  583.9 0.8 multiply_reduce_fusion
  584.6 1.3 dynamic-slice_divide_fusion.1
  586.0 120.8 %psum.39 = f32[8]{0:T(128)S(1)} all-reduce(f32[8]{0:T(128)S(1)} %multiply_reduce_fusion), channel_id=1, replica_groups=mesh['ia'=4,'ja'=8,'ka'=8] {'ja','ka'}, use_global_device_ids=true, to_apply=%region_10.13 | all-reduce | flops 8 | bytes 64 | tf_op jit(solution)/shard_map/psum | solution.py:65
  706.7 1.3 dynamic-slice_divide_fusion
  (37 shorter events, 5.4 us)
Async XLA Ops:
  7.2 130.1 %copy-start.1 = (u32[256]{0:T(256)S(1)}, u32[256]{0:T(256)}, u32[]{:S(2)}) copy-start(u32[256]{0:T(256)} %constant.49) | copy-start | bytes 3076
  7.2 300.2 %all-reduce.5.cloned.1.call-start = ((), (), s32[]{:S(2)}) async-start(), calls=%async_computation | async-start | bytes 262144
  135.9 312.7 %copy-start = (u32[256]{0:T(256)S(1)}, u32[256]{0:T(256)}, u32[]{:S(2)}) copy-start(u32[256]{0:T(256)} %constant.53) | copy-start | bytes 3076
  137.2 446.7 %all-reduce.7.cloned.1.call-start = ((), (), s32[]{:S(2)}) async-start(), calls=%async_computation.1 | async-start | bytes 262144
Sparse Core Ops, SparseCore 0:
  137.3 170.0 all-reduce.4
  448.8 135.0 all-reduce.6
where the time goes:
time: 723 us; the launch traced here: 715 us
  blocking collectives  367 us (51%)
  waiting for transfers between devices  303 us (42%)
  other arithmetic  18.4 us (3%)
  between operations  15.5 us (2%)
  matrix products  8.06 us (1%)
    unnamed x4, waiting for transfers between devices  303 us
    psum x1, blocking collectives, body(): squares_b = lax.psum(jnp.sum(raw_b * raw_b, axis=1), ('ja', 'ka'))  121 us
    all_gather x1, blocking collectives, body(): pieces_a = lax.all_gather(local_a[None], ('ja', 'ka'), axis=0, tiled=True)  59.8 us
    psum x1, blocking collectives, body(): squares_a = lax.psum(jnp.sum(raw_a * raw_a, axis=1), ('ia', 'ka'))  57.6 us
    psum x1, blocking collectives, body(): gram_b = lax.psum(gram_of(b_block), 'ja')  37.3 us
    all_gather x1, blocking collectives, body(): pieces = lax.all_gather(factor_b[None], ('ia', 'ka'), axis=0, tiled=True)  31.6 us
    psum x1, blocking collectives, body(): gram_c = lax.psum(gram_of(c_block), 'ka')  25.8 us
    all_gather x1, blocking collectives, body(): c_block = lax.all_gather(factor_c, ('ia', 'ja'), axis=0, tiled=True)  23.1 us
  transfers between devices with their start and end apart: 2, of which 2 were waited for; matrix products, arithmetic and copies ran while one was open for 0% of the time, Pallas kernels for 0%

commit v1 on v0

v1 whole, which is shorter than its diff:
```python
import jax
import jax.numpy as jnp
from jax import lax
from jax.experimental import pallas as pl
from jax.experimental.pallas import tpu as pltpu
from jax.sharding import PartitionSpec as P

EPS = 1e-06
HIGH = lax.Precision.HIGHEST
F32 = jnp.float32
RANK = 32
LANES = 128
NT = (((1,), (1,)), ((), ()))
VMEM = pl.BlockSpec(memory_space=pltpu.VMEM)


def iota(shape, axis):
    return lax.broadcasted_iota(jnp.int32, shape, axis)


def dot_nt(left, right):
    return lax.dot_general(left, right, NT, precision=HIGH, preferred_element_type=F32)


def split(x):
    high = x.astype(jnp.bfloat16)
    return high, (x - high.astype(F32)).astype(jnp.bfloat16)


def inverse(a):
    size = a.shape[0]
    rows, cols = iota(a.shape, 0), iota(a.shape, 1)
    for p in range(size):
        row, col = a[p : p + 1, :], a[:, p : p + 1]
        scale = 1.0 / a[p : p + 1, p : p + 1]
        row = jnp.where(cols[:1] == p, 1.0, row) * scale
        a = jnp.where(cols == p, 0.0, a) - col * row
        a = jnp.where(rows == p, row, a)
    return a


def gather_kernel(y_ref, t_ref, z_ref):
    lane = iota((8, LANES), 1)
    b_rows, c_rows = [], []
    for ia in range(4):
        parts = [y_ref[8 * ia + ka] for ka in range(8)]
        pairs = [
            jnp.where(lane < 64, parts[2 * q], pltpu.roll(parts[2 * q + 1], 64, 1))
            for q in range(4)
        ]
        b_rows.append(jnp.concatenate(pairs, axis=1))
        c_rows.append(sum(parts[1:], parts[0]))
    b = jnp.concatenate(b_rows, axis=0)
    c = jnp.concatenate(c_rows, axis=0)
    gram = dot_nt(b, jnp.concatenate([b, jnp.zeros((96, 512), F32)], axis=0))
    extra = jnp.where(iota((32, LANES), 1) < 64, gram, c)
    high, low = split(b)

    def placed(part, q):
        zeros = jnp.zeros((RANK, 512), jnp.bfloat16)
        return [part if n == q else zeros for n in range(4)]

    weights = jnp.concatenate(
        [jnp.concatenate(placed(high, q) + placed(low, q), axis=0) for q in range(4)], axis=1
    )
    for h in range(2):
        left = jnp.concatenate([t_ref[4 * h + q] for q in range(4)], axis=1)
        both = lax.dot_general(left, weights, NT, preferred_element_type=F32)
        y = both[:, :LANES] + both[:, LANES:]
        for ja in range(8):
            z_ref[ja, 64 * h : 64 * h + 64, :] = y[64 * ja : 64 * ja + 64]
    for ja in range(8):
        z_ref[ja, 128:160, :] = extra


def combine_kernel(z_ref, u_ref, inv_ref, gram_c_ref, c_ref):
    ka = lax.axis_index("ka")
    z = z_ref[0]
    for n in range(1, 8):
        z = z + z_ref[n]
    extra = z[128:160]
    c_all = pltpu.roll(extra, 64, 1)[:, :64]
    gram_c = dot_nt(c_all, c_all)
    gram_c_ref[...] = gram_c
    inv_ref[...] = inverse(extra[:, :32] * gram_c)
    c_here = pltpu.roll(extra, 64 - 8 * ka, 1)
    c_ref[...] = c_here
    c_t = c_here.T[:8]
    c_tiled = jnp.concatenate([c_t] * 4, axis=1)
    which = iota((8, LANES), 0) - iota((8, LANES), 1) // 32
    total = None
    for h in range(2):
        weight = jnp.sum(jnp.where(which == 4 * h, c_tiled, 0.0), axis=0, keepdims=True)
        term = z[64 * h : 64 * h + 64] * weight
        total = term if total is None else total + term
    total = total + pltpu.roll(total, 64, 1)
    total = total + pltpu.roll(total, 32, 1)
    group = iota((16, LANES), 1) // 32
    u = total[:16]
    for q in range(1, 4):
        u = jnp.where(group == q, total[16 * q : 16 * q + 16], u)
    for n in range(8):
        u_ref[n] = u


def solve_kernel(v_ref, inv_ref, x_ref):
    parity = lax.axis_index("ja") % 2
    u = v_ref[0]
    for n in range(1, 8):
        u = u + v_ref[n]
    m_t = jnp.concatenate([u] + [pltpu.roll(u, 128 - 32 * q, 1) for q in range(1, 4)], axis=0)
    m_t = m_t[:, :RANK]
    raw = dot_nt(inv_ref[...], jnp.concatenate([m_t, m_t], axis=0))
    raw = jnp.where(iota((RANK, LANES), 1) // 64 == parity, raw, 0.0)
    for n in range(8):
        x_ref[n] = raw


def second_kernel(x_ref, t_ref, c_ref, w_ref):
    a = jnp.concatenate([x_ref[2 * q] + x_ref[2 * q + 1] for q in range(4)], axis=1)
    zeros = jnp.zeros((RANK, 512), F32)
    extra = dot_nt(a, jnp.concatenate([zeros, zeros, a, zeros], axis=0))
    c = c_ref[...]
    highs, lows = [], []
    for k in range(8):
        high, low = split(a * c[:, k : k + 1])
        highs.append(high)
        lows.append(low)
    left = jnp.concatenate([jnp.concatenate(highs, axis=1), jnp.concatenate(lows, axis=1)], axis=0)
    both = jnp.dot(left, t_ref[...].reshape(4096, 512), preferred_element_type=F32)
    out = both[:RANK] + both[RANK:]
    lane = iota((RANK, LANES), 1)
    for q in range(4):
        pair = out[:, 128 * q : 128 * q + 128]
        even = jnp.where(lane < 64, pair, extra)
        odd = jnp.where(lane < 64, pltpu.roll(pair, 64, 1), extra)
        for ia in range(4):
            w_ref[8 * ia + 2 * q] = even
            w_ref[8 * ia + 2 * q + 1] = odd


def second_solve_kernel(total_i, w_ref, gram_c_ref, raw_ref, scale_ref, ss_ref):
    s = w_ref[0]
    for n in range(1, 32):
        s = s + w_ref[n]
    gram = pltpu.roll(s, 64, 1)[:, :RANK] * 0.125
    diag = jnp.where(iota(gram.shape, 0) == iota(gram.shape, 1), gram, 0.0)
    scale_col = 1.0 / jnp.sqrt(jnp.sum(diag, axis=1, keepdims=True) / total_i + EPS)
    scale_row = 1.0 / jnp.sqrt(jnp.sum(diag, axis=0, keepdims=True) / total_i + EPS)
    inv = inverse(gram * scale_col * scale_row * gram_c_ref[...])
    scale_ref[...] = jnp.broadcast_to(scale_col, (RANK, LANES))
    m = jnp.where(iota(s.shape, 1) < 64, s, 0.0) * scale_col
    raw = jnp.dot(inv, m, precision=HIGH, preferred_element_type=F32)
    raw_ref[...] = raw
    ss = jnp.sum(raw * raw, axis=1, keepdims=True)
    eye = iota((RANK, LANES), 0) == iota((RANK, LANES), 1)
    ss_row = jnp.sum(jnp.where(eye, ss, 0.0), axis=0, keepdims=True)
    ss_ref[...] = jnp.broadcast_to(ss_row[None], ss_ref.shape)


def finish_kernel(total_j, ss_ref, raw_ref, scale_ref, x_ref, out_a_ref, out_b_ref):
    ia, ja, ka = lax.axis_index("ia"), lax.axis_index("ja"), lax.axis_index("ka")
    ss_row = jnp.sum(ss_ref[...], axis=0)
    eye = iota((RANK, LANES), 0) == iota((RANK, LANES), 1)
    ss = jnp.sum(jnp.where(eye, ss_row, 0.0), axis=1, keepdims=True)
    b = raw_ref[...] / jnp.sqrt(ss / total_j + EPS)
    out_b_ref[...] = pltpu.roll(b, 32 - 8 * ia, 0)[:8, :64]
    mine = x_ref[ka]
    mine = (mine + pltpu.roll(mine, 64, 1)) * scale_ref[...]
    out_a_ref[...] = pltpu.roll(mine, 32 - 4 * ja, 0)[:4, :64]


def call(kernel, outs, *args):
    return pl.pallas_call(
        kernel,
        out_shape=[jax.ShapeDtypeStruct(s, F32) for s in outs],
        in_specs=[VMEM] * len(args),
        out_specs=[VMEM] * len(outs),
        compiler_params=pltpu.CompilerParams(vmem_limit_bytes=32 * 1024 * 1024),
    )(*args)


def exchange(x, axes):
    return lax.all_to_all(x, axes, 0, 0, tiled=True)


def body(tensor, factor_b, factor_c):
    total_i = tensor.shape[1] * lax.axis_size("ia")
    total_j = tensor.shape[2] * lax.axis_size("ja")
    ja, ka = lax.axis_index("ja"), lax.axis_index("ka")
    row, lane = iota((8, 64), 0), iota((8, 64), 1)
    c_placed = jnp.where((row == ja) & (lane // 8 == ka), jnp.tile(factor_c, (1, 8)), 0.0)
    start = jnp.concatenate([factor_b, c_placed], axis=1)
    y = exchange(jnp.broadcast_to(start[None], (32, 8, LANES)), ("ia", "ka"))
    (z,) = call(gather_kernel, [(8, 160, LANES)], y, tensor)
    z = exchange(z, "ja")
    u, inv_a, gram_c, c_here = call(
        combine_kernel, [(8, 16, LANES), (RANK, RANK), (RANK, RANK), (RANK, LANES)], z
    )
    v = exchange(u, "ka")
    (x,) = call(solve_kernel, [(8, RANK, LANES)], v, inv_a)
    x = exchange(x, "ja")
    (w,) = call(second_kernel, [(32, RANK, LANES)], x, tensor, c_here)
    w = exchange(w, ("ia", "ka"))
    raw_b, scale_a, ss = call(
        lambda *refs: second_solve_kernel(total_i, *refs),
        [(RANK, LANES), (RANK, LANES), (64, 1, LANES)],
        w,
        gram_c,
    )
    ss = exchange(ss, ("ja", "ka"))
    out_a, out_b = call(
        lambda *refs: finish_kernel(total_j, *refs), [(4, 64), (8, 64)], ss, raw_b, scale_a, x
    )
    return out_a, out_b


def solution(mesh):
    return jax.shard_map(
        body,
        mesh=mesh,
        in_specs=(P("ka", "ia", "ja"), P("ia", ("ja", "ka")), P(("ia", "ja"), "ka")),
        out_specs=(P("ja", ("ia", "ka")), P("ia", ("ja", "ka"))),
        check_vma=False,
    )
```

time: 723 us -> 107 us (0.15); the launches traced: 715 us -> 107 us
  waiting for transfers between devices: 303 us -> 0 us
  blocking collectives: 367 us -> 92.8 us
  other arithmetic: 18.4 us -> 0.85 us
  between operations: 15.5 us -> 0.7 us
  Pallas kernels: 0 us -> 9.57 us
  matrix products: 8.06 us -> 0 us
    unnamed x4 -> x0, waiting for transfers between devices: 303 us -> none
    psum x5 -> x0, blocking collectives: 252 us -> none  [the longest x1 121 us: body(): squares_b = lax.psum(jnp.sum(raw_b * raw_b, axis=1), ('ja', 'ka'))]
    all_gather x3 -> x0, blocking collectives: 115 us -> none  [the longest x1 59.8 us: body(): pieces_a = lax.all_gather(local_a[None], ('ja', 'ka'), axis=0, tiled=True)]
    all_to_all x0 -> x6, blocking collectives: none -> 92.8 us  [exchange(): return lax.all_to_all(x, axes, 0, 0, tiled=True)]
    another operation x10 -> x0, other arithmetic: 13.4 us -> none  [the longest x6 7.19 us: solve_with(): lower = jnp.linalg.cholesky(normal)]
    pallas_call x0 -> x6, Pallas kernels: none -> 9.57 us  [call(): pl.pallas_call(kernel, out_shape=[jax.ShapeDtypeStruct(s, F32) for s in o...]
  transfers between devices with their start and end apart: 2 -> 0, of which waited for: 2 -> 0; matrix products, arithmetic and copies ran while one was open for 0% -> 0% of each run, Pallas kernels for 0% -> 0%
where the time goes in v1:
time: 107 us
  blocking collectives  92.8 us (87%)
  Pallas kernels  9.57 us (9%)
  local copies, waits for them, and re-layouts  2.94 us (3%)
    all_to_all x6, blocking collectives, exchange(): return lax.all_to_all(x, axes, 0, 0, tiled=True)  92.8 us
    pallas_call x6, Pallas kernels, call(): pl.pallas_call(kernel, out_shape=[jax.ShapeDtypeStruct(s, F32) for s in o...  9.57 us
    unnamed x4, local copies, waits for them, and re-layouts  2.19 us

profile of v1, /device:TPU:1, one launch (start us, length us, event | category | flops | bytes accessed | tf_op | source)
XLA Modules:
  0.0 106.9 jit_solution(2596371288868076366)
XLA Ops:
  0.7 0.7 tile.12
  1.3 0.1 tile.13
  1.4 0.1 fusion.1
  1.5 0.8 pad_maximum_fusion
  2.3 20.8 %all_to_all.30.y_ref = f32[32,8,128]{2,1,0:T(8,128)S(1)} all-to-all(f32[32,8,128]{2,1,0:T(8,128)S(1)} %broadcast_in_dim.20), channel_id=1, replica_groups=mesh['ia'=4,'ja'=8,'ka'=8] {'ia','ka'}, dimensions={0} | all-to-all | bytes 262144 | tf_op jit(solution)/shard_map/all_to_all | solution.py:184
  23.1 0.0 copy-start
  23.1 2.2 %copy-done = bf16[8,512,512]{2,1,0:T(8,128)(2,1)S(1)} copy-done((bf16[8,512,512]{2,1,0:T(8,128)(2,1)S(1)}, bf16[8,512,512]{2,1,0:T(8,128)(2,1)}, u32[]{:S(2)}) %copy-start) | copy-done | bytes 4194328
  25.3 0.0 copy-start.1
  25.3 1.4 %shard_map.50 = f32[8,160,128]{2,1,0:T(8,128)S(1)} custom-call(f32[32,8,128]{2,1,0:T(8,128)S(1)} %all_to_all.30.y_ref, bf16[8,512,512]{2,1,0:T(8,128)(2,1)S(1)} %copy-done), custom_call_target="tpu_custom_call" | custom-call | tf_op jit(solution)/shard_map/pallas_call | solution.py:174
  26.6 17.3 %all_to_all.31.z_ref = f32[8,160,128]{2,1,0:T(8,128)S(1)} all-to-all(f32[8,160,128]{2,1,0:T(8,128)S(1)} %shard_map.50), channel_id=1, replica_groups=mesh['ia'=4,'ja'=8,'ka'=8] {'ja'}, dimensions={0} | all-to-all | bytes 1310720 | tf_op jit(solution)/shard_map/all_to_all | solution.py:184
  43.9 2.9 %shard_map.51 = (f32[8,16,128]{2,1,0:T(8,128)S(1)}, f32[32,32]{1,0:T(8,128)S(1)}, f32[32,32]{1,0:T(8,128)S(1)}, f32[32,128]{1,0:T(8,128)S(1)}) custom-call(f32[8,160,128]{2,1,0:T(8,128)S(1)} %all_to_all.31.z_ref), custom_call_target="tpu_custom_call" | custom-call | tf_op jit(solution)/shard_map/pallas_call | solution.py:174
  46.9 9.7 %all_to_all.32.v_ref = f32[8,16,128]{2,1,0:T(8,128)S(1)} all-to-all(f32[8,16,128]{2,1,0:T(8,128)S(1)} %get-tuple-element.9), channel_id=1, replica_groups=mesh['ia'=4,'ja'=8,'ka'=8] {'ka'}, dimensions={0} | all-to-all | bytes 131072 | tf_op jit(solution)/shard_map/all_to_all | solution.py:184
  56.6 0.3 shard_map.52
  56.9 9.7 %all_to_all.33.x_ref.refs_3_ = f32[8,32,128]{2,1,0:T(8,128)S(1)} all-to-all(f32[8,32,128]{2,1,0:T(8,128)S(1)} %shard_map.52), channel_id=1, replica_groups=mesh['ia'=4,'ja'=8,'ka'=8] {'ja'}, dimensions={0} | all-to-all | bytes 262144 | tf_op jit(solution)/shard_map/all_to_all | solution.py:184
  66.5 0.0 copy-done.1
  66.5 1.1 %shard_map.53 = f32[32,32,128]{2,1,0:T(8,128)S(1)} custom-call(f32[8,32,128]{2,1,0:T(8,128)S(1)} %all_to_all.33.x_ref.refs_3_, bf16[8,512,512]{2,1,0:T(8,128)(2,1)S(1)} %copy-done.1, f32[32,128]{1,0:T(8,128)S(1)} %get-tuple-element.11.c_ref), custom_call_target="tpu_custom_call" | custom-call | tf_op jit(solution)/shard_map/pallas_call | solution.py:174
  67.6 17.4 %all_to_all.34.refs_0_ = f32[32,32,128]{2,1,0:T(8,128)S(1)} all-to-all(f32[32,32,128]{2,1,0:T(8,128)S(1)} %shard_map.53), channel_id=1, replica_groups=mesh['ia'=4,'ja'=8,'ka'=8] {'ia','ka'}, dimensions={0} | all-to-all | bytes 1048576 | tf_op jit(solution)/shard_map/all_to_all | solution.py:184
  85.1 3.1 %shard_map.54 = (f32[32,128]{1,0:T(8,128)S(1)}, f32[32,128]{1,0:T(8,128)S(1)}, f32[64,1,128]{2,1,0:T(1,128)S(1)}) custom-call(f32[32,32,128]{2,1,0:T(8,128)S(1)} %all_to_all.34.refs_0_, f32[32,32]{1,0:T(8,128)S(1)} %get-tuple-element.12.refs_1_), custom_call_target="tpu_custom_call" | custom-call | tf_op jit(solution)/shard_map/pallas_call | solution.py:174
  88.2 17.9 %all_to_all.35.refs_0_ = f32[64,1,128]{2,1,0:T(1,128)S(1)} all-to-all(f32[64,1,128]{2,1,0:T(1,128)S(1)} %get-tuple-element.13), channel_id=1, replica_groups=mesh['ia'=4,'ja'=8,'ka'=8] {'ja','ka'}, dimensions={0} | all-to-all | bytes 65536 | tf_op jit(solution)/shard_map/all_to_all | solution.py:184
  106.1 0.8 shard_map.55
  (4 shorter events, 0.0 us)
Async XLA Ops:
  23.1 2.2 %copy-start = (bf16[8,512,512]{2,1,0:T(8,128)(2,1)S(1)}, bf16[8,512,512]{2,1,0:T(8,128)(2,1)}, u32[]{:S(2)}) copy-start(bf16[8,512,512]{2,1,0:T(8,128)(2,1)} %t_ref.3) | copy-start | bytes 12582916
  25.3 41.3 %copy-start.1 = (bf16[8,512,512]{2,1,0:T(8,128)(2,1)S(1)}, bf16[8,512,512]{2,1,0:T(8,128)(2,1)}, u32[]{:S(2)}) copy-start(bf16[8,512,512]{2,1,0:T(8,128)(2,1)} %t_ref.3) | copy-start | bytes 12582916

commit v2 on v1

v2 whole, which is shorter than its diff:
```python
import jax
import jax.numpy as jnp
from jax import lax
from jax.experimental import pallas as pl
from jax.experimental.pallas import tpu as pltpu
from jax.sharding import PartitionSpec as P

EPS = 1e-06
HIGH = lax.Precision.HIGHEST
F32 = jnp.float32
RANK = 32
LANES = 128
NT = (((1,), (1,)), ((), ()))
VMEM = pl.BlockSpec(memory_space=pltpu.VMEM)
HBM = pl.BlockSpec(memory_space=pltpu.HBM)
KEPT = 6


def iota(shape, axis):
    return lax.broadcasted_iota(jnp.int32, shape, axis)


def dot_nt(left, right):
    return lax.dot_general(left, right, NT, precision=HIGH, preferred_element_type=F32)


def split(x):
    high = x.astype(jnp.bfloat16)
    return high, (x - high.astype(F32)).astype(jnp.bfloat16)


def fold(x):
    n = x.shape[0] // 4
    group = iota((n, LANES), 1) // 32
    out = x[:n]
    for q in range(1, 4):
        out = jnp.where(group == q, x[n * q : n * q + n], out)
    return out


def unfold(x):
    parts = [x] + [pltpu.roll(x, LANES - 32 * q, 1) for q in range(1, 4)]
    return jnp.concatenate(parts, axis=0)[:, :32]


def total(ref, *index):
    out = ref[(0, *index)]
    for n in range(1, ref.shape[0]):
        out = out + ref[(n, *index)]
    return out


def folded_gram(x):
    return fold(dot_nt(x, jnp.concatenate([x] * 4, axis=0)))


def inverse(a):
    size = a.shape[0]
    rows, cols = iota(a.shape, 0), iota(a.shape, 1)
    for p in range(size):
        row, col = a[p : p + 1, :], a[:, p : p + 1]
        scale = 1.0 / a[p : p + 1, p : p + 1]
        row = jnp.where(cols[:1] == p, 1.0, row) * scale
        a = jnp.where(cols == p, 0.0, a) - col * row
        a = jnp.where(rows == p, row, a)
    return a


def fetch(t_ref, places, sems):
    copies = [
        pltpu.make_async_copy(t_ref.at[KEPT + n], places.at[n], sems.at[n])
        for n in range(t_ref.shape[0] - KEPT)
    ]
    for copy in copies:
        copy.start()
    return copies


def load_kernel(t_ref, *refs):
    sems = refs[-1]
    copies = [pltpu.make_async_copy(t_ref.at[k], refs[k], sems.at[k]) for k in range(KEPT)]
    for copy in copies:
        copy.start()
    for copy in copies:
        copy.wait()


def start_kernel(b_hbm, c_hbm, y_ref, b_ref, c_ref, sems):
    copies = [
        pltpu.make_async_copy(b_hbm, b_ref, sems.at[0]),
        pltpu.make_async_copy(c_hbm, c_ref, sems.at[1]),
    ]
    for copy in copies:
        copy.start()
    for copy in copies:
        copy.wait()
    ja, ka = lax.axis_index("ja"), lax.axis_index("ka")
    row, lane = iota((8, LANES), 0), iota((8, LANES), 1)
    c_tiled = jnp.concatenate([c_ref[...]] * 16, axis=1)
    c_placed = jnp.where((row == ja) & (lane // 8 == 8 + ka), c_tiled, 0.0)
    b_wide = jnp.concatenate([b_ref[...], jnp.zeros((8, 64), F32)], axis=1)
    tile = jnp.where(lane < 64, b_wide, c_placed)
    for n in range(32):
        y_ref[n] = tile


def first_kernel(t_hbm, y_ref, *refs):
    keep_ref, send_ref, scratch, rest, sems = refs[KEPT:]
    copies = fetch(t_hbm, rest, sems)
    steps = [*refs[:KEPT], *(rest.at[n] for n in range(8 - KEPT))]
    core = lax.axis_index("ja") % 2
    lane = iota((8, LANES), 1)
    b_rows, c_rows = [], []
    for ia in range(4):
        parts = [y_ref[8 * ia + ka] for ka in range(8)]
        pairs = [
            jnp.where(lane < 64, parts[2 * q], pltpu.roll(parts[2 * q + 1], 64, 1))
            for q in range(4)
        ]
        b_rows.append(jnp.concatenate(pairs, axis=1))
        c_rows.append(sum(parts[1:], parts[0]))
    b = jnp.concatenate(b_rows, axis=0)
    c = jnp.concatenate(c_rows, axis=0)
    gram = dot_nt(b, jnp.concatenate([b, jnp.zeros((96, 512), F32)], axis=0))
    extra = jnp.where(iota((32, LANES), 1) < 64, gram, c)
    high, low = split(b)

    def placed(part, q):
        zeros = jnp.zeros((RANK, 512), jnp.bfloat16)
        return [part if n == q else zeros for n in range(4)]

    weights = jnp.concatenate(
        [jnp.concatenate(placed(high, q) + placed(low, q), axis=0) for q in range(4)], axis=1
    )
    for h in range(2):
        if h == 1:
            for copy in copies:
                copy.wait()
        left = jnp.concatenate([steps[4 * h + q][...] for q in range(4)], axis=1)
        both = lax.dot_general(left, weights, NT, preferred_element_type=F32)
        scratch[h] = both[:, :LANES] + both[:, LANES:]
    for n in range(4):
        for ref, which in ((keep_ref, core), (send_ref, 1 - core)):
            start = pl.multiple_of(64 * (2 * n + which), 64)
            for h in range(2):
                ref[n, 64 * h : 64 * h + 64, :] = scratch[h, pl.ds(start, 64), :]
            ref[n, 128:160, :] = extra


def combine_kernel(z_ref, u_ref, gram_ref, c_all_ref, c_ref):
    ka = lax.axis_index("ka")
    z = total(z_ref)
    extra = z[128:160]
    gram_ref[...] = extra[:, :32]
    c_all_ref[...] = pltpu.roll(extra, 64, 1)[:, :64]
    c_here = pltpu.roll(extra, 64 - 8 * ka, 1)
    c_ref[...] = c_here
    c_t = c_here.T[:8]
    c_tiled = jnp.concatenate([c_t] * 4, axis=1)
    which = iota((8, LANES), 0) - iota((8, LANES), 1) // 32
    acc = None
    for h in range(2):
        weight = jnp.sum(jnp.where(which == 4 * h, c_tiled, 0.0), axis=0, keepdims=True)
        term = z[64 * h : 64 * h + 64] * weight
        acc = term if acc is None else acc + term
    acc = acc + pltpu.roll(acc, 64, 1)
    acc = acc + pltpu.roll(acc, 32, 1)
    u = fold(acc)
    for n in range(8):
        u_ref[n] = u


def invert_a_kernel(gram_b_ref, c_all_ref, inv_ref, gram_c_ref):
    gram_c = dot_nt(c_all_ref[...], c_all_ref[...])
    gram_c_ref[...] = gram_c
    inv_ref[...] = inverse(gram_b_ref[...] * gram_c)


def solve_kernel(v_ref, inv_ref, x_ref):
    parity = lax.axis_index("ja") % 2
    m_t = unfold(total(v_ref))
    raw = dot_nt(inv_ref[...], jnp.concatenate([m_t, m_t], axis=0))
    raw = jnp.where(iota((RANK, LANES), 1) // 64 == parity, raw, 0.0)
    for n in range(8):
        x_ref[n] = raw


def second_kernel(t_hbm, x_ref, c_ref, *refs):
    w_ref, g_ref, rest, sems = refs[KEPT:]
    copies = fetch(t_hbm, rest, sems)
    steps = [*refs[:KEPT], *(rest.at[n] for n in range(8 - KEPT))]
    a = jnp.concatenate([x_ref[2 * q] + x_ref[2 * q + 1] for q in range(4)], axis=1)
    g_ref[...] = folded_gram(a)
    c = c_ref[...]
    highs, lows = [], []
    for k in range(8):
        high, low = split(a * c[:, k : k + 1])
        highs.append(high)
        lows.append(low)
    left = jnp.concatenate([jnp.concatenate(highs, axis=1), jnp.concatenate(lows, axis=1)], axis=0)
    for copy in copies:
        copy.wait()
    right = jnp.concatenate([ref[...] for ref in steps], axis=0)
    both = jnp.dot(left, right, preferred_element_type=F32)
    out = both[:RANK] + both[RANK:]
    low_lanes = iota((16, LANES), 1) < 64
    for q in range(4):
        pair = out[:, 128 * q : 128 * q + 128]
        turned = pltpu.roll(pair, 64, 1)
        even = jnp.where(low_lanes, pair[:16], turned[16:])
        odd = jnp.where(low_lanes, turned[:16], pair[16:])
        for ia in range(4):
            w_ref[8 * ia + 2 * q] = even
            w_ref[8 * ia + 2 * q + 1] = odd


def invert_b_kernel(total_i, g0_ref, g1_ref, g2_ref, g3_ref, gram_c_ref, inv_ref, scale_ref):
    gram = unfold((g0_ref[...] + g1_ref[...]) + (g2_ref[...] + g3_ref[...]))
    diag = jnp.where(iota(gram.shape, 0) == iota(gram.shape, 1), gram, 0.0)
    scale_col = 1.0 / jnp.sqrt(jnp.sum(diag, axis=1, keepdims=True) / total_i + EPS)
    scale_row = 1.0 / jnp.sqrt(jnp.sum(diag, axis=0, keepdims=True) / total_i + EPS)
    inv_ref[...] = inverse(gram * scale_col * scale_row * gram_c_ref[...])
    scale_ref[...] = jnp.broadcast_to(scale_col, (RANK, LANES))


def second_solve_kernel(w_ref, inv_ref, scale_ref, raw_ref, ss_ref):
    s = total(w_ref)
    m = jnp.concatenate([s, pltpu.roll(s, 64, 1)], axis=0) * scale_ref[...]
    raw = jnp.dot(inv_ref[...], m, precision=HIGH, preferred_element_type=F32)
    raw_ref[...] = raw
    square = jnp.where(iota(raw.shape, 1) < 64, raw * raw, 0.0)
    ss = jnp.sum(square, axis=1, keepdims=True)
    eye = iota((RANK, LANES), 0) == iota((RANK, LANES), 1)
    ss_row = jnp.sum(jnp.where(eye, ss, 0.0), axis=0, keepdims=True)
    ss_ref[...] = jnp.broadcast_to(ss_row, ss_ref.shape)


def finish_kernel(total_j, ss_ref, raw_ref, scale_ref, x_ref, out_a_ref, out_b_ref):
    ia, ja, ka = lax.axis_index("ia"), lax.axis_index("ja"), lax.axis_index("ka")
    ss_row = jnp.sum(ss_ref[...], axis=0, keepdims=True)
    eye = iota((RANK, LANES), 0) == iota((RANK, LANES), 1)
    ss = jnp.sum(jnp.where(eye, ss_row, 0.0), axis=1, keepdims=True)
    b = raw_ref[...] / jnp.sqrt(ss / total_j + EPS)
    out_b_ref[...] = pltpu.roll(b, 32 - 8 * ia, 0)[:8, :64]
    mine = x_ref[ka]
    mine = (mine + pltpu.roll(mine, 64, 1)) * scale_ref[...]
    out_a_ref[...] = pltpu.roll(mine, 32 - 4 * ja, 0)[:4, :64]


def call(kernel, outs, *args, scratch=()):
    big = [a.ndim == 3 and a.dtype == jnp.bfloat16 for a in args]
    return pl.pallas_call(
        kernel,
        out_shape=[jax.ShapeDtypeStruct(s, F32) for s in outs],
        in_specs=[HBM if flag else VMEM for flag in big],
        out_specs=[VMEM] * len(outs),
        scratch_shapes=scratch,
        compiler_params=pltpu.CompilerParams(vmem_limit_bytes=32 * 1024 * 1024),
    )(*args)


def load(tensor):
    step = tensor.shape[1:]
    return pl.pallas_call(
        load_kernel,
        out_shape=[pltpu.VMEM(step, tensor.dtype)] * KEPT,
        in_specs=[HBM],
        out_specs=[VMEM] * KEPT,
        scratch_shapes=[pltpu.SemaphoreType.DMA((KEPT,))],
        compiler_params=pltpu.CompilerParams(vmem_limit_bytes=32 * 1024 * 1024),
    )(tensor)


def rest_scratch(tensor):
    count = tensor.shape[0] - KEPT
    return [
        pltpu.VMEM((count, *tensor.shape[1:]), tensor.dtype),
        pltpu.SemaphoreType.DMA((count,)),
    ]


def exchange(x, axes, groups=None):
    return lax.all_to_all(x, axes, 0, 0, tiled=True, axis_index_groups=groups)


def turned(x, axis, step):
    size = lax.axis_size(axis)
    return lax.ppermute(x, axis, [(n, (n + step) % size) for n in range(size)])


def body(tensor, factor_b, factor_c):
    total_i = tensor.shape[1] * lax.axis_size("ia")
    total_j = tensor.shape[2] * lax.axis_size("ja")
    tensor, factor_b, factor_c = (
        pltpu.with_memory_space_constraint(a, pltpu.HBM) for a in (tensor, factor_b, factor_c)
    )
    (y,) = pl.pallas_call(
        start_kernel,
        out_shape=[jax.ShapeDtypeStruct((32, 8, LANES), F32)],
        in_specs=[HBM, HBM],
        out_specs=[VMEM],
        scratch_shapes=[
            pltpu.VMEM(factor_b.shape, F32),
            pltpu.VMEM(factor_c.shape, F32),
            pltpu.SemaphoreType.DMA((2,)),
        ],
    )(factor_b, factor_c)
    y = exchange(y, ("ia", "ka"))
    steps = load(tensor)
    keep, send = call(
        first_kernel,
        [(4, 160, LANES), (4, 160, LANES)],
        tensor,
        y,
        *steps,
        scratch=[pltpu.VMEM((2, 512, LANES), F32), *rest_scratch(tensor)],
    )
    z = keep + lax.ppermute(send, "ja", [(n, n ^ 1) for n in range(8)])
    z = exchange(z, "ja", [[0, 2, 4, 6], [1, 3, 5, 7]])
    u, gram_b, c_all, c_here = call(
        combine_kernel, [(8, 16, LANES), (RANK, RANK), (RANK, 64), (RANK, LANES)], z
    )
    v = exchange(u, "ka")
    inv_a, gram_c = call(invert_a_kernel, [(RANK, RANK), (RANK, RANK)], gram_b, c_all)
    (x,) = call(solve_kernel, [(8, RANK, LANES)], v, inv_a)
    x = exchange(x, "ja")
    w, g = call(
        second_kernel,
        [(32, 16, LANES), (8, LANES)],
        tensor,
        x,
        c_here,
        *steps,
        scratch=rest_scratch(tensor),
    )
    w = exchange(w, ("ia", "ka"))
    inv_b, scale_a = call(
        lambda *refs: invert_b_kernel(total_i, *refs),
        [(RANK, RANK), (RANK, LANES)],
        g,
        *(turned(g, "ia", step) for step in (1, 2, 3)),
        gram_c,
    )
    raw_b, ss = call(second_solve_kernel, [(RANK, LANES), (64, LANES)], w, inv_b, scale_a)
    ss = exchange(ss.reshape(64, 1, LANES), ("ja", "ka")).reshape(64, LANES)
    out_a, out_b = call(
        lambda *refs: finish_kernel(total_j, *refs), [(4, 64), (8, 64)], ss, raw_b, scale_a, x
    )
    return out_a, out_b


def solution(mesh):
    return jax.shard_map(
        body,
        mesh=mesh,
        in_specs=(P("ka", "ia", "ja"), P("ia", ("ja", "ka")), P(("ia", "ja"), "ka")),
        out_specs=(P("ja", ("ia", "ka")), P("ia", ("ja", "ka"))),
        check_vma=False,
    )
```

time: 107 us -> 99.8 us (0.933)
  blocking collectives: 92.8 us -> 40.6 us
  starting transfers between devices: 0 us -> 24.9 us
  waiting for transfers between devices: 0 us -> 16.2 us
  Pallas kernels: 9.57 us -> 16.7 us
  local copies, waits for them, and re-layouts: 2.94 us -> 0 us
    all_to_all x6 -> x3, blocking collectives: 92.8 us -> 40.6 us  [exchange(): return lax.all_to_all(x, axes, 0, 0, tiled=True, axis_index_groups=groups)]
    all_to_all x0 -> x3, starting transfers between devices: none -> 19.1 us  [exchange(): return lax.all_to_all(x, axes, 0, 0, tiled=True, axis_index_groups=groups)]
    all_to_all x0 -> x3, waiting for transfers between devices: none -> 11.6 us  [exchange(): return lax.all_to_all(x, axes, 0, 0, tiled=True, axis_index_groups=groups)]
    ppermute x0 -> x4, starting transfers between devices: none -> 5.82 us  [the longest x3 3.66 us: turned(): return lax.ppermute(x, axis, [(n, (n + step) % size) for n in range(size)])]
    ppermute x0 -> x4, waiting for transfers between devices: none -> 4.59 us  [the longest x3 3.33 us: turned(): return lax.ppermute(x, axis, [(n, (n + step) % size) for n in range(size)])]
    pallas_call x6 -> x8, Pallas kernels: 9.57 us -> 13.4 us  [call(): pl.pallas_call(kernel, out_shape=[jax.ShapeDtypeStruct(s, F32) for s in o...]
    pallas_call x0 -> x2, Pallas kernels: none -> 3.34 us  [the longest x1 1.89 us: load(): pl.pallas_call(load_kernel, out_shape=[pltpu.VMEM(step, tensor.dtype)] *...]
    unnamed x4 -> x0, local copies, waits for them, and re-layouts: 2.19 us -> none
  transfers between devices with their start and end apart: 0 -> 7, of which waited for: 0 -> 5; matrix products, arithmetic and copies ran while one was open for 0% -> 0% of each run, Pallas kernels for 0% -> 7%
where the time goes in v2:
time: 99.8 us; the launch traced here: 99.3 us
  blocking collectives  40.6 us (41%)
  starting transfers between devices  24.9 us (25%)
  Pallas kernels  16.7 us (17%)
  waiting for transfers between devices  16.2 us (16%)
    all_to_all x3, blocking collectives, exchange(): return lax.all_to_all(x, axes, 0, 0, tiled=True, axis_index_groups=groups)  40.6 us
    all_to_all x3, starting transfers between devices, exchange(): return lax.all_to_all(x, axes, 0, 0, tiled=True, axis_index_groups=groups)  19.1 us
    pallas_call x8, Pallas kernels, call(): pl.pallas_call(kernel, out_shape=[jax.ShapeDtypeStruct(s, F32) for s in o...  13.4 us
    all_to_all x3, waiting for transfers between devices, exchange(): return lax.all_to_all(x, axes, 0, 0, tiled=True, axis_index_groups=groups)  11.6 us
    ppermute x3, starting transfers between devices, turned(): return lax.ppermute(x, axis, [(n, (n + step) % size) for n in range(size)])  3.66 us
    ppermute x3, waiting for transfers between devices, turned(): return lax.ppermute(x, axis, [(n, (n + step) % size) for n in range(size)])  3.33 us
    ppermute x1, starting transfers between devices, body(): z = keep + lax.ppermute(send, 'ja', [(n, n ^ 1) for n in range(8)])  2.16 us
  transfers between devices with their start and end apart: 7, of which 5 were waited for; matrix products, arithmetic and copies ran while one was open for 0% of the time, Pallas kernels for 7%

profile of v2, /device:TPU:1, one launch (start us, length us, event | category | flops | bytes accessed | tf_op | source)
XLA Modules:
  0.0 99.3 jit_solution(15692518368926691018)
XLA Ops:
  0.6 1.5 %shard_map.50 = f32[32,8,128]{2,1,0:T(8,128)} custom-call(f32[8,64]{1,0:T(8,128)} %b_hbm.1, f32[1,8]{1,0:T(1,128)} %c_hbm.1), custom_call_target="tpu_custom_call" | custom-call | tf_op jit(solution)/shard_map/pallas_call | solution.py:297
  2.1 11.9 %all-to-all-start = ((f32[32,8,128]{2,1,0:T(8,128)}), f32[32,8,128]{2,1,0:T(8,128)S(1)}, u32[]{:S(2)}, u32[]{:S(2)}) async-start(f32[32,8,128]{2,1,0:T(8,128)} %shard_map.50), calls=%async_computation | async-start | bytes 262144 | tf_op jit(solution)/shard_map/all_to_all | solution.py:283
  14.0 1.9 %shard_map.51 = (bf16[512,512]{1,0:T(8,128)(2,1)S(1)}, bf16[512,512]{1,0:T(8,128)(2,1)S(1)}, bf16[512,512]{1,0:T(8,128)(2,1)S(1)}, bf16[512,512]{1,0:T(8,128)(2,...) custom-call(bf16[8,512,512]{2,1,0:T(8,128)(2,1)} %t_hbm.3), custom_call_target="tpu_custom_call" | custom-call | tf_op jit(solution)/shard_map/pallas_call | solution.py:264
  15.9 7.3 %all-to-all-done.y_ref = f32[32,8,128]{2,1,0:T(8,128)S(1)} async-done(((f32[32,8,128]{2,1,0:T(8,128)}), f32[32,8,128]{2,1,0:T(8,128)S(1)}, u32[]{:S(2)}, u32[]{:S(2)}) %all-to-all-start) | async-done | bytes 131104 | tf_op jit(solution)/shard_map/all_to_all | solution.py:283
  23.1 2.6 %shard_map.52 = (f32[4,160,128]{2,1,0:T(8,128)S(1)}, f32[4,160,128]{2,1,0:T(8,128)S(1)}) custom-call(bf16[8,512,512]{2,1,0:T(8,128)(2,1)} %t_hbm.3, f32[32,8,128]{2,1,0:T(8,128)S(1)} %all-to-all-done.y_ref, bf16[512,512]{1,0:T(8,128)(2,1)S(1)} %get-tuple-element.22.refs_0_, bf16[512,512]{1,0:T(8,128)(2,1)S(1)} %get-tuple-element.23.refs_1_, ...), custom_call_target="tpu_custom_call" | custom-call | tf_op jit(solution)/shard_map/pallas_call | solution.py:252
  25.7 2.2 %collective-permute-start = (f32[4,160,128]{2,1,0:T(8,128)S(1)}, f32[4,160,128]{2,1,0:T(8,128)S(1)}, u32[]{:S(2)}, u32[]{:S(2)}) collective-permute-start(f32[4,160,128]{2,1,0:T(8,128)S(1)} %get-tuple-element.29), channel_id=1, source_target_pairs={{0,8},{8,0},{16,24},{24,16},{32,40},{40,32},{48,56},{56,48},{1,9},... | collective-permute-start | bytes 983048 | tf_op jit(solution)/shard_map/ppermute | solution.py:318
  27.8 1.3 %collective-permute-done = f32[4,160,128]{2,1,0:T(8,128)S(1)} collective-permute-done((f32[4,160,128]{2,1,0:T(8,128)S(1)}, f32[4,160,128]{2,1,0:T(8,128)S(1)}, u32[]{:S(2)}, u32[]{:S(2)}) %collective-permute-start) | collective-permute-done | bytes 327712 | tf_op jit(solution)/shard_map/ppermute | solution.py:318
  29.2 10.8 %all_to_all.30.z_ref = f32[4,160,128]{2,1,0:T(8,128)S(1)} all-to-all(f32[4,160,128]{2,1,0:T(8,128)S(1)} %add.3), channel_id=1, replica_groups={{0,16,32,48},{8,24,40,56},{1,17,33,49},{9,25,41,57},{2,18,34,50},{10,26..., dimensions={0} | all-to-all | bytes 655360 | tf_op jit(solution)/shard_map/all_to_all | solution.py:283
  39.9 1.0 %shard_map.53 = (f32[8,16,128]{2,1,0:T(8,128)}, f32[32,32]{1,0:T(8,128)S(1)}, f32[32,64]{1,0:T(8,128)S(1)}, f32[32,128]{1,0:T(8,128)S(1)}) custom-call(f32[4,160,128]{2,1,0:T(8,128)S(1)} %all_to_all.30.z_ref), custom_call_target="tpu_custom_call" | custom-call | tf_op jit(solution)/shard_map/pallas_call | solution.py:252
  40.9 3.3 %all-to-all-start.2 = ((f32[8,16,128]{2,1,0:T(8,128)}), f32[8,16,128]{2,1,0:T(8,128)S(1)}, u32[]{:S(2)}, u32[]{:S(2)}) async-start(f32[8,16,128]{2,1,0:T(8,128)} %get-tuple-element.30), calls=%async_computation.2 | async-start | bytes 131072 | tf_op jit(solution)/shard_map/all_to_all | solution.py:283
  44.3 2.8 %shard_map.54 = (f32[32,32]{1,0:T(8,128)S(1)}, f32[32,32]{1,0:T(8,128)S(1)}) custom-call(f32[32,32]{1,0:T(8,128)S(1)} %get-tuple-element.31.gram_b_ref, f32[32,64]{1,0:T(8,128)S(1)} %get-tuple-element.32.c_all_ref), custom_call_target="tpu_custom_call" | custom-call | tf_op jit(solution)/shard_map/pallas_call | solution.py:252
  47.1 4.4 %all-to-all-done.2.v_ref = f32[8,16,128]{2,1,0:T(8,128)S(1)} async-done(((f32[8,16,128]{2,1,0:T(8,128)}), f32[8,16,128]{2,1,0:T(8,128)S(1)}, u32[]{:S(2)}, u32[]{:S(2)}) %all-to-all-start.2) | async-done | bytes 65568 | tf_op jit(solution)/shard_map/all_to_all | solution.py:283
  51.7 10.3 %all_to_all.31.x_ref.refs_3_ = f32[8,32,128]{2,1,0:T(8,128)S(1)} all-to-all(f32[8,32,128]{2,1,0:T(8,128)S(1)} %shard_map.55), channel_id=1, replica_groups=mesh['ia'=4,'ja'=8,'ka'=8] {'ja'}, dimensions={0} | all-to-all | bytes 262144 | tf_op jit(solution)/shard_map/all_to_all | solution.py:283
  62.1 2.9 %shard_map.56 = (f32[32,16,128]{2,1,0:T(8,128)}, f32[8,128]{1,0:T(8,128)S(1)}) custom-call(bf16[8,512,512]{2,1,0:T(8,128)(2,1)} %t_hbm.3, f32[8,32,128]{2,1,0:T(8,128)S(1)} %all_to_all.31.x_ref.refs_3_, f32[32,128]{1,0:T(8,128)S(1)} %get-tuple-element.34.c_ref, bf16[512,512]{1,0:T(8,128)(2,1)S(1)} %get-tuple-element.22.refs_0_, ...), custom_call_target="tpu_custom_call" | custom-call | tf_op jit(solution)/shard_map/pallas_call | solution.py:252
  65.0 3.9 %all-to-all-start.4 = ((f32[32,16,128]{2,1,0:T(8,128)}), f32[32,16,128]{2,1,0:T(8,128)S(1)}, u32[]{:S(2)}, u32[]{:S(2)}) async-start(f32[32,16,128]{2,1,0:T(8,128)} %get-tuple-element.35), calls=%async_computation.4 | async-start | bytes 524288 | tf_op jit(solution)/shard_map/all_to_all | solution.py:283
  68.9 2.6 %collective-permute-start.3 = (f32[8,128]{1,0:T(8,128)S(1)}, f32[8,128]{1,0:T(8,128)S(1)}, u32[]{:S(2)}, u32[]{:S(2)}) collective-permute-start(f32[8,128]{1,0:T(8,128)S(1)} %get-tuple-element.36.refs_0_), channel_id=1, source_target_pairs={{0,192},{64,0},{128,64},{192,128},{1,193},{65,1},{129,65},{193,129... | collective-permute-start | bytes 12296 | tf_op jit(solution)/shard_map/ppermute | solution.py:288
  71.5 0.5 collective-permute-start.2
  72.0 0.6 collective-permute-start.1
  72.6 2.9 %collective-permute-done.2.refs_2_ = f32[8,128]{1,0:T(8,128)S(1)} collective-permute-done((f32[8,128]{1,0:T(8,128)S(1)}, f32[8,128]{1,0:T(8,128)S(1)}, u32[]{:S(2)}, u32[]{:S(2)}) %collective-permute-start.2) | collective-permute-done | bytes 4128 | tf_op jit(solution)/shard_map/ppermute | solution.py:288
  75.4 0.5 collective-permute-done.1.refs_1_
  75.9 2.8 %shard_map.57 = (f32[32,32]{1,0:T(8,128)S(1)}, f32[32,128]{1,0:T(8,128)S(1)}) custom-call(f32[8,128]{1,0:T(8,128)S(1)} %get-tuple-element.36.refs_0_, f32[8,128]{1,0:T(8,128)S(1)} %collective-permute-done.1.refs_1_, f32[8,128]{1,0:T(8,128)S(1)} %collective-permute-done.2.refs_2_, f32[8,128]{1,0:T(8,128)S(1)} %collective-permute-done.3.refs_3_, ...), custom_call_target="tpu_custom_call" | custom-call | tf_op jit(solution)/shard_map/pallas_call | solution.py:252
  78.7 0.3 shard_map.58
  79.1 19.5 %all_to_all.32 = f32[64,1,128]{2,1,0:T(1,128)S(1)} all-to-all(f32[64,1,128]{2,1,0:T(1,128)S(1)} %bitcast.5), channel_id=1, replica_groups=mesh['ia'=4,'ja'=8,'ka'=8] {'ja','ka'}, dimensions={0} | all-to-all | bytes 65536 | tf_op jit(solution)/shard_map/all_to_all | solution.py:283
  98.6 0.7 shard_map.59
  (4 shorter events, 0.4 us)
Async XLA Ops:
  2.1 21.0 %all-to-all-start = ((f32[32,8,128]{2,1,0:T(8,128)}), f32[32,8,128]{2,1,0:T(8,128)S(1)}, u32[]{:S(2)}, u32[]{:S(2)}) async-start(f32[32,8,128]{2,1,0:T(8,128)} %shard_map.50), calls=%async_computation | async-start | bytes 262144 | tf_op jit(solution)/shard_map/all_to_all | solution.py:283
  25.7 3.4 %collective-permute-start = (f32[4,160,128]{2,1,0:T(8,128)S(1)}, f32[4,160,128]{2,1,0:T(8,128)S(1)}, u32[]{:S(2)}, u32[]{:S(2)}) collective-permute-start(f32[4,160,128]{2,1,0:T(8,128)S(1)} %get-tuple-element.29), channel_id=1, source_target_pairs={{0,8},{8,0},{16,24},{24,16},{32,40},{40,32},{48,56},{56,48},{1,9},... | collective-permute-start | bytes 983048 | tf_op jit(solution)/shard_map/ppermute | solution.py:318
  40.9 10.5 %all-to-all-start.2 = ((f32[8,16,128]{2,1,0:T(8,128)}), f32[8,16,128]{2,1,0:T(8,128)S(1)}, u32[]{:S(2)}, u32[]{:S(2)}) async-start(f32[8,16,128]{2,1,0:T(8,128)} %get-tuple-element.30), calls=%async_computation.2 | async-start | bytes 131072 | tf_op jit(solution)/shard_map/all_to_all | solution.py:283
  65.0 13.7 %all-to-all-start.4 = ((f32[32,16,128]{2,1,0:T(8,128)}), f32[32,16,128]{2,1,0:T(8,128)S(1)}, u32[]{:S(2)}, u32[]{:S(2)}) async-start(f32[32,16,128]{2,1,0:T(8,128)} %get-tuple-element.35), calls=%async_computation.4 | async-start | bytes 524288 | tf_op jit(solution)/shard_map/all_to_all | solution.py:283
  68.9 3.7 %collective-permute-start.3 = (f32[8,128]{1,0:T(8,128)S(1)}, f32[8,128]{1,0:T(8,128)S(1)}, u32[]{:S(2)}, u32[]{:S(2)}) collective-permute-start(f32[8,128]{1,0:T(8,128)S(1)} %get-tuple-element.36.refs_0_), channel_id=1, source_target_pairs={{0,192},{64,0},{128,64},{192,128},{1,193},{65,1},{129,65},{193,129... | collective-permute-start | bytes 12296 | tf_op jit(solution)/shard_map/ppermute | solution.py:288
  71.5 4.0 %collective-permute-start.2 = (f32[8,128]{1,0:T(8,128)S(1)}, f32[8,128]{1,0:T(8,128)S(1)}, u32[]{:S(2)}, u32[]{:S(2)}) collective-permute-start(f32[8,128]{1,0:T(8,128)S(1)} %get-tuple-element.36.refs_0_), channel_id=1, source_target_pairs={{0,128},{64,192},{128,0},{192,64},{1,129},{65,193},{129,1},{193,65... | collective-permute-start | bytes 12296 | tf_op jit(solution)/shard_map/ppermute | solution.py:288
  72.0 4.0 %collective-permute-start.1 = (f32[8,128]{1,0:T(8,128)S(1)}, f32[8,128]{1,0:T(8,128)S(1)}, u32[]{:S(2)}, u32[]{:S(2)}) collective-permute-start(f32[8,128]{1,0:T(8,128)S(1)} %get-tuple-element.36.refs_0_), channel_id=1, source_target_pairs={{0,64},{64,128},{128,192},{192,0},{1,65},{65,129},{129,193},{193,1... | collective-permute-start | bytes 12296 | tf_op jit(solution)/shard_map/ppermute | solution.py:288

commit v3 on v2

--- a/solution.py
+++ b/solution.py
@@ -13,7 +13,7 @@
 NT = (((1,), (1,)), ((), ()))
 VMEM = pl.BlockSpec(memory_space=pltpu.VMEM)
 HBM = pl.BlockSpec(memory_space=pltpu.HBM)
-KEPT = 6
+LONG = pl.CostEstimate(flops=10**10, bytes_accessed=0, transcendentals=0)
 
 
 def iota(shape, axis):
@@ -57,32 +57,18 @@
 def inverse(a):
     size = a.shape[0]
     rows, cols = iota(a.shape, 0), iota(a.shape, 1)
-    for p in range(size):
-        row, col = a[p : p + 1, :], a[:, p : p + 1]
-        scale = 1.0 / a[p : p + 1, p : p + 1]
-        row = jnp.where(cols[:1] == p, 1.0, row) * scale
-        a = jnp.where(cols == p, 0.0, a) - col * row
-        a = jnp.where(rows == p, row, a)
+    for start in range(0, size, size // 2):
+        spread = {p: jnp.broadcast_to(a[:, p : p + 1], a.shape) for p in range(start, start + size // 2)}
+        for p in range(start, start + size // 2):
+            col = spread.pop(p)
+            scale = 1.0 / col[p : p + 1, :]
+            row = jnp.where(cols[:1] == p, 1.0, a[p : p + 1, :]) * scale
+            a = jnp.where(cols == p, 0.0, a) - col * row
+            a = jnp.where(rows == p, row, a)
+            for q, other in spread.items():
+                there = other[p : p + 1, :] * scale
+                spread[q] = jnp.where(rows == p, there, other - col * there)
     return a
-
-
-def fetch(t_ref, places, sems):
-    copies = [
-        pltpu.make_async_copy(t_ref.at[KEPT + n], places.at[n], sems.at[n])
-        for n in range(t_ref.shape[0] - KEPT)
-    ]
-    for copy in copies:
-        copy.start()
-    return copies
-
-
-def load_kernel(t_ref, *refs):
-    sems = refs[-1]
-    copies = [pltpu.make_async_copy(t_ref.at[k], refs[k], sems.at[k]) for k in range(KEPT)]
-    for copy in copies:
-        copy.start()
-    for copy in copies:
-        copy.wait()
 
 
 def start_kernel(b_hbm, c_hbm, y_ref, b_ref, c_ref, sems):
@@ -104,10 +90,7 @@
         y_ref[n] = tile
 
 
-def first_kernel(t_hbm, y_ref, *refs):
-    keep_ref, send_ref, scratch, rest, sems = refs[KEPT:]
-    copies = fetch(t_hbm, rest, sems)
-    steps = [*refs[:KEPT], *(rest.at[n] for n in range(8 - KEPT))]
+def first_kernel(y_ref, t_ref, keep_ref, send_ref, scratch):
     core = lax.axis_index("ja") % 2
     lane = iota((8, LANES), 1)
     b_rows, c_rows = [], []
@@ -133,10 +116,7 @@
         [jnp.concatenate(placed(high, q) + placed(low, q), axis=0) for q in range(4)], axis=1
     )
     for h in range(2):
-        if h == 1:
-            for copy in copies:
-                copy.wait()
-        left = jnp.concatenate([steps[4 * h + q][...] for q in range(4)], axis=1)
+        left = jnp.concatenate([t_ref[4 * h + q] for q in range(4)], axis=1)
         both = lax.dot_general(left, weights, NT, preferred_element_type=F32)
         scratch[h] = both[:, :LANES] + both[:, LANES:]
     for n in range(4):
@@ -177,19 +157,22 @@
 
 
 def solve_kernel(v_ref, inv_ref, x_ref):
-    parity = lax.axis_index("ja") % 2
     m_t = unfold(total(v_ref))
     raw = dot_nt(inv_ref[...], jnp.concatenate([m_t, m_t], axis=0))
-    raw = jnp.where(iota((RANK, LANES), 1) // 64 == parity, raw, 0.0)
+    raw = jnp.where(iota((16, LANES), 1) < 64, raw[:16], raw[16:])
     for n in range(8):
         x_ref[n] = raw
 
 
-def second_kernel(t_hbm, x_ref, c_ref, *refs):
-    w_ref, g_ref, rest, sems = refs[KEPT:]
-    copies = fetch(t_hbm, rest, sems)
-    steps = [*refs[:KEPT], *(rest.at[n] for n in range(8 - KEPT))]
-    a = jnp.concatenate([x_ref[2 * q] + x_ref[2 * q + 1] for q in range(4)], axis=1)
+def second_kernel(x_ref, t_ref, c_ref, w_ref, g_ref):
+    low_lanes = iota((16, LANES), 1) < 64
+    parts = []
+    for q in range(4):
+        one, two = x_ref[2 * q], x_ref[2 * q + 1]
+        top = jnp.where(low_lanes, one, pltpu.roll(two, 64, 1))
+        bottom = jnp.where(low_lanes, pltpu.roll(one, 64, 1), two)
+        parts.append(jnp.concatenate([top, bottom], axis=0))
+    a = jnp.concatenate(parts, axis=1)
     g_ref[...] = folded_gram(a)
     c = c_ref[...]
     highs, lows = [], []
@@ -198,12 +181,8 @@
         highs.append(high)
         lows.append(low)
     left = jnp.concatenate([jnp.concatenate(highs, axis=1), jnp.concatenate(lows, axis=1)], axis=0)
-    for copy in copies:
-        copy.wait()
-    right = jnp.concatenate([ref[...] for ref in steps], axis=0)
-    both = jnp.dot(left, right, preferred_element_type=F32)
+    both = jnp.dot(left, t_ref[...].reshape(4096, 512), preferred_element_type=F32)
     out = both[:RANK] + both[RANK:]
-    low_lanes = iota((16, LANES), 1) < 64
     for q in range(4):
         pair = out[:, 128 * q : 128 * q + 128]
         turned = pltpu.roll(pair, 64, 1)
@@ -243,40 +222,20 @@
     b = raw_ref[...] / jnp.sqrt(ss / total_j + EPS)
     out_b_ref[...] = pltpu.roll(b, 32 - 8 * ia, 0)[:8, :64]
     mine = x_ref[ka]
-    mine = (mine + pltpu.roll(mine, 64, 1)) * scale_ref[...]
+    mine = jnp.concatenate([mine, pltpu.roll(mine, 64, 1)], axis=0) * scale_ref[...]
     out_a_ref[...] = pltpu.roll(mine, 32 - 4 * ja, 0)[:4, :64]
 
 
-def call(kernel, outs, *args, scratch=()):
-    big = [a.ndim == 3 and a.dtype == jnp.bfloat16 for a in args]
+def call(kernel, outs, *args, scratch=(), cost=None, space=VMEM):
     return pl.pallas_call(
         kernel,
         out_shape=[jax.ShapeDtypeStruct(s, F32) for s in outs],
-        in_specs=[HBM if flag else VMEM for flag in big],
+        in_specs=[space] * len(args),
         out_specs=[VMEM] * len(outs),
         scratch_shapes=scratch,
+        cost_estimate=cost,
         compiler_params=pltpu.CompilerParams(vmem_limit_bytes=32 * 1024 * 1024),
     )(*args)
-
-
-def load(tensor):
-    step = tensor.shape[1:]
-    return pl.pallas_call(
-        load_kernel,
-        out_shape=[pltpu.VMEM(step, tensor.dtype)] * KEPT,
-        in_specs=[HBM],
-        out_specs=[VMEM] * KEPT,
-        scratch_shapes=[pltpu.SemaphoreType.DMA((KEPT,))],
-        compiler_params=pltpu.CompilerParams(vmem_limit_bytes=32 * 1024 * 1024),
-    )(tensor)
-
-
-def rest_scratch(tensor):
-    count = tensor.shape[0] - KEPT
-    return [
-        pltpu.VMEM((count, *tensor.shape[1:]), tensor.dtype),
-        pltpu.SemaphoreType.DMA((count,)),
-    ]
 
 
 def exchange(x, axes, groups=None):
@@ -291,29 +250,29 @@
 def body(tensor, factor_b, factor_c):
     total_i = tensor.shape[1] * lax.axis_size("ia")
     total_j = tensor.shape[2] * lax.axis_size("ja")
-    tensor, factor_b, factor_c = (
-        pltpu.with_memory_space_constraint(a, pltpu.HBM) for a in (tensor, factor_b, factor_c)
-    )
-    (y,) = pl.pallas_call(
+    factor_b, factor_c = (
+        pltpu.with_memory_space_constraint(a, pltpu.HBM) for a in (factor_b, factor_c)
+    )
+    (y,) = call(
         start_kernel,
-        out_shape=[jax.ShapeDtypeStruct((32, 8, LANES), F32)],
-        in_specs=[HBM, HBM],
-        out_specs=[VMEM],
-        scratch_shapes=[
+        [(32, 8, LANES)],
+        factor_b,
+        factor_c,
+        scratch=[
             pltpu.VMEM(factor_b.shape, F32),
             pltpu.VMEM(factor_c.shape, F32),
             pltpu.SemaphoreType.DMA((2,)),
         ],
-    )(factor_b, factor_c)
+        cost=LONG,
+        space=HBM,
+    )
     y = exchange(y, ("ia", "ka"))
-    steps = load(tensor)
     keep, send = call(
         first_kernel,
         [(4, 160, LANES), (4, 160, LANES)],
+        y,
         tensor,
-        y,
-        *steps,
-        scratch=[pltpu.VMEM((2, 512, LANES), F32), *rest_scratch(tensor)],
+        scratch=[pltpu.VMEM((2, 512, LANES), F32)],
     )
     z = keep + lax.ppermute(send, "ja", [(n, n ^ 1) for n in range(8)])
     z = exchange(z, "ja", [[0, 2, 4, 6], [1, 3, 5, 7]])
@@ -322,17 +281,9 @@
     )
     v = exchange(u, "ka")
     inv_a, gram_c = call(invert_a_kernel, [(RANK, RANK), (RANK, RANK)], gram_b, c_all)
-    (x,) = call(solve_kernel, [(8, RANK, LANES)], v, inv_a)
+    (x,) = call(solve_kernel, [(8, 16, LANES)], v, inv_a, cost=LONG)
     x = exchange(x, "ja")
-    w, g = call(
-        second_kernel,
-        [(32, 16, LANES), (8, LANES)],
-        tensor,
-        x,
-        c_here,
-        *steps,
-        scratch=rest_scratch(tensor),
-    )
+    w, g = call(second_kernel, [(32, 16, LANES), (8, LANES)], x, tensor, c_here)
     w = exchange(w, ("ia", "ka"))
     inv_b, scale_a = call(
         lambda *refs: invert_b_kernel(total_i, *refs),

time: 99.8 us -> 94.8 us (0.950)
  blocking collectives: 40.6 us -> 59.6 us
  starting transfers between devices: 24.9 us -> 13 us
  Pallas kernels: 16.7 us -> 8.28 us
  waiting for transfers between devices: 16.2 us -> 12.7 us
    all_to_all x3 -> x4, blocking collectives: 40.6 us -> 59.6 us  [exchange(): return lax.all_to_all(x, axes, 0, 0, tiled=True, axis_index_groups=groups)]
    all_to_all x3 -> x2, starting transfers between devices: 19.1 us -> 7.22 us  [exchange(): return lax.all_to_all(x, axes, 0, 0, tiled=True, axis_index_groups=groups)]
    pallas_call x8 -> x9, Pallas kernels: 13.4 us -> 8.28 us  [call(): pl.pallas_call(kernel, out_shape=[jax.ShapeDtypeStruct(s, F32) for s in o...]
    all_to_all x3 -> x2, waiting for transfers between devices: 11.6 us -> 8.16 us  [exchange(): return lax.all_to_all(x, axes, 0, 0, tiled=True, axis_index_groups=groups)]
    pallas_call x2 -> x0, Pallas kernels: 3.34 us -> none  [the longest x1 1.89 us: load(): pl.pallas_call(load_kernel, out_shape=[pltpu.VMEM(step, tensor.dtype)] *...]
  transfers between devices with their start and end apart: 7 -> 6, of which waited for: 5 -> 5; matrix products, arithmetic and copies ran while one was open for 0% -> 0% of each run, Pallas kernels for 7% -> 2%
where the time goes in v3:
time: 94.8 us; the launch traced here: 94.4 us
  blocking collectives  59.6 us (63%)
  starting transfers between devices  13 us (14%)
  waiting for transfers between devices  12.7 us (13%)
  Pallas kernels  8.28 us (9%)
    all_to_all x4, blocking collectives, exchange(): return lax.all_to_all(x, axes, 0, 0, tiled=True, axis_index_groups=groups)  59.6 us
    pallas_call x9, Pallas kernels, call(): pl.pallas_call(kernel, out_shape=[jax.ShapeDtypeStruct(s, F32) for s in o...  8.28 us
    all_to_all x2, waiting for transfers between devices, exchange(): return lax.all_to_all(x, axes, 0, 0, tiled=True, axis_index_groups=groups)  8.16 us
    all_to_all x2, starting transfers between devices, exchange(): return lax.all_to_all(x, axes, 0, 0, tiled=True, axis_index_groups=groups)  7.22 us
    ppermute x3, starting transfers between devices, turned(): return lax.ppermute(x, axis, [(n, (n + step) % size) for n in range(size)])  3.66 us
    ppermute x3, waiting for transfers between devices, turned(): return lax.ppermute(x, axis, [(n, (n + step) % size) for n in range(size)])  3.33 us
    ppermute x1, starting transfers between devices, body(): z = keep + lax.ppermute(send, 'ja', [(n, n ^ 1) for n in range(8)])  2.16 us
  transfers between devices with their start and end apart: 6, of which 5 were waited for; matrix products, arithmetic and copies ran while one was open for 0% of the time, Pallas kernels for 2%

profile of v3, /device:TPU:1, one launch (start us, length us, event | category | flops | bytes accessed | tf_op | source)
XLA Modules:
  0.0 94.4 jit_solution(4902372043421097936)
XLA Ops:
  0.6 1.0 %shard_map.50 = f32[32,8,128]{2,1,0:T(8,128)S(1)} custom-call(f32[8,64]{1,0:T(8,128)} %b_hbm.1, f32[1,8]{1,0:T(1,128)} %c_hbm.1), custom_call_target="tpu_custom_call" | custom-call | flops 10000000000 | tf_op jit(solution)/shard_map/pallas_call | solution.py:230
  1.6 20.9 %all_to_all.30.y_ref = f32[32,8,128]{2,1,0:T(8,128)S(1)} all-to-all(f32[32,8,128]{2,1,0:T(8,128)S(1)} %shard_map.50), channel_id=1, replica_groups=mesh['ia'=4,'ja'=8,'ka'=8] {'ia','ka'}, dimensions={0} | all-to-all | bytes 262144 | tf_op jit(solution)/shard_map/all_to_all | solution.py:242
  22.6 1.4 %shard_map.51 = (f32[4,160,128]{2,1,0:T(8,128)S(1)}, f32[4,160,128]{2,1,0:T(8,128)S(1)}) custom-call(f32[32,8,128]{2,1,0:T(8,128)S(1)} %all_to_all.30.y_ref, bf16[8,512,512]{2,1,0:T(8,128)(2,1)S(1)} %copy-done), custom_call_target="tpu_custom_call" | custom-call | tf_op jit(solution)/shard_map/pallas_call | solution.py:230
  24.0 2.2 %collective-permute-start = (f32[4,160,128]{2,1,0:T(8,128)S(1)}, f32[4,160,128]{2,1,0:T(8,128)S(1)}, u32[]{:S(2)}, u32[]{:S(2)}) collective-permute-start(f32[4,160,128]{2,1,0:T(8,128)S(1)} %get-tuple-element.17), channel_id=1, source_target_pairs={{0,8},{8,0},{16,24},{24,16},{32,40},{40,32},{48,56},{56,48},{1,9},... | collective-permute-start | bytes 983048 | tf_op jit(solution)/shard_map/ppermute | solution.py:277
  26.1 1.3 %collective-permute-done = f32[4,160,128]{2,1,0:T(8,128)S(1)} collective-permute-done((f32[4,160,128]{2,1,0:T(8,128)S(1)}, f32[4,160,128]{2,1,0:T(8,128)S(1)}, u32[]{:S(2)}, u32[]{:S(2)}) %collective-permute-start) | collective-permute-done | bytes 327712 | tf_op jit(solution)/shard_map/ppermute | solution.py:277
  27.4 10.8 %all_to_all.31.z_ref = f32[4,160,128]{2,1,0:T(8,128)S(1)} all-to-all(f32[4,160,128]{2,1,0:T(8,128)S(1)} %add.3), channel_id=1, replica_groups={{0,16,32,48},{8,24,40,56},{1,17,33,49},{9,25,41,57},{2,18,34,50},{10,26..., dimensions={0} | all-to-all | bytes 655360 | tf_op jit(solution)/shard_map/all_to_all | solution.py:242
  38.2 1.0 %shard_map.52 = (f32[8,16,128]{2,1,0:T(8,128)}, f32[32,32]{1,0:T(8,128)S(1)}, f32[32,64]{1,0:T(8,128)S(1)}, f32[32,128]{1,0:T(8,128)S(1)}) custom-call(f32[4,160,128]{2,1,0:T(8,128)S(1)} %all_to_all.31.z_ref), custom_call_target="tpu_custom_call" | custom-call | tf_op jit(solution)/shard_map/pallas_call | solution.py:230
  39.2 3.3 %all-to-all-start.2 = ((f32[8,16,128]{2,1,0:T(8,128)}), f32[8,16,128]{2,1,0:T(8,128)S(1)}, u32[]{:S(2)}, u32[]{:S(2)}) async-start(f32[8,16,128]{2,1,0:T(8,128)} %get-tuple-element.18), calls=%async_computation.2 | async-start | bytes 131072 | tf_op jit(solution)/shard_map/all_to_all | solution.py:242
  42.6 0.8 shard_map.53
  43.4 6.3 %all-to-all-done.2.v_ref = f32[8,16,128]{2,1,0:T(8,128)S(1)} async-done(((f32[8,16,128]{2,1,0:T(8,128)}), f32[8,16,128]{2,1,0:T(8,128)S(1)}, u32[]{:S(2)}, u32[]{:S(2)}) %all-to-all-start.2) | async-done | bytes 65568 | tf_op jit(solution)/shard_map/all_to_all | solution.py:242
  49.7 0.3 shard_map.54
  50.0 10.2 %all_to_all.32.x_ref.refs_3_ = f32[8,16,128]{2,1,0:T(8,128)S(1)} all-to-all(f32[8,16,128]{2,1,0:T(8,128)S(1)} %shard_map.54), channel_id=1, replica_groups=mesh['ia'=4,'ja'=8,'ka'=8] {'ja'}, dimensions={0} | all-to-all | bytes 131072 | tf_op jit(solution)/shard_map/all_to_all | solution.py:242
  60.2 2.0 %shard_map.55 = (f32[32,16,128]{2,1,0:T(8,128)}, f32[8,128]{1,0:T(8,128)S(1)}) custom-call(f32[8,16,128]{2,1,0:T(8,128)S(1)} %all_to_all.32.x_ref.refs_3_, bf16[8,512,512]{2,1,0:T(8,128)(2,1)S(1)} %copy-done.1, f32[32,128]{1,0:T(8,128)S(1)} %get-tuple-element.22.c_ref), custom_call_target="tpu_custom_call" | custom-call | tf_op jit(solution)/shard_map/pallas_call | solution.py:230
  62.1 3.9 %all-to-all-start.4 = ((f32[32,16,128]{2,1,0:T(8,128)}), f32[32,16,128]{2,1,0:T(8,128)S(1)}, u32[]{:S(2)}, u32[]{:S(2)}) async-start(f32[32,16,128]{2,1,0:T(8,128)} %get-tuple-element.23), calls=%async_computation.4 | async-start | bytes 524288 | tf_op jit(solution)/shard_map/all_to_all | solution.py:242
  66.0 2.6 %collective-permute-start.3 = (f32[8,128]{1,0:T(8,128)S(1)}, f32[8,128]{1,0:T(8,128)S(1)}, u32[]{:S(2)}, u32[]{:S(2)}) collective-permute-start(f32[8,128]{1,0:T(8,128)S(1)} %get-tuple-element.24.refs_0_), channel_id=1, source_target_pairs={{0,192},{64,0},{128,64},{192,128},{1,193},{65,1},{129,65},{193,129... | collective-permute-start | bytes 12296 | tf_op jit(solution)/shard_map/ppermute | solution.py:247
  68.6 0.5 collective-permute-start.2
  69.0 0.6 collective-permute-start.1
  69.7 2.9 %collective-permute-done.2.refs_2_ = f32[8,128]{1,0:T(8,128)S(1)} collective-permute-done((f32[8,128]{1,0:T(8,128)S(1)}, f32[8,128]{1,0:T(8,128)S(1)}, u32[]{:S(2)}, u32[]{:S(2)}) %collective-permute-start.2) | collective-permute-done | bytes 4128 | tf_op jit(solution)/shard_map/ppermute | solution.py:247
  72.5 0.5 collective-permute-done.1.refs_1_
  73.0 0.9 shard_map.56
  73.9 1.8 %all-to-all-done.4.w_ref = f32[32,16,128]{2,1,0:T(8,128)S(1)} async-done(((f32[32,16,128]{2,1,0:T(8,128)}), f32[32,16,128]{2,1,0:T(8,128)S(1)}, u32[]{:S(2)}, u32[]{:S(2)}) %all-to-all-start.4) | async-done | bytes 262176 | tf_op jit(solution)/shard_map/all_to_all | solution.py:242
  75.7 0.3 shard_map.57
  76.0 17.7 %all_to_all.33 = f32[64,1,128]{2,1,0:T(1,128)S(1)} all-to-all(f32[64,1,128]{2,1,0:T(1,128)S(1)} %bitcast.5), channel_id=1, replica_groups=mesh['ia'=4,'ja'=8,'ka'=8] {'ja','ka'}, dimensions={0} | all-to-all | bytes 65536 | tf_op jit(solution)/shard_map/all_to_all | solution.py:242
  93.7 0.7 shard_map.58
  (6 shorter events, 0.0 us)
Async XLA Ops:
  0.6 21.9 %copy-start = (bf16[8,512,512]{2,1,0:T(8,128)(2,1)S(1)}, bf16[8,512,512]{2,1,0:T(8,128)(2,1)}, u32[]{:S(2)}) copy-start(bf16[8,512,512]{2,1,0:T(8,128)(2,1)} %t_ref.3) | copy-start | bytes 12582916
  24.0 3.4 %collective-permute-start = (f32[4,160,128]{2,1,0:T(8,128)S(1)}, f32[4,160,128]{2,1,0:T(8,128)S(1)}, u32[]{:S(2)}, u32[]{:S(2)}) collective-permute-start(f32[4,160,128]{2,1,0:T(8,128)S(1)} %get-tuple-element.17), channel_id=1, source_target_pairs={{0,8},{8,0},{16,24},{24,16},{32,40},{40,32},{48,56},{56,48},{1,9},... | collective-permute-start | bytes 983048 | tf_op jit(solution)/shard_map/ppermute | solution.py:277
  39.2 10.5 %all-to-all-start.2 = ((f32[8,16,128]{2,1,0:T(8,128)}), f32[8,16,128]{2,1,0:T(8,128)S(1)}, u32[]{:S(2)}, u32[]{:S(2)}) async-start(f32[8,16,128]{2,1,0:T(8,128)} %get-tuple-element.18), calls=%async_computation.2 | async-start | bytes 131072 | tf_op jit(solution)/shard_map/all_to_all | solution.py:242
  49.7 10.4 %copy-start.1 = (bf16[8,512,512]{2,1,0:T(8,128)(2,1)S(1)}, bf16[8,512,512]{2,1,0:T(8,128)(2,1)}, u32[]{:S(2)}) copy-start(bf16[8,512,512]{2,1,0:T(8,128)(2,1)} %t_ref.3) | copy-start | bytes 12582916
  62.1 13.6 %all-to-all-start.4 = ((f32[32,16,128]{2,1,0:T(8,128)}), f32[32,16,128]{2,1,0:T(8,128)S(1)}, u32[]{:S(2)}, u32[]{:S(2)}) async-start(f32[32,16,128]{2,1,0:T(8,128)} %get-tuple-element.23), calls=%async_computation.4 | async-start | bytes 524288 | tf_op jit(solution)/shard_map/all_to_all | solution.py:242
  66.0 3.7 %collective-permute-start.3 = (f32[8,128]{1,0:T(8,128)S(1)}, f32[8,128]{1,0:T(8,128)S(1)}, u32[]{:S(2)}, u32[]{:S(2)}) collective-permute-start(f32[8,128]{1,0:T(8,128)S(1)} %get-tuple-element.24.refs_0_), channel_id=1, source_target_pairs={{0,192},{64,0},{128,64},{192,128},{1,193},{65,1},{129,65},{193,129... | collective-permute-start | bytes 12296 | tf_op jit(solution)/shard_map/ppermute | solution.py:247
  68.6 4.0 %collective-permute-start.2 = (f32[8,128]{1,0:T(8,128)S(1)}, f32[8,128]{1,0:T(8,128)S(1)}, u32[]{:S(2)}, u32[]{:S(2)}) collective-permute-start(f32[8,128]{1,0:T(8,128)S(1)} %get-tuple-element.24.refs_0_), channel_id=1, source_target_pairs={{0,128},{64,192},{128,0},{192,64},{1,129},{65,193},{129,1},{193,65... | collective-permute-start | bytes 12296 | tf_op jit(solution)/shard_map/ppermute | solution.py:247
  69.0 4.0 %collective-permute-start.1 = (f32[8,128]{1,0:T(8,128)S(1)}, f32[8,128]{1,0:T(8,128)S(1)}, u32[]{:S(2)}, u32[]{:S(2)}) collective-permute-start(f32[8,128]{1,0:T(8,128)S(1)} %get-tuple-element.24.refs_0_), channel_id=1, source_target_pairs={{0,64},{64,128},{128,192},{192,0},{1,65},{65,129},{129,193},{193,1... | collective-permute-start | bytes 12296 | tf_op jit(solution)/shard_map/ppermute | solution.py:247

commit v4 on v3

--- a/solution.py
+++ b/solution.py
@@ -146,7 +146,7 @@
     acc = acc + pltpu.roll(acc, 64, 1)
     acc = acc + pltpu.roll(acc, 32, 1)
     u = fold(acc)
-    for n in range(8):
+    for n in range(32):
         u_ref[n] = u
 
 
@@ -156,23 +156,33 @@
     inv_ref[...] = inverse(gram_b_ref[...] * gram_c)
 
 
-def solve_kernel(v_ref, inv_ref, x_ref):
-    m_t = unfold(total(v_ref))
-    raw = dot_nt(inv_ref[...], jnp.concatenate([m_t, m_t], axis=0))
-    raw = jnp.where(iota((16, LANES), 1) < 64, raw[:16], raw[16:])
-    for n in range(8):
-        x_ref[n] = raw
-
-
-def second_kernel(x_ref, t_ref, c_ref, w_ref, g_ref):
-    low_lanes = iota((16, LANES), 1) < 64
+def turn_kernel(v_ref, m_ref):
     parts = []
+    for y in range(4):
+        part = v_ref[8 * y]
+        for ka in range(1, 8):
+            part = part + v_ref[8 * y + ka]
+        parts.append(unfold(part))
+    m_ref[...] = jnp.concatenate(parts, axis=0).T
+
+
+def second_kernel(mine_ref, other_ref, inv_ref, t_ref, c_ref, w_ref, g_ref, a_ref, scratch):
+    ka, core = lax.axis_index("ka"), lax.axis_index("ja") % 2
+    low_lanes = iota((RANK, LANES), 1) < 64
+    even = jnp.where(core == 0, mine_ref[...], other_ref[...])
+    odd = jnp.where(core == 0, other_ref[...], mine_ref[...])
+    parts = []
+    for p in range(2):
+        one, two = even[:, 128 * p : 128 * p + 128], odd[:, 128 * p : 128 * p + 128]
+        parts.append(jnp.where(low_lanes, one, pltpu.roll(two, 64, 1)))
+        parts.append(jnp.where(low_lanes, pltpu.roll(one, 64, 1), two))
+    m = jnp.concatenate(parts, axis=1)
+    a = jnp.dot(inv_ref[...], m, precision=HIGH, preferred_element_type=F32)
     for q in range(4):
-        one, two = x_ref[2 * q], x_ref[2 * q + 1]
-        top = jnp.where(low_lanes, one, pltpu.roll(two, 64, 1))
-        bottom = jnp.where(low_lanes, pltpu.roll(one, 64, 1), two)
-        parts.append(jnp.concatenate([top, bottom], axis=0))
-    a = jnp.concatenate(parts, axis=1)
+        pair = a[:, 128 * q : 128 * q + 128]
+        scratch[2 * q] = pair
+        scratch[2 * q + 1] = pltpu.roll(pair, 64, 1)
+    a_ref[...] = scratch[ka]
     g_ref[...] = folded_gram(a)
     c = c_ref[...]
     highs, lows = [], []
@@ -183,6 +193,7 @@
     left = jnp.concatenate([jnp.concatenate(highs, axis=1), jnp.concatenate(lows, axis=1)], axis=0)
     both = jnp.dot(left, t_ref[...].reshape(4096, 512), preferred_element_type=F32)
     out = both[:RANK] + both[RANK:]
+    low_lanes = low_lanes[:16]
     for q in range(4):
         pair = out[:, 128 * q : 128 * q + 128]
         turned = pltpu.roll(pair, 64, 1)
@@ -193,13 +204,17 @@
             w_ref[8 * ia + 2 * q + 1] = odd
 
 
-def invert_b_kernel(total_i, g0_ref, g1_ref, g2_ref, g3_ref, gram_c_ref, inv_ref, scale_ref):
+def invert_b_kernel(
+    total_i, g0_ref, g1_ref, g2_ref, g3_ref, gram_c_ref, a_ref, inv_ref, scale_ref, out_ref
+):
+    ja = lax.axis_index("ja")
     gram = unfold((g0_ref[...] + g1_ref[...]) + (g2_ref[...] + g3_ref[...]))
     diag = jnp.where(iota(gram.shape, 0) == iota(gram.shape, 1), gram, 0.0)
     scale_col = 1.0 / jnp.sqrt(jnp.sum(diag, axis=1, keepdims=True) / total_i + EPS)
     scale_row = 1.0 / jnp.sqrt(jnp.sum(diag, axis=0, keepdims=True) / total_i + EPS)
     inv_ref[...] = inverse(gram * scale_col * scale_row * gram_c_ref[...])
     scale_ref[...] = jnp.broadcast_to(scale_col, (RANK, LANES))
+    out_ref[...] = pltpu.roll(a_ref[...] * scale_col, 32 - 4 * ja, 0)[:4, :64]
 
 
 def second_solve_kernel(w_ref, inv_ref, scale_ref, raw_ref, ss_ref):
@@ -214,16 +229,13 @@
     ss_ref[...] = jnp.broadcast_to(ss_row, ss_ref.shape)
 
 
-def finish_kernel(total_j, ss_ref, raw_ref, scale_ref, x_ref, out_a_ref, out_b_ref):
-    ia, ja, ka = lax.axis_index("ia"), lax.axis_index("ja"), lax.axis_index("ka")
+def finish_kernel(total_j, ss_ref, raw_ref, out_ref):
+    ia = lax.axis_index("ia")
     ss_row = jnp.sum(ss_ref[...], axis=0, keepdims=True)
     eye = iota((RANK, LANES), 0) == iota((RANK, LANES), 1)
     ss = jnp.sum(jnp.where(eye, ss_row, 0.0), axis=1, keepdims=True)
     b = raw_ref[...] / jnp.sqrt(ss / total_j + EPS)
-    out_b_ref[...] = pltpu.roll(b, 32 - 8 * ia, 0)[:8, :64]
-    mine = x_ref[ka]
-    mine = jnp.concatenate([mine, pltpu.roll(mine, 64, 1)], axis=0) * scale_ref[...]
-    out_a_ref[...] = pltpu.roll(mine, 32 - 4 * ja, 0)[:4, :64]
+    out_ref[...] = pltpu.roll(b, 32 - 8 * ia, 0)[:8, :64]
 
 
 def call(kernel, outs, *args, scratch=(), cost=None, space=VMEM):
@@ -240,6 +252,10 @@
 
 def exchange(x, axes, groups=None):
     return lax.all_to_all(x, axes, 0, 0, tiled=True, axis_index_groups=groups)
+
+
+def other_core(x):
+    return lax.ppermute(x, "ja", [(n, n ^ 1) for n in range(8)])
 
 
 def turned(x, axis, step):
@@ -274,29 +290,37 @@
         tensor,
         scratch=[pltpu.VMEM((2, 512, LANES), F32)],
     )
-    z = keep + lax.ppermute(send, "ja", [(n, n ^ 1) for n in range(8)])
+    z = keep + other_core(send)
+    same_core = [[8 * ja + ka for ja in range(core, 8, 2) for ka in range(8)] for core in range(2)]
     z = exchange(z, "ja", [[0, 2, 4, 6], [1, 3, 5, 7]])
     u, gram_b, c_all, c_here = call(
-        combine_kernel, [(8, 16, LANES), (RANK, RANK), (RANK, 64), (RANK, LANES)], z
-    )
-    v = exchange(u, "ka")
+        combine_kernel, [(32, 16, LANES), (RANK, RANK), (RANK, 64), (RANK, LANES)], z, cost=LONG
+    )
+    v = exchange(u, ("ja", "ka"), same_core)
+    (m,) = call(turn_kernel, [(RANK, 256)], v)
     inv_a, gram_c = call(invert_a_kernel, [(RANK, RANK), (RANK, RANK)], gram_b, c_all)
-    (x,) = call(solve_kernel, [(8, 16, LANES)], v, inv_a, cost=LONG)
-    x = exchange(x, "ja")
-    w, g = call(second_kernel, [(32, 16, LANES), (8, LANES)], x, tensor, c_here)
+    w, g, a = call(
+        second_kernel,
+        [(32, 16, LANES), (8, LANES), (RANK, LANES)],
+        m,
+        other_core(m),
+        inv_a,
+        tensor,
+        c_here,
+        scratch=[pltpu.VMEM((8, RANK, LANES), F32)],
+    )
     w = exchange(w, ("ia", "ka"))
-    inv_b, scale_a = call(
+    inv_b, scale_a, out_a = call(
         lambda *refs: invert_b_kernel(total_i, *refs),
-        [(RANK, RANK), (RANK, LANES)],
+        [(RANK, RANK), (RANK, LANES), (4, 64)],
         g,
         *(turned(g, "ia", step) for step in (1, 2, 3)),
         gram_c,
+        a,
     )
     raw_b, ss = call(second_solve_kernel, [(RANK, LANES), (64, LANES)], w, inv_b, scale_a)
     ss = exchange(ss.reshape(64, 1, LANES), ("ja", "ka")).reshape(64, LANES)
-    out_a, out_b = call(
-        lambda *refs: finish_kernel(total_j, *refs), [(4, 64), (8, 64)], ss, raw_b, scale_a, x
-    )
+    (out_b,) = call(lambda *refs: finish_kernel(total_j, *refs), [(8, 64)], ss, raw_b)
     return out_a, out_b
 
 

time: 94.8 us -> 91.3 us (0.963)
  waiting for transfers between devices: 12.7 us -> 6.19 us
  blocking collectives: 59.6 us -> 62.4 us
    all_to_all x2 -> x1, waiting for transfers between devices: 8.16 us -> 1.5 us  [exchange(): return lax.all_to_all(x, axes, 0, 0, tiled=True, axis_index_groups=groups)]
    ppermute x1 -> x2, starting transfers between devices: 2.16 us -> 5.82 us  [other_core(): return lax.ppermute(x, 'ja', [(n, n ^ 1) for n in range(8)])]
    all_to_all x2 -> x1, starting transfers between devices: 7.22 us -> 4.19 us  [exchange(): return lax.all_to_all(x, axes, 0, 0, tiled=True, axis_index_groups=groups)]
    all_to_all x4, blocking collectives: 59.6 us -> 62.4 us  [exchange(): return lax.all_to_all(x, axes, 0, 0, tiled=True, axis_index_groups=groups)]
where the time goes in v4:
time: 91.3 us; the launch traced here: 91 us
  blocking collectives  62.4 us (68%)
  starting transfers between devices  13.7 us (15%)
  Pallas kernels  7.98 us (9%)
  waiting for transfers between devices  6.19 us (7%)
    all_to_all x4, blocking collectives, exchange(): return lax.all_to_all(x, axes, 0, 0, tiled=True, axis_index_groups=groups)  62.4 us
    pallas_call x9, Pallas kernels, call(): pl.pallas_call(kernel, out_shape=[jax.ShapeDtypeStruct(s, F32) for s in o...  7.98 us
    ppermute x2, starting transfers between devices, other_core(): return lax.ppermute(x, 'ja', [(n, n ^ 1) for n in range(8)])  5.82 us
    all_to_all x1, starting transfers between devices, exchange(): return lax.all_to_all(x, axes, 0, 0, tiled=True, axis_index_groups=groups)  4.19 us
    ppermute x3, starting transfers between devices, turned(): return lax.ppermute(x, axis, [(n, (n + step) % size) for n in range(size)])  3.68 us
    ppermute x3, waiting for transfers between devices, turned(): return lax.ppermute(x, axis, [(n, (n + step) % size) for n in range(size)])  3.38 us
  transfers between devices with their start and end apart: 6, of which 5 were waited for; matrix products, arithmetic and copies ran while one was open for 0% of the time, Pallas kernels for 2%

profile of v4, /device:TPU:1, one launch (start us, length us, event | category | flops | bytes accessed | tf_op | source)
XLA Modules:
  0.0 91.0 jit_solution(1512804567730141289)
XLA Ops:
  0.6 1.0 %shard_map.50 = f32[32,8,128]{2,1,0:T(8,128)S(1)} custom-call(f32[8,64]{1,0:T(8,128)} %b_hbm.1, f32[1,8]{1,0:T(1,128)} %c_hbm.1), custom_call_target="tpu_custom_call" | custom-call | flops 10000000000 | tf_op jit(solution)/shard_map/pallas_call | solution.py:242
  1.6 20.9 %all_to_all.25.y_ref = f32[32,8,128]{2,1,0:T(8,128)S(1)} all-to-all(f32[32,8,128]{2,1,0:T(8,128)S(1)} %shard_map.50), channel_id=1, replica_groups=mesh['ia'=4,'ja'=8,'ka'=8] {'ia','ka'}, dimensions={0} | all-to-all | bytes 262144 | tf_op jit(solution)/shard_map/all_to_all | solution.py:254
  22.6 1.4 %shard_map.51 = (f32[4,160,128]{2,1,0:T(8,128)S(1)}, f32[4,160,128]{2,1,0:T(8,128)S(1)}) custom-call(f32[32,8,128]{2,1,0:T(8,128)S(1)} %all_to_all.25.y_ref, bf16[8,512,512]{2,1,0:T(8,128)(2,1)S(1)} %copy-done), custom_call_target="tpu_custom_call" | custom-call | tf_op jit(solution)/shard_map/pallas_call | solution.py:242
  24.0 2.2 %collective-permute-start = (f32[4,160,128]{2,1,0:T(8,128)S(1)}, f32[4,160,128]{2,1,0:T(8,128)S(1)}, u32[]{:S(2)}, u32[]{:S(2)}) collective-permute-start(f32[4,160,128]{2,1,0:T(8,128)S(1)} %get-tuple-element.19), channel_id=1, source_target_pairs={{0,8},{8,0},{16,24},{24,16},{32,40},{40,32},{48,56},{56,48},{1,9},... | collective-permute-start | bytes 983048 | tf_op jit(solution)/shard_map/ppermute | solution.py:258
  26.1 1.3 %collective-permute-done = f32[4,160,128]{2,1,0:T(8,128)S(1)} collective-permute-done((f32[4,160,128]{2,1,0:T(8,128)S(1)}, f32[4,160,128]{2,1,0:T(8,128)S(1)}, u32[]{:S(2)}, u32[]{:S(2)}) %collective-permute-start) | collective-permute-done | bytes 327712 | tf_op jit(solution)/shard_map/ppermute | solution.py:258
  27.4 10.8 %all_to_all.26.z_ref = f32[4,160,128]{2,1,0:T(8,128)S(1)} all-to-all(f32[4,160,128]{2,1,0:T(8,128)S(1)} %add.3), channel_id=1, replica_groups={{0,16,32,48},{8,24,40,56},{1,17,33,49},{9,25,41,57},{2,18,34,50},{10,26..., dimensions={0} | all-to-all | bytes 655360 | tf_op jit(solution)/shard_map/all_to_all | solution.py:254
  38.2 0.4 shard_map.52
  38.6 12.9 %all_to_all.27.v_ref = f32[32,16,128]{2,1,0:T(8,128)S(1)} all-to-all(f32[32,16,128]{2,1,0:T(8,128)S(1)} %get-tuple-element.20), channel_id=1, replica_groups={{0,1,2,3,4,5,6,7,16,17,18,19,20,21,22,23,32,33,34,35,36,37,38,39,48,49,..., dimensions={0} | all-to-all | bytes 524288 | tf_op jit(solution)/shard_map/all_to_all | solution.py:254
  51.5 0.1 shard_map.53.mine_ref
  51.6 3.7 %collective-permute-start.1 = (f32[32,256]{1,0:T(8,128)S(1)}, f32[32,256]{1,0:T(8,128)S(1)}, u32[]{:S(2)}, u32[]{:S(2)}) collective-permute-start(f32[32,256]{1,0:T(8,128)S(1)} %shard_map.53.mine_ref), channel_id=1, source_target_pairs={{0,8},{8,0},{16,24},{24,16},{32,40},{40,32},{48,56},{56,48},{1,9},... | collective-permute-start | bytes 98312 | tf_op jit(solution)/shard_map/ppermute | solution.py:258
  55.3 0.8 shard_map.54
  56.1 0.1 collective-permute-done.1.other_ref
  56.1 2.1 %shard_map.55 = (f32[32,16,128]{2,1,0:T(8,128)}, f32[8,128]{1,0:T(8,128)S(1)}, f32[32,128]{1,0:T(8,128)S(1)}) custom-call(f32[32,256]{1,0:T(8,128)S(1)} %shard_map.53.mine_ref, f32[32,256]{1,0:T(8,128)S(1)} %collective-permute-done.1.other_ref, f32[32,32]{1,0:T(8,128)S(1)} %get-tuple-element.23.inv_ref, bf16[8,512,512]{2,1,0:T(8,128)(2,1)S(1)} %copy-done, ...), custom_call_target="tpu_custom_call" | custom-call | tf_op jit(solution)/shard_map/pallas_call | solution.py:242
  58.3 4.2 %all-to-all-start.3 = ((f32[32,16,128]{2,1,0:T(8,128)}), f32[32,16,128]{2,1,0:T(8,128)S(1)}, u32[]{:S(2)}, u32[]{:S(2)}) async-start(f32[32,16,128]{2,1,0:T(8,128)} %get-tuple-element.29), calls=%async_computation.3 | async-start | bytes 524288 | tf_op jit(solution)/shard_map/all_to_all | solution.py:254
  62.5 2.6 %collective-permute-start.4 = (f32[8,128]{1,0:T(8,128)S(1)}, f32[8,128]{1,0:T(8,128)S(1)}, u32[]{:S(2)}, u32[]{:S(2)}) collective-permute-start(f32[8,128]{1,0:T(8,128)S(1)} %get-tuple-element.25.refs_0_), channel_id=1, source_target_pairs={{0,192},{64,0},{128,64},{192,128},{1,193},{65,1},{129,65},{193,129... | collective-permute-start | bytes 12296 | tf_op jit(solution)/shard_map/ppermute | solution.py:263
  65.0 0.5 collective-permute-start.3
  65.6 0.6 collective-permute-start.2
  66.1 2.8 %collective-permute-done.3.refs_2_ = f32[8,128]{1,0:T(8,128)S(1)} collective-permute-done((f32[8,128]{1,0:T(8,128)S(1)}, f32[8,128]{1,0:T(8,128)S(1)}, u32[]{:S(2)}, u32[]{:S(2)}) %collective-permute-start.3) | collective-permute-done | bytes 4128 | tf_op jit(solution)/shard_map/ppermute | solution.py:263
  69.0 0.5 collective-permute-done.2.refs_1_
  69.5 1.1 %shard_map.56 = (f32[32,32]{1,0:T(8,128)S(1)}, f32[32,128]{1,0:T(8,128)S(1)}, f32[4,64]{1,0:T(4,128)}) custom-call(f32[8,128]{1,0:T(8,128)S(1)} %get-tuple-element.25.refs_0_, f32[8,128]{1,0:T(8,128)S(1)} %collective-permute-done.2.refs_1_, f32[8,128]{1,0:T(8,128)S(1)} %collective-permute-done.3.refs_2_, f32[8,128]{1,0:T(8,128)S(1)} %collective-permute-done.4.refs_3_, ...), custom_call_target="tpu_custom_call" | custom-call | tf_op jit(solution)/shard_map/pallas_call | solution.py:242
  70.6 1.5 %all-to-all-done.3.w_ref = f32[32,16,128]{2,1,0:T(8,128)S(1)} async-done(((f32[32,16,128]{2,1,0:T(8,128)}), f32[32,16,128]{2,1,0:T(8,128)S(1)}, u32[]{:S(2)}, u32[]{:S(2)}) %all-to-all-start.3) | async-done | bytes 262176 | tf_op jit(solution)/shard_map/all_to_all | solution.py:254
  72.1 0.3 shard_map.57
  72.5 17.8 %all_to_all.28 = f32[64,1,128]{2,1,0:T(1,128)S(1)} all-to-all(f32[64,1,128]{2,1,0:T(1,128)S(1)} %bitcast.5), channel_id=1, replica_groups=mesh['ia'=4,'ja'=8,'ka'=8] {'ja','ka'}, dimensions={0} | all-to-all | bytes 65536 | tf_op jit(solution)/shard_map/all_to_all | solution.py:254
  90.3 0.7 shard_map.58
  (4 shorter events, 0.0 us)
Async XLA Ops:
  0.6 21.9 %copy-start = (bf16[8,512,512]{2,1,0:T(8,128)(2,1)S(1)}, bf16[8,512,512]{2,1,0:T(8,128)(2,1)}, u32[]{:S(2)}) copy-start(bf16[8,512,512]{2,1,0:T(8,128)(2,1)} %t_ref.3) | copy-start | bytes 12582916
  24.0 3.4 %collective-permute-start = (f32[4,160,128]{2,1,0:T(8,128)S(1)}, f32[4,160,128]{2,1,0:T(8,128)S(1)}, u32[]{:S(2)}, u32[]{:S(2)}) collective-permute-start(f32[4,160,128]{2,1,0:T(8,128)S(1)} %get-tuple-element.19), channel_id=1, source_target_pairs={{0,8},{8,0},{16,24},{24,16},{32,40},{40,32},{48,56},{56,48},{1,9},... | collective-permute-start | bytes 983048 | tf_op jit(solution)/shard_map/ppermute | solution.py:258
  51.6 4.5 %collective-permute-start.1 = (f32[32,256]{1,0:T(8,128)S(1)}, f32[32,256]{1,0:T(8,128)S(1)}, u32[]{:S(2)}, u32[]{:S(2)}) collective-permute-start(f32[32,256]{1,0:T(8,128)S(1)} %shard_map.53.mine_ref), channel_id=1, source_target_pairs={{0,8},{8,0},{16,24},{24,16},{32,40},{40,32},{48,56},{56,48},{1,9},... | collective-permute-start | bytes 98312 | tf_op jit(solution)/shard_map/ppermute | solution.py:258
  58.3 13.9 %all-to-all-start.3 = ((f32[32,16,128]{2,1,0:T(8,128)}), f32[32,16,128]{2,1,0:T(8,128)S(1)}, u32[]{:S(2)}, u32[]{:S(2)}) async-start(f32[32,16,128]{2,1,0:T(8,128)} %get-tuple-element.29), calls=%async_computation.3 | async-start | bytes 524288 | tf_op jit(solution)/shard_map/all_to_all | solution.py:254
  62.5 3.7 %collective-permute-start.4 = (f32[8,128]{1,0:T(8,128)S(1)}, f32[8,128]{1,0:T(8,128)S(1)}, u32[]{:S(2)}, u32[]{:S(2)}) collective-permute-start(f32[8,128]{1,0:T(8,128)S(1)} %get-tuple-element.25.refs_0_), channel_id=1, source_target_pairs={{0,192},{64,0},{128,64},{192,128},{1,193},{65,1},{129,65},{193,129... | collective-permute-start | bytes 12296 | tf_op jit(solution)/shard_map/ppermute | solution.py:263
  65.0 4.0 %collective-permute-start.3 = (f32[8,128]{1,0:T(8,128)S(1)}, f32[8,128]{1,0:T(8,128)S(1)}, u32[]{:S(2)}, u32[]{:S(2)}) collective-permute-start(f32[8,128]{1,0:T(8,128)S(1)} %get-tuple-element.25.refs_0_), channel_id=1, source_target_pairs={{0,128},{64,192},{128,0},{192,64},{1,129},{65,193},{129,1},{193,65... | collective-permute-start | bytes 12296 | tf_op jit(solution)/shard_map/ppermute | solution.py:263
  65.6 4.0 %collective-permute-start.2 = (f32[8,128]{1,0:T(8,128)S(1)}, f32[8,128]{1,0:T(8,128)S(1)}, u32[]{:S(2)}, u32[]{:S(2)}) collective-permute-start(f32[8,128]{1,0:T(8,128)S(1)} %get-tuple-element.25.refs_0_), channel_id=1, source_target_pairs={{0,64},{64,128},{128,192},{192,0},{1,65},{65,129},{129,193},{193,1... | collective-permute-start | bytes 12296 | tf_op jit(solution)/shard_map/ppermute | solution.py:263

commit v5 on v4

--- a/solution.py
+++ b/solution.py
@@ -90,8 +90,9 @@
         y_ref[n] = tile
 
 
-def first_kernel(y_ref, t_ref, keep_ref, send_ref, scratch):
-    core = lax.axis_index("ja") % 2
+def first_kernel(other, y_ref, t_ref, *refs):
+    out_ref, extra_ref = refs if other else refs[::-1]
+    ja = lax.axis_index("ja")
     lane = iota((8, LANES), 1)
     b_rows, c_rows = [], []
     for ia in range(4):
@@ -103,9 +104,11 @@
         b_rows.append(jnp.concatenate(pairs, axis=1))
         c_rows.append(sum(parts[1:], parts[0]))
     b = jnp.concatenate(b_rows, axis=0)
-    c = jnp.concatenate(c_rows, axis=0)
-    gram = dot_nt(b, jnp.concatenate([b, jnp.zeros((96, 512), F32)], axis=0))
-    extra = jnp.where(iota((32, LANES), 1) < 64, gram, c)
+    if other:
+        c = jnp.concatenate(c_rows, axis=0)
+        gram = dot_nt(b, jnp.concatenate([b, jnp.zeros((96, 512), F32)], axis=0))
+        extra_ref[...] = jnp.where(iota((32, LANES), 1) < 64, gram, c)
+    extra = extra_ref[...]
     high, low = split(b)
 
     def placed(part, q):
@@ -115,21 +118,27 @@
     weights = jnp.concatenate(
         [jnp.concatenate(placed(high, q) + placed(low, q), axis=0) for q in range(4)], axis=1
     )
+    core = 1 - ja % 2 if other else ja % 2
+    starts = [pl.multiple_of(64 * (2 * ((ja // 2 + n) % 4) + core), 64) for n in range(4)]
     for h in range(2):
-        left = jnp.concatenate([t_ref[4 * h + q] for q in range(4)], axis=1)
+        left = jnp.concatenate(
+            [
+                jnp.concatenate([t_ref[4 * h + q, pl.ds(start, 64), :] for start in starts], axis=0)
+                for q in range(4)
+            ],
+            axis=1,
+        )
         both = lax.dot_general(left, weights, NT, preferred_element_type=F32)
-        scratch[h] = both[:, :LANES] + both[:, LANES:]
+        y = both[:, :LANES] + both[:, LANES:]
+        for n in range(4):
+            out_ref[n, 64 * h : 64 * h + 64, :] = y[64 * n : 64 * n + 64]
     for n in range(4):
-        for ref, which in ((keep_ref, core), (send_ref, 1 - core)):
-            start = pl.multiple_of(64 * (2 * n + which), 64)
-            for h in range(2):
-                ref[n, 64 * h : 64 * h + 64, :] = scratch[h, pl.ds(start, 64), :]
-            ref[n, 128:160, :] = extra
-
-
-def combine_kernel(z_ref, u_ref, gram_ref, c_all_ref, c_ref):
+        out_ref[n, 128:160, :] = extra
+
+
+def combine_kernel(z0_ref, z1_ref, z2_ref, z3_ref, u_ref, gram_ref, c_all_ref, c_ref):
     ka = lax.axis_index("ka")
-    z = total(z_ref)
+    z = (z0_ref[...] + z1_ref[...]) + (z2_ref[...] + z3_ref[...])
     extra = z[128:160]
     gram_ref[...] = extra[:, :32]
     c_all_ref[...] = pltpu.roll(extra, 64, 1)[:, :64]
@@ -166,8 +175,10 @@
     m_ref[...] = jnp.concatenate(parts, axis=0).T
 
 
-def second_kernel(mine_ref, other_ref, inv_ref, t_ref, c_ref, w_ref, g_ref, a_ref, scratch):
-    ka, core = lax.axis_index("ka"), lax.axis_index("ja") % 2
+def second_kernel(
+    mine_ref, other_ref, inv_ref, t_ref, c_ref, p0_ref, p1_ref, p2_ref, p3_ref, a_ref, scratch, quarters
+):
+    ia, ka, core = lax.axis_index("ia"), lax.axis_index("ka"), lax.axis_index("ja") % 2
     low_lanes = iota((RANK, LANES), 1) < 64
     even = jnp.where(core == 0, mine_ref[...], other_ref[...])
     odd = jnp.where(core == 0, other_ref[...], mine_ref[...])
@@ -183,7 +194,7 @@
         scratch[2 * q] = pair
         scratch[2 * q + 1] = pltpu.roll(pair, 64, 1)
     a_ref[...] = scratch[ka]
-    g_ref[...] = folded_gram(a)
+    gram = folded_gram(a)
     c = c_ref[...]
     highs, lows = [], []
     for k in range(8):
@@ -193,49 +204,47 @@
     left = jnp.concatenate([jnp.concatenate(highs, axis=1), jnp.concatenate(lows, axis=1)], axis=0)
     both = jnp.dot(left, t_ref[...].reshape(4096, 512), preferred_element_type=F32)
     out = both[:RANK] + both[RANK:]
-    low_lanes = low_lanes[:16]
     for q in range(4):
-        pair = out[:, 128 * q : 128 * q + 128]
-        turned = pltpu.roll(pair, 64, 1)
-        even = jnp.where(low_lanes, pair[:16], turned[16:])
-        odd = jnp.where(low_lanes, turned[:16], pair[16:])
-        for ia in range(4):
-            w_ref[8 * ia + 2 * q] = even
-            w_ref[8 * ia + 2 * q + 1] = odd
-
-
-def invert_b_kernel(
-    total_i, g0_ref, g1_ref, g2_ref, g3_ref, gram_c_ref, a_ref, inv_ref, scale_ref, out_ref
-):
-    ja = lax.axis_index("ja")
-    gram = unfold((g0_ref[...] + g1_ref[...]) + (g2_ref[...] + g3_ref[...]))
+        quarters[q] = out[:, 128 * q : 128 * q + 128]
+    for n, ref in enumerate((p0_ref, p1_ref, p2_ref, p3_ref)):
+        ref[:RANK] = quarters[(ia + n) % 4]
+        ref[RANK:] = gram
+
+
+def sum_kernel(p0_ref, p1_ref, p2_ref, p3_ref, u_ref, gram_ref):
+    p = (p0_ref[...] + p1_ref[...]) + (p2_ref[...] + p3_ref[...])
+    for n in range(8):
+        u_ref[n] = p[:RANK]
+    gram_ref[...] = p[RANK:]
+
+
+def second_solve_kernel(total_i, u_ref, gram_ref, gram_c_ref, ss_ref, scale_ref):
+    half = lax.axis_index("ka") % 2
+    gram = unfold(gram_ref[...])
     diag = jnp.where(iota(gram.shape, 0) == iota(gram.shape, 1), gram, 0.0)
     scale_col = 1.0 / jnp.sqrt(jnp.sum(diag, axis=1, keepdims=True) / total_i + EPS)
     scale_row = 1.0 / jnp.sqrt(jnp.sum(diag, axis=0, keepdims=True) / total_i + EPS)
-    inv_ref[...] = inverse(gram * scale_col * scale_row * gram_c_ref[...])
+    inv = inverse(gram * scale_col * scale_row * gram_c_ref[...])
     scale_ref[...] = jnp.broadcast_to(scale_col, (RANK, LANES))
-    out_ref[...] = pltpu.roll(a_ref[...] * scale_col, 32 - 4 * ja, 0)[:4, :64]
-
-
-def second_solve_kernel(w_ref, inv_ref, scale_ref, raw_ref, ss_ref):
-    s = total(w_ref)
-    m = jnp.concatenate([s, pltpu.roll(s, 64, 1)], axis=0) * scale_ref[...]
-    raw = jnp.dot(inv_ref[...], m, precision=HIGH, preferred_element_type=F32)
-    raw_ref[...] = raw
-    square = jnp.where(iota(raw.shape, 1) < 64, raw * raw, 0.0)
-    ss = jnp.sum(square, axis=1, keepdims=True)
-    eye = iota((RANK, LANES), 0) == iota((RANK, LANES), 1)
-    ss_row = jnp.sum(jnp.where(eye, ss, 0.0), axis=0, keepdims=True)
-    ss_ref[...] = jnp.broadcast_to(ss_row, ss_ref.shape)
-
-
-def finish_kernel(total_j, ss_ref, raw_ref, out_ref):
-    ia = lax.axis_index("ia")
-    ss_row = jnp.sum(ss_ref[...], axis=0, keepdims=True)
-    eye = iota((RANK, LANES), 0) == iota((RANK, LANES), 1)
-    ss = jnp.sum(jnp.where(eye, ss_row, 0.0), axis=1, keepdims=True)
-    b = raw_ref[...] / jnp.sqrt(ss / total_j + EPS)
-    out_ref[...] = pltpu.roll(b, 32 - 8 * ia, 0)[:8, :64]
+    m = total(u_ref) * scale_col
+    raw = jnp.dot(inv, m, precision=HIGH, preferred_element_type=F32)
+    ss = jnp.sum(raw * raw, axis=1, keepdims=True)
+    place = iota((RANK, LANES), 0) + 64 == iota((RANK, LANES), 1)
+    ss_row = jnp.sum(jnp.where(place, ss, 0.0), axis=0, keepdims=True)
+    raw = jnp.where(half == 0, raw, pltpu.roll(raw, 64, 1))
+    tile = jnp.where(iota((RANK, LANES), 1) < 64, raw, ss_row)
+    for n in range(32):
+        ia = n // 8
+        ss_ref[n] = tile[8 * ia : 8 * ia + 8]
+
+
+def finish_kernel(total_j, ss_ref, a_ref, scale_ref, out_a_ref, out_b_ref):
+    ia, ja, ka = lax.axis_index("ia"), lax.axis_index("ja"), lax.axis_index("ka")
+    place = iota((8, LANES), 1) == iota((8, LANES), 0) + (64 + 8 * ia)
+    ss = jnp.sum(jnp.where(place, total(ss_ref), 0.0), axis=1, keepdims=True)
+    b = ss_ref[8 * (ka // 2) + ja] / jnp.sqrt(ss / total_j + EPS)
+    out_b_ref[...] = b[:, :64]
+    out_a_ref[...] = pltpu.roll(a_ref[...] * scale_ref[...], 32 - 4 * ja, 0)[:4, :64]
 
 
 def call(kernel, outs, *args, scratch=(), cost=None, space=VMEM):
@@ -283,44 +292,45 @@
         space=HBM,
     )
     y = exchange(y, ("ia", "ka"))
-    keep, send = call(
-        first_kernel,
-        [(4, 160, LANES), (4, 160, LANES)],
-        y,
-        tensor,
-        scratch=[pltpu.VMEM((2, 512, LANES), F32)],
-    )
-    z = keep + other_core(send)
+    half = (4, 160, LANES)
+    send, extra = call(
+        lambda *refs: first_kernel(True, *refs), [half, (RANK, LANES)], y, tensor
+    )
+    received = other_core(send)
+    (keep,) = call(lambda *refs: first_kernel(False, *refs), [half], y, tensor, extra)
+    z = [keep[n] + received[n] for n in range(4)]
+    z = [z[0]] + [turned(z[n], "ja", 2 * n) for n in range(1, 4)]
     same_core = [[8 * ja + ka for ja in range(core, 8, 2) for ka in range(8)] for core in range(2)]
-    z = exchange(z, "ja", [[0, 2, 4, 6], [1, 3, 5, 7]])
     u, gram_b, c_all, c_here = call(
-        combine_kernel, [(32, 16, LANES), (RANK, RANK), (RANK, 64), (RANK, LANES)], z, cost=LONG
+        combine_kernel, [(32, 16, LANES), (RANK, RANK), (RANK, 64), (RANK, LANES)], *z, cost=LONG
     )
     v = exchange(u, ("ja", "ka"), same_core)
     (m,) = call(turn_kernel, [(RANK, 256)], v)
     inv_a, gram_c = call(invert_a_kernel, [(RANK, RANK), (RANK, RANK)], gram_b, c_all)
-    w, g, a = call(
+    *p, a = call(
         second_kernel,
-        [(32, 16, LANES), (8, LANES), (RANK, LANES)],
+        [(40, LANES)] * 4 + [(RANK, LANES)],
         m,
         other_core(m),
         inv_a,
         tensor,
         c_here,
-        scratch=[pltpu.VMEM((8, RANK, LANES), F32)],
-    )
-    w = exchange(w, ("ia", "ka"))
-    inv_b, scale_a, out_a = call(
-        lambda *refs: invert_b_kernel(total_i, *refs),
-        [(RANK, RANK), (RANK, LANES), (4, 64)],
-        g,
-        *(turned(g, "ia", step) for step in (1, 2, 3)),
+        scratch=[pltpu.VMEM((8, RANK, LANES), F32), pltpu.VMEM((4, RANK, LANES), F32)],
+    )
+    p = [p[0]] + [turned(p[n], "ia", n) for n in range(1, 4)]
+    u, gram_a = call(sum_kernel, [(8, RANK, LANES), (8, LANES)], *p)
+    u = exchange(u, "ka")
+    ss, scale_a = call(
+        lambda *refs: second_solve_kernel(total_i, *refs),
+        [(32, 8, LANES), (RANK, LANES)],
+        u,
+        gram_a,
         gram_c,
-        a,
-    )
-    raw_b, ss = call(second_solve_kernel, [(RANK, LANES), (64, LANES)], w, inv_b, scale_a)
-    ss = exchange(ss.reshape(64, 1, LANES), ("ja", "ka")).reshape(64, LANES)
-    (out_b,) = call(lambda *refs: finish_kernel(total_j, *refs), [(8, 64)], ss, raw_b)
+    )
+    ss = exchange(ss, ("ia", "ja"))
+    out_a, out_b = call(
+        lambda *refs: finish_kernel(total_j, *refs), [(4, 64), (8, 64)], ss, a, scale_a
+    )
     return out_a, out_b
 
 

time: 91.3 us -> 88.5 us (0.969)
  blocking collectives: 62.4 us -> 61 us
    ppermute x3 -> x6, starting transfers between devices: 3.68 us -> 8.21 us  [turned(): return lax.ppermute(x, axis, [(n, (n + step) % size) for n in range(size)])]
    all_to_all x1 -> x0, starting transfers between devices: 4.19 us -> none  [exchange(): return lax.all_to_all(x, axes, 0, 0, tiled=True, axis_index_groups=groups)]
    all_to_all x1 -> x0, waiting for transfers between devices: 1.5 us -> none  [exchange(): return lax.all_to_all(x, axes, 0, 0, tiled=True, axis_index_groups=groups)]
    all_to_all x4, blocking collectives: 62.4 us -> 61 us  [exchange(): return lax.all_to_all(x, axes, 0, 0, tiled=True, axis_index_groups=groups)]
    ppermute x3 -> x6, waiting for transfers between devices: 3.38 us -> 4.77 us  [turned(): return lax.ppermute(x, axis, [(n, (n + step) % size) for n in range(size)])]
    pallas_call x9 -> x10, Pallas kernels: 7.98 us -> 7.09 us  [call(): pl.pallas_call(kernel, out_shape=[jax.ShapeDtypeStruct(s, F32) for s in o...]
  transfers between devices with their start and end apart: 6 -> 8, of which waited for: 5 -> 6; matrix products, arithmetic and copies ran while one was open for 0% -> 0% of each run, Pallas kernels for 2% -> 2%
where the time goes in v5:
time: 88.5 us; the launch traced here: 88.3 us
  blocking collectives  61 us (69%)
  starting transfers between devices  14.1 us (16%)
  Pallas kernels  7.09 us (8%)
  waiting for transfers between devices  5.3 us (6%)
    all_to_all x4, blocking collectives, exchange(): return lax.all_to_all(x, axes, 0, 0, tiled=True, axis_index_groups=groups)  61 us
    ppermute x6, starting transfers between devices, turned(): return lax.ppermute(x, axis, [(n, (n + step) % size) for n in range(size)])  8.21 us
    pallas_call x10, Pallas kernels, call(): pl.pallas_call(kernel, out_shape=[jax.ShapeDtypeStruct(s, F32) for s in o...  7.09 us
    ppermute x2, starting transfers between devices, other_core(): return lax.ppermute(x, 'ja', [(n, n ^ 1) for n in range(8)])  5.89 us
    ppermute x6, waiting for transfers between devices, turned(): return lax.ppermute(x, axis, [(n, (n + step) % size) for n in range(size)])  4.77 us
  transfers between devices with their start and end apart: 8, of which 6 were waited for; matrix products, arithmetic and copies ran while one was open for 0% of the time, Pallas kernels for 2%

profile of v5, /device:TPU:1, one launch (start us, length us, event | category | flops | bytes accessed | tf_op | source)
XLA Modules:
  0.0 88.3 jit_solution(1802204088302036784)
XLA Ops:
  0.6 1.0 %shard_map.50 = f32[32,8,128]{2,1,0:T(8,128)S(1)} custom-call(f32[8,64]{1,0:T(8,128)} %b_hbm.1, f32[1,8]{1,0:T(1,128)} %c_hbm.1), custom_call_target="tpu_custom_call" | custom-call | flops 10000000000 | tf_op jit(solution)/shard_map/pallas_call | solution.py:251
  1.6 20.9 %all_to_all.20.refs_0_ = f32[32,8,128]{2,1,0:T(8,128)S(1)} all-to-all(f32[32,8,128]{2,1,0:T(8,128)S(1)} %shard_map.50), channel_id=1, replica_groups=mesh['ia'=4,'ja'=8,'ka'=8] {'ia','ka'}, dimensions={0} | all-to-all | bytes 262144 | tf_op jit(solution)/shard_map/all_to_all | solution.py:263
  22.6 0.8 shard_map.51
  23.4 2.2 %collective-permute-start = (f32[4,160,128]{2,1,0:T(8,128)S(1)}, f32[4,160,128]{2,1,0:T(8,128)S(1)}, u32[]{:S(2)}, u32[]{:S(2)}) collective-permute-start(f32[4,160,128]{2,1,0:T(8,128)S(1)} %get-tuple-element.20), channel_id=1, source_target_pairs={{0,8},{8,0},{16,24},{24,16},{32,40},{40,32},{48,56},{56,48},{1,9},... | collective-permute-start | bytes 983048 | tf_op jit(solution)/shard_map/ppermute | solution.py:267
  25.5 0.8 shard_map.52
  26.3 0.5 collective-permute-done
  26.8 1.4 %collective-permute-start.1 = (f32[160,128]{1,0:T(8,128)S(1)}, f32[160,128]{1,0:T(8,128)S(1)}, u32[]{:S(2)}, u32[]{:S(2)}) collective-permute-start(f32[160,128]{1,0:T(8,128)S(1)} %get-tuple-element.38), channel_id=1, source_target_pairs={{0,16},{8,24},{16,32},{24,40},{32,48},{40,56},{48,0},{56,8},{1,17}... | collective-permute-start | bytes 245768 | tf_op jit(solution)/shard_map/ppermute | solution.py:272
  28.2 2.6 %collective-permute-start.2 = (f32[160,128]{1,0:T(8,128)S(1)}, f32[160,128]{1,0:T(8,128)S(1)}, u32[]{:S(2)}, u32[]{:S(2)}) collective-permute-start(f32[160,128]{1,0:T(8,128)S(1)} %get-tuple-element.37), channel_id=1, source_target_pairs={{0,32},{8,40},{16,48},{24,56},{32,0},{40,8},{48,16},{56,24},{1,33}... | collective-permute-start | bytes 245768 | tf_op jit(solution)/shard_map/ppermute | solution.py:272
  30.8 1.1 %collective-permute-start.3 = (f32[160,128]{1,0:T(8,128)S(1)}, f32[160,128]{1,0:T(8,128)S(1)}, u32[]{:S(2)}, u32[]{:S(2)}) collective-permute-start(f32[160,128]{1,0:T(8,128)S(1)} %get-tuple-element.36), channel_id=1, source_target_pairs={{0,48},{8,56},{16,0},{24,8},{32,16},{40,24},{48,32},{56,40},{1,49}... | collective-permute-start | bytes 245768 | tf_op jit(solution)/shard_map/ppermute | solution.py:272
  31.9 2.9 %collective-permute-done.2.z2_ref = f32[160,128]{1,0:T(8,128)S(1)} collective-permute-done((f32[160,128]{1,0:T(8,128)S(1)}, f32[160,128]{1,0:T(8,128)S(1)}, u32[]{:S(2)}, u32[]{:S(2)}) %collective-permute-start.2) | collective-permute-done | bytes 81952 | tf_op jit(solution)/shard_map/ppermute | solution.py:272
  35.2 13.9 %all_to_all.21.v_ref = f32[32,16,128]{2,1,0:T(8,128)S(1)} all-to-all(f32[32,16,128]{2,1,0:T(8,128)S(1)} %get-tuple-element.21), channel_id=1, replica_groups={{0,1,2,3,4,5,6,7,16,17,18,19,20,21,22,23,32,33,34,35,36,37,38,39,48,49,..., dimensions={0} | all-to-all | bytes 524288 | tf_op jit(solution)/shard_map/all_to_all | solution.py:263
  49.2 3.7 %collective-permute-start.4 = (f32[32,256]{1,0:T(8,128)S(1)}, f32[32,256]{1,0:T(8,128)S(1)}, u32[]{:S(2)}, u32[]{:S(2)}) collective-permute-start(f32[32,256]{1,0:T(8,128)S(1)} %shard_map.54.mine_ref), channel_id=1, source_target_pairs={{0,8},{8,0},{16,24},{24,16},{32,40},{40,32},{48,56},{56,48},{1,9},... | collective-permute-start | bytes 98312 | tf_op jit(solution)/shard_map/ppermute | solution.py:267
  52.9 0.8 shard_map.55
  53.8 1.4 %shard_map.56 = (f32[40,128]{1,0:T(8,128)S(1)}, f32[40,128]{1,0:T(8,128)S(1)}, f32[40,128]{1,0:T(8,128)S(1)}, f32[40,128]{1,0:T(8,128)S(1)}, f32[32,128]{1,0:T(8,128)S(1)}) custom-call(f32[32,256]{1,0:T(8,128)S(1)} %shard_map.54.mine_ref, f32[32,256]{1,0:T(8,128)S(1)} %collective-permute-done.4.other_ref, f32[32,32]{1,0:T(8,128)S(1)} %get-tuple-element.24.inv_ref, ...), custom_call_target="tpu_custom_call" | custom-call | tf_op jit(solution)/shard_map/pallas_call | solution.py:251
  55.1 0.4 collective-permute-start.5
  55.6 1.7 %collective-permute-start.6 = (f32[40,128]{1,0:T(8,128)S(1)}, f32[40,128]{1,0:T(8,128)S(1)}, u32[]{:S(2)}, u32[]{:S(2)}) collective-permute-start(f32[40,128]{1,0:T(8,128)S(1)} %get-tuple-element.28), channel_id=1, source_target_pairs={{0,128},{64,192},{128,0},{192,64},{1,129},{65,193},{129,1},{193,65... | collective-permute-start | bytes 61448 | tf_op jit(solution)/shard_map/ppermute | solution.py:272
  57.3 1.0 %collective-permute-start.7 = (f32[40,128]{1,0:T(8,128)S(1)}, f32[40,128]{1,0:T(8,128)S(1)}, u32[]{:S(2)}, u32[]{:S(2)}) collective-permute-start(f32[40,128]{1,0:T(8,128)S(1)} %get-tuple-element.29), channel_id=1, source_target_pairs={{0,192},{64,0},{128,64},{192,128},{1,193},{65,1},{129,65},{193,129... | collective-permute-start | bytes 61448 | tf_op jit(solution)/shard_map/ppermute | solution.py:272
  58.3 0.8 collective-permute-done.5.p1_ref
  59.1 0.6 collective-permute-done.6.p2_ref
  59.7 0.5 collective-permute-done.7.p3_ref
  60.2 10.9 %all_to_all.22.refs_0_ = f32[8,32,128]{2,1,0:T(8,128)S(1)} all-to-all(f32[8,32,128]{2,1,0:T(8,128)S(1)} %get-tuple-element.30), channel_id=1, replica_groups=mesh['ia'=4,'ja'=8,'ka'=8] {'ka'}, dimensions={0} | all-to-all | bytes 262144 | tf_op jit(solution)/shard_map/all_to_all | solution.py:263
  71.1 1.1 %shard_map.58 = (f32[32,8,128]{2,1,0:T(8,128)S(1)}, f32[32,128]{1,0:T(8,128)S(1)}) custom-call(f32[8,32,128]{2,1,0:T(8,128)S(1)} %all_to_all.22.refs_0_, f32[8,128]{1,0:T(8,128)S(1)} %get-tuple-element.31.refs_1_, f32[32,32]{1,0:T(8,128)S(1)} %get-tuple-element.32.refs_2_), custom_call_target="tpu_custom_call" | custom-call | tf_op jit(solution)/shard_map/pallas_call | solution.py:251
  72.2 15.3 %all_to_all.23.refs_0_ = f32[32,8,128]{2,1,0:T(8,128)S(1)} all-to-all(f32[32,8,128]{2,1,0:T(8,128)S(1)} %get-tuple-element.33), channel_id=1, replica_groups=mesh['ia'=4,'ja'=8,'ka'=8] {'ia','ja'}, dimensions={0} | all-to-all | bytes 262144 | tf_op jit(solution)/shard_map/all_to_all | solution.py:263
  87.5 0.7 shard_map.59
  (9 shorter events, 0.6 us)
Async XLA Ops:
  0.6 21.9 %copy-start = (bf16[8,512,512]{2,1,0:T(8,128)(2,1)S(1)}, bf16[8,512,512]{2,1,0:T(8,128)(2,1)}, u32[]{:S(2)}) copy-start(bf16[8,512,512]{2,1,0:T(8,128)(2,1)} %t_ref.1) | copy-start | bytes 12582916
  23.4 3.4 %collective-permute-start = (f32[4,160,128]{2,1,0:T(8,128)S(1)}, f32[4,160,128]{2,1,0:T(8,128)S(1)}, u32[]{:S(2)}, u32[]{:S(2)}) collective-permute-start(f32[4,160,128]{2,1,0:T(8,128)S(1)} %get-tuple-element.20), channel_id=1, source_target_pairs={{0,8},{8,0},{16,24},{24,16},{32,40},{40,32},{48,56},{56,48},{1,9},... | collective-permute-start | bytes 983048 | tf_op jit(solution)/shard_map/ppermute | solution.py:267
  26.8 5.1 %collective-permute-start.1 = (f32[160,128]{1,0:T(8,128)S(1)}, f32[160,128]{1,0:T(8,128)S(1)}, u32[]{:S(2)}, u32[]{:S(2)}) collective-permute-start(f32[160,128]{1,0:T(8,128)S(1)} %get-tuple-element.38), channel_id=1, source_target_pairs={{0,16},{8,24},{16,32},{24,40},{32,48},{40,56},{48,0},{56,8},{1,17}... | collective-permute-start | bytes 245768 | tf_op jit(solution)/shard_map/ppermute | solution.py:272
  28.2 6.6 %collective-permute-start.2 = (f32[160,128]{1,0:T(8,128)S(1)}, f32[160,128]{1,0:T(8,128)S(1)}, u32[]{:S(2)}, u32[]{:S(2)}) collective-permute-start(f32[160,128]{1,0:T(8,128)S(1)} %get-tuple-element.37), channel_id=1, source_target_pairs={{0,32},{8,40},{16,48},{24,56},{32,0},{40,8},{48,16},{56,24},{1,33}... | collective-permute-start | bytes 245768 | tf_op jit(solution)/shard_map/ppermute | solution.py:272
  30.8 3.9 %collective-permute-start.3 = (f32[160,128]{1,0:T(8,128)S(1)}, f32[160,128]{1,0:T(8,128)S(1)}, u32[]{:S(2)}, u32[]{:S(2)}) collective-permute-start(f32[160,128]{1,0:T(8,128)S(1)} %get-tuple-element.36), channel_id=1, source_target_pairs={{0,48},{8,56},{16,0},{24,8},{32,16},{40,24},{48,32},{56,40},{1,49}... | collective-permute-start | bytes 245768 | tf_op jit(solution)/shard_map/ppermute | solution.py:272
  49.2 4.6 %collective-permute-start.4 = (f32[32,256]{1,0:T(8,128)S(1)}, f32[32,256]{1,0:T(8,128)S(1)}, u32[]{:S(2)}, u32[]{:S(2)}) collective-permute-start(f32[32,256]{1,0:T(8,128)S(1)} %shard_map.54.mine_ref), channel_id=1, source_target_pairs={{0,8},{8,0},{16,24},{24,16},{32,40},{40,32},{48,56},{56,48},{1,9},... | collective-permute-start | bytes 98312 | tf_op jit(solution)/shard_map/ppermute | solution.py:267
  55.1 3.9 %collective-permute-start.5 = (f32[40,128]{1,0:T(8,128)S(1)}, f32[40,128]{1,0:T(8,128)S(1)}, u32[]{:S(2)}, u32[]{:S(2)}) collective-permute-start(f32[40,128]{1,0:T(8,128)S(1)} %get-tuple-element.27), channel_id=1, source_target_pairs={{0,64},{64,128},{128,192},{192,0},{1,65},{65,129},{129,193},{193,1... | collective-permute-start | bytes 61448 | tf_op jit(solution)/shard_map/ppermute | solution.py:272
  55.6 4.1 %collective-permute-start.6 = (f32[40,128]{1,0:T(8,128)S(1)}, f32[40,128]{1,0:T(8,128)S(1)}, u32[]{:S(2)}, u32[]{:S(2)}) collective-permute-start(f32[40,128]{1,0:T(8,128)S(1)} %get-tuple-element.28), channel_id=1, source_target_pairs={{0,128},{64,192},{128,0},{192,64},{1,129},{65,193},{129,1},{193,65... | collective-permute-start | bytes 61448 | tf_op jit(solution)/shard_map/ppermute | solution.py:272
  57.3 2.9 %collective-permute-start.7 = (f32[40,128]{1,0:T(8,128)S(1)}, f32[40,128]{1,0:T(8,128)S(1)}, u32[]{:S(2)}, u32[]{:S(2)}) collective-permute-start(f32[40,128]{1,0:T(8,128)S(1)} %get-tuple-element.29), channel_id=1, source_target_pairs={{0,192},{64,0},{128,64},{192,128},{1,193},{65,1},{129,65},{193,129... | collective-permute-start | bytes 61448 | tf_op jit(solution)/shard_map/ppermute | solution.py:272

commit v6 on v5

--- a/solution.py
+++ b/solution.py
@@ -80,34 +80,38 @@
         copy.start()
     for copy in copies:
         copy.wait()
-    ja, ka = lax.axis_index("ja"), lax.axis_index("ka")
-    row, lane = iota((8, LANES), 0), iota((8, LANES), 1)
+    lane = iota((1, LANES), 1)
     c_tiled = jnp.concatenate([c_ref[...]] * 16, axis=1)
-    c_placed = jnp.where((row == ja) & (lane // 8 == 8 + ka), c_tiled, 0.0)
-    b_wide = jnp.concatenate([b_ref[...], jnp.zeros((8, 64), F32)], axis=1)
-    tile = jnp.where(lane < 64, b_wide, c_placed)
+    c_row = jnp.where(lane // 8 == 8 + lax.axis_index("ka"), c_tiled, 0.0)
+    b_pairs = jnp.concatenate([b_ref[:4], b_ref[4:]], axis=1)
+    tile = jnp.concatenate([b_pairs, c_row], axis=0)
     for n in range(32):
-        y_ref[n] = tile
+        y_ref[5 * n : 5 * n + 5] = tile
 
 
 def first_kernel(other, y_ref, t_ref, *refs):
     out_ref, extra_ref = refs if other else refs[::-1]
     ja = lax.axis_index("ja")
-    lane = iota((8, LANES), 1)
-    b_rows, c_rows = [], []
+    low_lanes = iota((4, LANES), 1) < 64
+    b_rows = []
     for ia in range(4):
-        parts = [y_ref[8 * ia + ka] for ka in range(8)]
-        pairs = [
-            jnp.where(lane < 64, parts[2 * q], pltpu.roll(parts[2 * q + 1], 64, 1))
-            for q in range(4)
-        ]
+        starts = [5 * (8 * ia + ka) for ka in range(8)]
+        parts = [y_ref[start : start + 4] for start in starts]
+        pairs = []
+        for one, two in zip(parts[::2], parts[1::2]):
+            top = jnp.where(low_lanes, one, pltpu.roll(two, 64, 1))
+            bottom = jnp.where(low_lanes, pltpu.roll(one, 64, 1), two)
+            pairs.append(jnp.concatenate([top, bottom], axis=0))
         b_rows.append(jnp.concatenate(pairs, axis=1))
-        c_rows.append(sum(parts[1:], parts[0]))
     b = jnp.concatenate(b_rows, axis=0)
     if other:
-        c = jnp.concatenate(c_rows, axis=0)
-        gram = dot_nt(b, jnp.concatenate([b, jnp.zeros((96, 512), F32)], axis=0))
-        extra_ref[...] = jnp.where(iota((32, LANES), 1) < 64, gram, c)
+        extra = dot_nt(b, jnp.concatenate([b, jnp.zeros((96, 512), F32)], axis=0))
+        row, lane = iota((RANK, LANES), 0), iota((RANK, LANES), 1)
+        for ia in range(4):
+            starts = [5 * (8 * ia + ka) + 4 for ka in range(8)]
+            c_row = sum(y_ref[start : start + 1] for start in starts)
+            extra = jnp.where((lane >= 64) & (row == 8 * ia + ja), c_row, extra)
+        extra_ref[...] = extra
     extra = extra_ref[...]
     high, low = split(b)
 
@@ -229,22 +233,28 @@
     m = total(u_ref) * scale_col
     raw = jnp.dot(inv, m, precision=HIGH, preferred_element_type=F32)
     ss = jnp.sum(raw * raw, axis=1, keepdims=True)
-    place = iota((RANK, LANES), 0) + 64 == iota((RANK, LANES), 1)
+    place = iota((RANK, LANES), 0) == iota((RANK, LANES), 1)
     ss_row = jnp.sum(jnp.where(place, ss, 0.0), axis=0, keepdims=True)
     raw = jnp.where(half == 0, raw, pltpu.roll(raw, 64, 1))
-    tile = jnp.where(iota((RANK, LANES), 1) < 64, raw, ss_row)
-    for n in range(32):
-        ia = n // 8
-        ss_ref[n] = tile[8 * ia : 8 * ia + 8]
+    turned_raw = pltpu.roll(raw, 64, 1)
+    low_lanes = iota((4, LANES), 1) < 64
+    for ia in range(4):
+        data = jnp.where(low_lanes, raw[8 * ia : 8 * ia + 4], turned_raw[8 * ia + 4 : 8 * ia + 8])
+        tile = jnp.concatenate([data, ss_row], axis=0)
+        for ja in range(8):
+            start = 5 * (8 * ia + ja)
+            ss_ref[start : start + 5] = tile
 
 
 def finish_kernel(total_j, ss_ref, a_ref, scale_ref, out_a_ref, out_b_ref):
     ia, ja, ka = lax.axis_index("ia"), lax.axis_index("ja"), lax.axis_index("ka")
-    place = iota((8, LANES), 1) == iota((8, LANES), 0) + (64 + 8 * ia)
-    ss = jnp.sum(jnp.where(place, total(ss_ref), 0.0), axis=1, keepdims=True)
-    b = ss_ref[8 * (ka // 2) + ja] / jnp.sqrt(ss / total_j + EPS)
+    place = iota((8, LANES), 1) == iota((8, LANES), 0) + 8 * ia
+    ss_row = jnp.sum(ss_ref[pl.ds(4, 32, stride=5), :], axis=0, keepdims=True)
+    ss = jnp.sum(jnp.where(place, ss_row, 0.0), axis=1, keepdims=True)
+    data = ss_ref[pl.ds(5 * (8 * (ka // 2) + ja), 4), :]
+    b = jnp.concatenate([data, pltpu.roll(data, 64, 1)], axis=0) / jnp.sqrt(ss / total_j + EPS)
     out_b_ref[...] = b[:, :64]
-    out_a_ref[...] = pltpu.roll(a_ref[...] * scale_ref[...], 32 - 4 * ja, 0)[:4, :64]
+    out_a_ref[...] = pltpu.roll(a_ref[...] * scale_ref[...], (32 - 4 * ja) % 32, 0)[:4, :64]
 
 
 def call(kernel, outs, *args, scratch=(), cost=None, space=VMEM):
@@ -280,7 +290,7 @@
     )
     (y,) = call(
         start_kernel,
-        [(32, 8, LANES)],
+        [(160, LANES)],
         factor_b,
         factor_c,
         scratch=[
@@ -291,7 +301,7 @@
         cost=LONG,
         space=HBM,
     )
-    y = exchange(y, ("ia", "ka"))
+    y = exchange(y.reshape(32, 1, 5 * LANES), ("ia", "ka")).reshape(160, LANES)
     half = (4, 160, LANES)
     send, extra = call(
         lambda *refs: first_kernel(True, *refs), [half, (RANK, LANES)], y, tensor
@@ -322,12 +332,12 @@
     u = exchange(u, "ka")
     ss, scale_a = call(
         lambda *refs: second_solve_kernel(total_i, *refs),
-        [(32, 8, LANES), (RANK, LANES)],
+        [(160, LANES), (RANK, LANES)],
         u,
         gram_a,
         gram_c,
     )
-    ss = exchange(ss, ("ia", "ja"))
+    ss = exchange(ss.reshape(32, 1, 5 * LANES), ("ia", "ja")).reshape(160, LANES)
     out_a, out_b = call(
         lambda *refs: finish_kernel(total_j, *refs), [(4, 64), (8, 64)], ss, a, scale_a
     )

time: 88.5 us -> 87.7 us (level)
  no operation moved by 1% of the time
where the time goes in v6:
time: 87.7 us; the launch traced here: 87.4 us
  blocking collectives  60.2 us (69%)
  starting transfers between devices  14.1 us (16%)
  Pallas kernels  7.1 us (8%)
  waiting for transfers between devices  5.33 us (6%)
    all_to_all x4, blocking collectives, exchange(): return lax.all_to_all(x, axes, 0, 0, tiled=True, axis_index_groups=groups)  60.2 us
    ppermute x6, starting transfers between devices, turned(): return lax.ppermute(x, axis, [(n, (n + step) % size) for n in range(size)])  8.18 us
    pallas_call x10, Pallas kernels, call(): pl.pallas_call(kernel, out_shape=[jax.ShapeDtypeStruct(s, F32) for s in o...  7.1 us
    ppermute x2, starting transfers between devices, other_core(): return lax.ppermute(x, 'ja', [(n, n ^ 1) for n in range(8)])  5.91 us
    ppermute x6, waiting for transfers between devices, turned(): return lax.ppermute(x, axis, [(n, (n + step) % size) for n in range(size)])  4.82 us
  transfers between devices with their start and end apart: 8, of which 6 were waited for; matrix products, arithmetic and copies ran while one was open for 0% of the time, Pallas kernels for 2%

profile of v6, /device:TPU:1, one launch (start us, length us, event | category | flops | bytes accessed | tf_op | source)
XLA Modules:
  0.0 87.4 jit_solution(15930090417056219120)
XLA Ops:
  0.6 0.9 %shard_map.50 = f32[160,128]{1,0:T(8,128)S(1)} custom-call(f32[8,64]{1,0:T(8,128)} %b_hbm.1, f32[1,8]{1,0:T(1,128)} %c_hbm.1), custom_call_target="tpu_custom_call" | custom-call | flops 10000000000 | tf_op jit(solution)/shard_map/pallas_call | solution.py:261
  1.6 20.7 %all_to_all.20 = f32[32,1,640]{2,1,0:T(1,128)S(1)} all-to-all(f32[32,1,640]{2,1,0:T(1,128)S(1)} %bitcast.16), channel_id=1, replica_groups=mesh['ia'=4,'ja'=8,'ka'=8] {'ia','ka'}, dimensions={0} | all-to-all | bytes 163840 | tf_op jit(solution)/shard_map/all_to_all | solution.py:273
  22.3 0.8 shard_map.51
  23.2 2.2 %collective-permute-start = (f32[4,160,128]{2,1,0:T(8,128)S(1)}, f32[4,160,128]{2,1,0:T(8,128)S(1)}, u32[]{:S(2)}, u32[]{:S(2)}) collective-permute-start(f32[4,160,128]{2,1,0:T(8,128)S(1)} %get-tuple-element.20), channel_id=1, source_target_pairs={{0,8},{8,0},{16,24},{24,16},{32,40},{40,32},{48,56},{56,48},{1,9},... | collective-permute-start | bytes 983048 | tf_op jit(solution)/shard_map/ppermute | solution.py:277
  25.4 0.8 shard_map.52
  26.1 0.5 collective-permute-done
  26.6 1.4 %collective-permute-start.1 = (f32[160,128]{1,0:T(8,128)S(1)}, f32[160,128]{1,0:T(8,128)S(1)}, u32[]{:S(2)}, u32[]{:S(2)}) collective-permute-start(f32[160,128]{1,0:T(8,128)S(1)} %get-tuple-element.38), channel_id=1, source_target_pairs={{0,16},{8,24},{16,32},{24,40},{32,48},{40,56},{48,0},{56,8},{1,17}... | collective-permute-start | bytes 245768 | tf_op jit(solution)/shard_map/ppermute | solution.py:282
  28.0 2.6 %collective-permute-start.2 = (f32[160,128]{1,0:T(8,128)S(1)}, f32[160,128]{1,0:T(8,128)S(1)}, u32[]{:S(2)}, u32[]{:S(2)}) collective-permute-start(f32[160,128]{1,0:T(8,128)S(1)} %get-tuple-element.37), channel_id=1, source_target_pairs={{0,32},{8,40},{16,48},{24,56},{32,0},{40,8},{48,16},{56,24},{1,33}... | collective-permute-start | bytes 245768 | tf_op jit(solution)/shard_map/ppermute | solution.py:282
  30.6 1.1 %collective-permute-start.3 = (f32[160,128]{1,0:T(8,128)S(1)}, f32[160,128]{1,0:T(8,128)S(1)}, u32[]{:S(2)}, u32[]{:S(2)}) collective-permute-start(f32[160,128]{1,0:T(8,128)S(1)} %get-tuple-element.36), channel_id=1, source_target_pairs={{0,48},{8,56},{16,0},{24,8},{32,16},{40,24},{48,32},{56,40},{1,49}... | collective-permute-start | bytes 245768 | tf_op jit(solution)/shard_map/ppermute | solution.py:282
  31.7 2.9 %collective-permute-done.2.z2_ref = f32[160,128]{1,0:T(8,128)S(1)} collective-permute-done((f32[160,128]{1,0:T(8,128)S(1)}, f32[160,128]{1,0:T(8,128)S(1)}, u32[]{:S(2)}, u32[]{:S(2)}) %collective-permute-start.2) | collective-permute-done | bytes 81952 | tf_op jit(solution)/shard_map/ppermute | solution.py:282
  35.0 13.6 %all_to_all.21.v_ref = f32[32,16,128]{2,1,0:T(8,128)S(1)} all-to-all(f32[32,16,128]{2,1,0:T(8,128)S(1)} %get-tuple-element.21), channel_id=1, replica_groups={{0,1,2,3,4,5,6,7,16,17,18,19,20,21,22,23,32,33,34,35,36,37,38,39,48,49,..., dimensions={0} | all-to-all | bytes 524288 | tf_op jit(solution)/shard_map/all_to_all | solution.py:273
  48.7 3.7 %collective-permute-start.4 = (f32[32,256]{1,0:T(8,128)S(1)}, f32[32,256]{1,0:T(8,128)S(1)}, u32[]{:S(2)}, u32[]{:S(2)}) collective-permute-start(f32[32,256]{1,0:T(8,128)S(1)} %shard_map.54.mine_ref), channel_id=1, source_target_pairs={{0,8},{8,0},{16,24},{24,16},{32,40},{40,32},{48,56},{56,48},{1,9},... | collective-permute-start | bytes 98312 | tf_op jit(solution)/shard_map/ppermute | solution.py:277
  52.4 0.8 shard_map.55
  53.3 1.4 %shard_map.56 = (f32[40,128]{1,0:T(8,128)S(1)}, f32[40,128]{1,0:T(8,128)S(1)}, f32[40,128]{1,0:T(8,128)S(1)}, f32[40,128]{1,0:T(8,128)S(1)}, f32[32,128]{1,0:T(8,128)S(1)}) custom-call(f32[32,256]{1,0:T(8,128)S(1)} %shard_map.54.mine_ref, f32[32,256]{1,0:T(8,128)S(1)} %collective-permute-done.4.other_ref, f32[32,32]{1,0:T(8,128)S(1)} %get-tuple-element.24.inv_ref, ...), custom_call_target="tpu_custom_call" | custom-call | tf_op jit(solution)/shard_map/pallas_call | solution.py:261
  54.7 0.4 collective-permute-start.5
  55.1 1.7 %collective-permute-start.6 = (f32[40,128]{1,0:T(8,128)S(1)}, f32[40,128]{1,0:T(8,128)S(1)}, u32[]{:S(2)}, u32[]{:S(2)}) collective-permute-start(f32[40,128]{1,0:T(8,128)S(1)} %get-tuple-element.28), channel_id=1, source_target_pairs={{0,128},{64,192},{128,0},{192,64},{1,129},{65,193},{129,1},{193,65... | collective-permute-start | bytes 61448 | tf_op jit(solution)/shard_map/ppermute | solution.py:282
  56.8 1.0 %collective-permute-start.7 = (f32[40,128]{1,0:T(8,128)S(1)}, f32[40,128]{1,0:T(8,128)S(1)}, u32[]{:S(2)}, u32[]{:S(2)}) collective-permute-start(f32[40,128]{1,0:T(8,128)S(1)} %get-tuple-element.29), channel_id=1, source_target_pairs={{0,192},{64,0},{128,64},{192,128},{1,193},{65,1},{129,65},{193,129... | collective-permute-start | bytes 61448 | tf_op jit(solution)/shard_map/ppermute | solution.py:282
  57.8 0.8 collective-permute-done.5.p1_ref
  58.6 0.6 collective-permute-done.6.p2_ref
  59.2 0.5 collective-permute-done.7.p3_ref
  59.7 10.9 %all_to_all.22.refs_0_ = f32[8,32,128]{2,1,0:T(8,128)S(1)} all-to-all(f32[8,32,128]{2,1,0:T(8,128)S(1)} %get-tuple-element.30), channel_id=1, replica_groups=mesh['ia'=4,'ja'=8,'ka'=8] {'ka'}, dimensions={0} | all-to-all | bytes 262144 | tf_op jit(solution)/shard_map/all_to_all | solution.py:273
  70.6 1.1 %shard_map.58 = (f32[160,128]{1,0:T(8,128)S(1)}, f32[32,128]{1,0:T(8,128)S(1)}) custom-call(f32[8,32,128]{2,1,0:T(8,128)S(1)} %all_to_all.22.refs_0_, f32[8,128]{1,0:T(8,128)S(1)} %get-tuple-element.31.refs_1_, f32[32,32]{1,0:T(8,128)S(1)} %get-tuple-element.32.refs_2_), custom_call_target="tpu_custom_call" | custom-call | tf_op jit(solution)/shard_map/pallas_call | solution.py:261
  71.8 15.0 %all_to_all.23 = f32[32,1,640]{2,1,0:T(1,128)S(1)} all-to-all(f32[32,1,640]{2,1,0:T(1,128)S(1)} %bitcast.15), channel_id=1, replica_groups=mesh['ia'=4,'ja'=8,'ka'=8] {'ia','ja'}, dimensions={0} | all-to-all | bytes 163840 | tf_op jit(solution)/shard_map/all_to_all | solution.py:273
  86.7 0.7 shard_map.59
  (9 shorter events, 0.6 us)
Async XLA Ops:
  0.6 21.7 %copy-start = (bf16[8,512,512]{2,1,0:T(8,128)(2,1)S(1)}, bf16[8,512,512]{2,1,0:T(8,128)(2,1)}, u32[]{:S(2)}) copy-start(bf16[8,512,512]{2,1,0:T(8,128)(2,1)} %t_ref.1) | copy-start | bytes 12582916
  23.2 3.4 %collective-permute-start = (f32[4,160,128]{2,1,0:T(8,128)S(1)}, f32[4,160,128]{2,1,0:T(8,128)S(1)}, u32[]{:S(2)}, u32[]{:S(2)}) collective-permute-start(f32[4,160,128]{2,1,0:T(8,128)S(1)} %get-tuple-element.20), channel_id=1, source_target_pairs={{0,8},{8,0},{16,24},{24,16},{32,40},{40,32},{48,56},{56,48},{1,9},... | collective-permute-start | bytes 983048 | tf_op jit(solution)/shard_map/ppermute | solution.py:277
  26.6 5.1 %collective-permute-start.1 = (f32[160,128]{1,0:T(8,128)S(1)}, f32[160,128]{1,0:T(8,128)S(1)}, u32[]{:S(2)}, u32[]{:S(2)}) collective-permute-start(f32[160,128]{1,0:T(8,128)S(1)} %get-tuple-element.38), channel_id=1, source_target_pairs={{0,16},{8,24},{16,32},{24,40},{32,48},{40,56},{48,0},{56,8},{1,17}... | collective-permute-start | bytes 245768 | tf_op jit(solution)/shard_map/ppermute | solution.py:282
  28.0 6.6 %collective-permute-start.2 = (f32[160,128]{1,0:T(8,128)S(1)}, f32[160,128]{1,0:T(8,128)S(1)}, u32[]{:S(2)}, u32[]{:S(2)}) collective-permute-start(f32[160,128]{1,0:T(8,128)S(1)} %get-tuple-element.37), channel_id=1, source_target_pairs={{0,32},{8,40},{16,48},{24,56},{32,0},{40,8},{48,16},{56,24},{1,33}... | collective-permute-start | bytes 245768 | tf_op jit(solution)/shard_map/ppermute | solution.py:282
  30.6 3.9 %collective-permute-start.3 = (f32[160,128]{1,0:T(8,128)S(1)}, f32[160,128]{1,0:T(8,128)S(1)}, u32[]{:S(2)}, u32[]{:S(2)}) collective-permute-start(f32[160,128]{1,0:T(8,128)S(1)} %get-tuple-element.36), channel_id=1, source_target_pairs={{0,48},{8,56},{16,0},{24,8},{32,16},{40,24},{48,32},{56,40},{1,49}... | collective-permute-start | bytes 245768 | tf_op jit(solution)/shard_map/ppermute | solution.py:282
  48.7 4.6 %collective-permute-start.4 = (f32[32,256]{1,0:T(8,128)S(1)}, f32[32,256]{1,0:T(8,128)S(1)}, u32[]{:S(2)}, u32[]{:S(2)}) collective-permute-start(f32[32,256]{1,0:T(8,128)S(1)} %shard_map.54.mine_ref), channel_id=1, source_target_pairs={{0,8},{8,0},{16,24},{24,16},{32,40},{40,32},{48,56},{56,48},{1,9},... | collective-permute-start | bytes 98312 | tf_op jit(solution)/shard_map/ppermute | solution.py:277
  54.7 3.9 %collective-permute-start.5 = (f32[40,128]{1,0:T(8,128)S(1)}, f32[40,128]{1,0:T(8,128)S(1)}, u32[]{:S(2)}, u32[]{:S(2)}) collective-permute-start(f32[40,128]{1,0:T(8,128)S(1)} %get-tuple-element.27), channel_id=1, source_target_pairs={{0,64},{64,128},{128,192},{192,0},{1,65},{65,129},{129,193},{193,1... | collective-permute-start | bytes 61448 | tf_op jit(solution)/shard_map/ppermute | solution.py:282
  55.1 4.1 %collective-permute-start.6 = (f32[40,128]{1,0:T(8,128)S(1)}, f32[40,128]{1,0:T(8,128)S(1)}, u32[]{:S(2)}, u32[]{:S(2)}) collective-permute-start(f32[40,128]{1,0:T(8,128)S(1)} %get-tuple-element.28), channel_id=1, source_target_pairs={{0,128},{64,192},{128,0},{192,64},{1,129},{65,193},{129,1},{193,65... | collective-permute-start | bytes 61448 | tf_op jit(solution)/shard_map/ppermute | solution.py:282
  56.8 2.9 %collective-permute-start.7 = (f32[40,128]{1,0:T(8,128)S(1)}, f32[40,128]{1,0:T(8,128)S(1)}, u32[]{:S(2)}, u32[]{:S(2)}) collective-permute-start(f32[40,128]{1,0:T(8,128)S(1)} %get-tuple-element.29), channel_id=1, source_target_pairs={{0,192},{64,0},{128,64},{192,128},{1,193},{65,1},{129,65},{193,129... | collective-permute-start | bytes 61448 | tf_op jit(solution)/shard_map/ppermute | solution.py:282

commit v7 on v6

--- a/solution.py
+++ b/solution.py
@@ -105,13 +105,14 @@
         b_rows.append(jnp.concatenate(pairs, axis=1))
     b = jnp.concatenate(b_rows, axis=0)
     if other:
-        extra = dot_nt(b, jnp.concatenate([b, jnp.zeros((96, 512), F32)], axis=0))
-        row, lane = iota((RANK, LANES), 0), iota((RANK, LANES), 1)
+        extra_ref[:8] = folded_gram(b)
+        row = iota((8, LANES), 0)
+        c_rows = jnp.zeros((8, LANES), F32)
         for ia in range(4):
             starts = [5 * (8 * ia + ka) + 4 for ka in range(8)]
             c_row = sum(y_ref[start : start + 1] for start in starts)
-            extra = jnp.where((lane >= 64) & (row == 8 * ia + ja), c_row, extra)
-        extra_ref[...] = extra
+            c_rows = jnp.where(row == 4 * (ja % 2) + ia, c_row, c_rows)
+        extra_ref[8:] = c_rows
     extra = extra_ref[...]
     high, low = split(b)
 
@@ -137,14 +138,18 @@
         for n in range(4):
             out_ref[n, 64 * h : 64 * h + 64, :] = y[64 * n : 64 * n + 64]
     for n in range(4):
-        out_ref[n, 128:160, :] = extra
-
-
-def combine_kernel(z0_ref, z1_ref, z2_ref, z3_ref, u_ref, gram_ref, c_all_ref, c_ref):
-    ka = lax.axis_index("ka")
+        out_ref[n, 128:144, :] = extra
+
+
+def combine_kernel(z0_ref, z1_ref, z2_ref, z3_ref, u_ref, gram_ref, c_all_ref, c_ref, scratch):
+    ka, y = lax.axis_index("ka"), lax.axis_index("ja") // 2
+    for n, ref in enumerate((z0_ref, z1_ref, z2_ref, z3_ref)):
+        for core in range(2):
+            place = pl.ds(2 * ((y + 4 - n) % 4) + core, 4, stride=8)
+            scratch[place, :] = ref[136 + 4 * core : 140 + 4 * core]
+    extra = scratch[...]
     z = (z0_ref[...] + z1_ref[...]) + (z2_ref[...] + z3_ref[...])
-    extra = z[128:160]
-    gram_ref[...] = extra[:, :32]
+    gram_ref[...] = unfold(z[128:136])
     c_all_ref[...] = pltpu.roll(extra, 64, 1)[:, :64]
     c_here = pltpu.roll(extra, 64 - 8 * ka, 1)
     c_ref[...] = c_here
@@ -302,9 +307,9 @@
         space=HBM,
     )
     y = exchange(y.reshape(32, 1, 5 * LANES), ("ia", "ka")).reshape(160, LANES)
-    half = (4, 160, LANES)
+    half = (4, 144, LANES)
     send, extra = call(
-        lambda *refs: first_kernel(True, *refs), [half, (RANK, LANES)], y, tensor
+        lambda *refs: first_kernel(True, *refs), [half, (16, LANES)], y, tensor
     )
     received = other_core(send)
     (keep,) = call(lambda *refs: first_kernel(False, *refs), [half], y, tensor, extra)
@@ -312,7 +317,11 @@
     z = [z[0]] + [turned(z[n], "ja", 2 * n) for n in range(1, 4)]
     same_core = [[8 * ja + ka for ja in range(core, 8, 2) for ka in range(8)] for core in range(2)]
     u, gram_b, c_all, c_here = call(
-        combine_kernel, [(32, 16, LANES), (RANK, RANK), (RANK, 64), (RANK, LANES)], *z, cost=LONG
+        combine_kernel,
+        [(32, 16, LANES), (RANK, RANK), (RANK, 64), (RANK, LANES)],
+        *z,
+        scratch=[pltpu.VMEM((RANK, LANES), F32)],
+        cost=LONG,
     )
     v = exchange(u, ("ja", "ka"), same_core)
     (m,) = call(turn_kernel, [(RANK, 256)], v)

time: 87.7 us -> 87.4 us (level)
  transfers between devices with their start and end apart: 8 -> 8, of which waited for: 6 -> 7; matrix products, arithmetic and copies ran while one was open for 0% -> 0% of each run, Pallas kernels for 2% -> 2%
where the time goes in v7:
time: 87.4 us; the launch traced here: 87.2 us
  blocking collectives  59.9 us (69%)
  starting transfers between devices  14.4 us (16%)
  Pallas kernels  7.27 us (8%)
  waiting for transfers between devices  4.83 us (6%)
    all_to_all x4, blocking collectives, exchange(): return lax.all_to_all(x, axes, 0, 0, tiled=True, axis_index_groups=groups)  59.9 us
    ppermute x6, starting transfers between devices, turned(): return lax.ppermute(x, axis, [(n, (n + step) % size) for n in range(size)])  8.18 us
    pallas_call x10, Pallas kernels, call(): pl.pallas_call(kernel, out_shape=[jax.ShapeDtypeStruct(s, F32) for s in o...  7.27 us
    ppermute x2, starting transfers between devices, other_core(): return lax.ppermute(x, 'ja', [(n, n ^ 1) for n in range(8)])  6.25 us
    ppermute x6, waiting for transfers between devices, turned(): return lax.ppermute(x, axis, [(n, (n + step) % size) for n in range(size)])  4.37 us
  transfers between devices with their start and end apart: 8, of which 7 were waited for; matrix products, arithmetic and copies ran while one was open for 0% of the time, Pallas kernels for 2%

profile of v7, /device:TPU:1, one launch (start us, length us, event | category | flops | bytes accessed | tf_op | source)
XLA Modules:
  0.0 87.2 jit_solution(8968575530202766808)
XLA Ops:
  0.6 0.9 %shard_map.50 = f32[160,128]{1,0:T(8,128)S(1)} custom-call(f32[8,64]{1,0:T(8,128)} %b_hbm.1, f32[1,8]{1,0:T(1,128)} %c_hbm.1), custom_call_target="tpu_custom_call" | custom-call | flops 10000000000 | tf_op jit(solution)/shard_map/pallas_call | solution.py:266
  1.6 20.7 %all_to_all.20 = f32[32,1,640]{2,1,0:T(1,128)S(1)} all-to-all(f32[32,1,640]{2,1,0:T(1,128)S(1)} %bitcast.16), channel_id=1, replica_groups=mesh['ia'=4,'ja'=8,'ka'=8] {'ia','ka'}, dimensions={0} | all-to-all | bytes 163840 | tf_op jit(solution)/shard_map/all_to_all | solution.py:278
  22.3 1.0 %shard_map.51 = (f32[4,144,128]{2,1,0:T(8,128)S(1)}, f32[16,128]{1,0:T(8,128)S(1)}) custom-call(f32[160,128]{1,0:T(8,128)S(1)} %bitcast.12, bf16[8,512,512]{2,1,0:T(8,128)(2,1)S(1)} %copy-done), custom_call_target="tpu_custom_call" | custom-call | tf_op jit(solution)/shard_map/pallas_call | solution.py:266
  23.3 2.2 %collective-permute-start = (f32[4,144,128]{2,1,0:T(8,128)S(1)}, f32[4,144,128]{2,1,0:T(8,128)S(1)}, u32[]{:S(2)}, u32[]{:S(2)}) collective-permute-start(f32[4,144,128]{2,1,0:T(8,128)S(1)} %get-tuple-element.20), channel_id=1, source_target_pairs={{0,8},{8,0},{16,24},{24,16},{32,40},{40,32},{48,56},{56,48},{1,9},... | collective-permute-start | bytes 884744 | tf_op jit(solution)/shard_map/ppermute | solution.py:282
  25.5 0.8 shard_map.52
  26.3 0.4 collective-permute-done
  26.8 1.4 %collective-permute-start.1 = (f32[144,128]{1,0:T(8,128)S(1)}, f32[144,128]{1,0:T(8,128)S(1)}, u32[]{:S(2)}, u32[]{:S(2)}) collective-permute-start(f32[144,128]{1,0:T(8,128)S(1)} %get-tuple-element.38), channel_id=1, source_target_pairs={{0,16},{8,24},{16,32},{24,40},{32,48},{40,56},{48,0},{56,8},{1,17}... | collective-permute-start | bytes 221192 | tf_op jit(solution)/shard_map/ppermute | solution.py:287
  28.1 2.6 %collective-permute-start.2 = (f32[144,128]{1,0:T(8,128)S(1)}, f32[144,128]{1,0:T(8,128)S(1)}, u32[]{:S(2)}, u32[]{:S(2)}) collective-permute-start(f32[144,128]{1,0:T(8,128)S(1)} %get-tuple-element.37), channel_id=1, source_target_pairs={{0,32},{8,40},{16,48},{24,56},{32,0},{40,8},{48,16},{56,24},{1,33}... | collective-permute-start | bytes 221192 | tf_op jit(solution)/shard_map/ppermute | solution.py:287
  30.8 1.1 %collective-permute-start.3 = (f32[144,128]{1,0:T(8,128)S(1)}, f32[144,128]{1,0:T(8,128)S(1)}, u32[]{:S(2)}, u32[]{:S(2)}) collective-permute-start(f32[144,128]{1,0:T(8,128)S(1)} %get-tuple-element.36), channel_id=1, source_target_pairs={{0,48},{8,56},{16,0},{24,8},{32,16},{40,24},{48,32},{56,40},{1,49}... | collective-permute-start | bytes 221192 | tf_op jit(solution)/shard_map/ppermute | solution.py:287
  31.8 2.2 %collective-permute-done.2.z2_ref = f32[144,128]{1,0:T(8,128)S(1)} collective-permute-done((f32[144,128]{1,0:T(8,128)S(1)}, f32[144,128]{1,0:T(8,128)S(1)}, u32[]{:S(2)}, u32[]{:S(2)}) %collective-permute-start.2) | collective-permute-done | bytes 73760 | tf_op jit(solution)/shard_map/ppermute | solution.py:287
  34.7 13.7 %all_to_all.21.v_ref = f32[32,16,128]{2,1,0:T(8,128)S(1)} all-to-all(f32[32,16,128]{2,1,0:T(8,128)S(1)} %get-tuple-element.21), channel_id=1, replica_groups={{0,1,2,3,4,5,6,7,16,17,18,19,20,21,22,23,32,33,34,35,36,37,38,39,48,49,..., dimensions={0} | all-to-all | bytes 524288 | tf_op jit(solution)/shard_map/all_to_all | solution.py:278
  48.5 4.1 %collective-permute-start.4 = (f32[32,256]{1,0:T(8,128)S(1)}, f32[32,256]{1,0:T(8,128)S(1)}, u32[]{:S(2)}, u32[]{:S(2)}) collective-permute-start(f32[32,256]{1,0:T(8,128)S(1)} %shard_map.54.mine_ref), channel_id=1, source_target_pairs={{0,8},{8,0},{16,24},{24,16},{32,40},{40,32},{48,56},{56,48},{1,9},... | collective-permute-start | bytes 98312 | tf_op jit(solution)/shard_map/ppermute | solution.py:282
  52.6 0.8 shard_map.55
  53.4 1.4 %shard_map.56 = (f32[40,128]{1,0:T(8,128)S(1)}, f32[40,128]{1,0:T(8,128)S(1)}, f32[40,128]{1,0:T(8,128)S(1)}, f32[40,128]{1,0:T(8,128)S(1)}, f32[32,128]{1,0:T(8,128)S(1)}) custom-call(f32[32,256]{1,0:T(8,128)S(1)} %shard_map.54.mine_ref, f32[32,256]{1,0:T(8,128)S(1)} %collective-permute-done.4.other_ref, f32[32,32]{1,0:T(8,128)S(1)} %get-tuple-element.24.inv_ref, ...), custom_call_target="tpu_custom_call" | custom-call | tf_op jit(solution)/shard_map/pallas_call | solution.py:266
  54.8 0.4 collective-permute-start.5
  55.2 1.7 %collective-permute-start.6 = (f32[40,128]{1,0:T(8,128)S(1)}, f32[40,128]{1,0:T(8,128)S(1)}, u32[]{:S(2)}, u32[]{:S(2)}) collective-permute-start(f32[40,128]{1,0:T(8,128)S(1)} %get-tuple-element.28), channel_id=1, source_target_pairs={{0,128},{64,192},{128,0},{192,64},{1,129},{65,193},{129,1},{193,65... | collective-permute-start | bytes 61448 | tf_op jit(solution)/shard_map/ppermute | solution.py:287
  56.9 1.0 %collective-permute-start.7 = (f32[40,128]{1,0:T(8,128)S(1)}, f32[40,128]{1,0:T(8,128)S(1)}, u32[]{:S(2)}, u32[]{:S(2)}) collective-permute-start(f32[40,128]{1,0:T(8,128)S(1)} %get-tuple-element.29), channel_id=1, source_target_pairs={{0,192},{64,0},{128,64},{192,128},{1,193},{65,1},{129,65},{193,129... | collective-permute-start | bytes 61448 | tf_op jit(solution)/shard_map/ppermute | solution.py:287
  57.9 0.8 collective-permute-done.5.p1_ref
  58.7 0.6 collective-permute-done.6.p2_ref
  59.3 0.5 collective-permute-done.7.p3_ref
  59.9 10.5 %all_to_all.22.refs_0_ = f32[8,32,128]{2,1,0:T(8,128)S(1)} all-to-all(f32[8,32,128]{2,1,0:T(8,128)S(1)} %get-tuple-element.30), channel_id=1, replica_groups=mesh['ia'=4,'ja'=8,'ka'=8] {'ka'}, dimensions={0} | all-to-all | bytes 262144 | tf_op jit(solution)/shard_map/all_to_all | solution.py:278
  70.4 1.1 %shard_map.58 = (f32[160,128]{1,0:T(8,128)S(1)}, f32[32,128]{1,0:T(8,128)S(1)}) custom-call(f32[8,32,128]{2,1,0:T(8,128)S(1)} %all_to_all.22.refs_0_, f32[8,128]{1,0:T(8,128)S(1)} %get-tuple-element.31.refs_1_, f32[32,32]{1,0:T(8,128)S(1)} %get-tuple-element.32.refs_2_), custom_call_target="tpu_custom_call" | custom-call | tf_op jit(solution)/shard_map/pallas_call | solution.py:266
  71.5 15.0 %all_to_all.23 = f32[32,1,640]{2,1,0:T(1,128)S(1)} all-to-all(f32[32,1,640]{2,1,0:T(1,128)S(1)} %bitcast.15), channel_id=1, replica_groups=mesh['ia'=4,'ja'=8,'ka'=8] {'ia','ja'}, dimensions={0} | all-to-all | bytes 163840 | tf_op jit(solution)/shard_map/all_to_all | solution.py:278
  86.5 0.7 shard_map.59
  (9 shorter events, 0.9 us)
Async XLA Ops:
  0.6 21.7 %copy-start = (bf16[8,512,512]{2,1,0:T(8,128)(2,1)S(1)}, bf16[8,512,512]{2,1,0:T(8,128)(2,1)}, u32[]{:S(2)}) copy-start(bf16[8,512,512]{2,1,0:T(8,128)(2,1)} %t_ref.1) | copy-start | bytes 12582916
  23.3 3.4 %collective-permute-start = (f32[4,144,128]{2,1,0:T(8,128)S(1)}, f32[4,144,128]{2,1,0:T(8,128)S(1)}, u32[]{:S(2)}, u32[]{:S(2)}) collective-permute-start(f32[4,144,128]{2,1,0:T(8,128)S(1)} %get-tuple-element.20), channel_id=1, source_target_pairs={{0,8},{8,0},{16,24},{24,16},{32,40},{40,32},{48,56},{56,48},{1,9},... | collective-permute-start | bytes 884744 | tf_op jit(solution)/shard_map/ppermute | solution.py:282
  26.8 5.1 %collective-permute-start.1 = (f32[144,128]{1,0:T(8,128)S(1)}, f32[144,128]{1,0:T(8,128)S(1)}, u32[]{:S(2)}, u32[]{:S(2)}) collective-permute-start(f32[144,128]{1,0:T(8,128)S(1)} %get-tuple-element.38), channel_id=1, source_target_pairs={{0,16},{8,24},{16,32},{24,40},{32,48},{40,56},{48,0},{56,8},{1,17}... | collective-permute-start | bytes 221192 | tf_op jit(solution)/shard_map/ppermute | solution.py:287
  28.1 5.9 %collective-permute-start.2 = (f32[144,128]{1,0:T(8,128)S(1)}, f32[144,128]{1,0:T(8,128)S(1)}, u32[]{:S(2)}, u32[]{:S(2)}) collective-permute-start(f32[144,128]{1,0:T(8,128)S(1)} %get-tuple-element.37), channel_id=1, source_target_pairs={{0,32},{8,40},{16,48},{24,56},{32,0},{40,8},{48,16},{56,24},{1,33}... | collective-permute-start | bytes 221192 | tf_op jit(solution)/shard_map/ppermute | solution.py:287
  30.8 3.5 %collective-permute-start.3 = (f32[144,128]{1,0:T(8,128)S(1)}, f32[144,128]{1,0:T(8,128)S(1)}, u32[]{:S(2)}, u32[]{:S(2)}) collective-permute-start(f32[144,128]{1,0:T(8,128)S(1)} %get-tuple-element.36), channel_id=1, source_target_pairs={{0,48},{8,56},{16,0},{24,8},{32,16},{40,24},{48,32},{56,40},{1,49}... | collective-permute-start | bytes 221192 | tf_op jit(solution)/shard_map/ppermute | solution.py:287
  48.5 4.9 %collective-permute-start.4 = (f32[32,256]{1,0:T(8,128)S(1)}, f32[32,256]{1,0:T(8,128)S(1)}, u32[]{:S(2)}, u32[]{:S(2)}) collective-permute-start(f32[32,256]{1,0:T(8,128)S(1)} %shard_map.54.mine_ref), channel_id=1, source_target_pairs={{0,8},{8,0},{16,24},{24,16},{32,40},{40,32},{48,56},{56,48},{1,9},... | collective-permute-start | bytes 98312 | tf_op jit(solution)/shard_map/ppermute | solution.py:282
  54.8 3.9 %collective-permute-start.5 = (f32[40,128]{1,0:T(8,128)S(1)}, f32[40,128]{1,0:T(8,128)S(1)}, u32[]{:S(2)}, u32[]{:S(2)}) collective-permute-start(f32[40,128]{1,0:T(8,128)S(1)} %get-tuple-element.27), channel_id=1, source_target_pairs={{0,64},{64,128},{128,192},{192,0},{1,65},{65,129},{129,193},{193,1... | collective-permute-start | bytes 61448 | tf_op jit(solution)/shard_map/ppermute | solution.py:287
  55.2 4.1 %collective-permute-start.6 = (f32[40,128]{1,0:T(8,128)S(1)}, f32[40,128]{1,0:T(8,128)S(1)}, u32[]{:S(2)}, u32[]{:S(2)}) collective-permute-start(f32[40,128]{1,0:T(8,128)S(1)} %get-tuple-element.28), channel_id=1, source_target_pairs={{0,128},{64,192},{128,0},{192,64},{1,129},{65,193},{129,1},{193,65... | collective-permute-start | bytes 61448 | tf_op jit(solution)/shard_map/ppermute | solution.py:287
  56.9 2.9 %collective-permute-start.7 = (f32[40,128]{1,0:T(8,128)S(1)}, f32[40,128]{1,0:T(8,128)S(1)}, u32[]{:S(2)}, u32[]{:S(2)}) collective-permute-start(f32[40,128]{1,0:T(8,128)S(1)} %get-tuple-element.29), channel_id=1, source_target_pairs={{0,192},{64,0},{128,64},{192,128},{1,193},{65,1},{129,65},{193,129... | collective-permute-start | bytes 61448 | tf_op jit(solution)/shard_map/ppermute | solution.py:287

commit v8 on v7

--- a/solution.py
+++ b/solution.py
@@ -51,7 +51,8 @@
 
 
 def folded_gram(x):
-    return fold(dot_nt(x, jnp.concatenate([x] * 4, axis=0)))
+    gram = dot_nt(x, x)
+    return jnp.concatenate([gram[8 * q : 8 * q + 8] for q in range(4)], axis=1)
 
 
 def inverse(a):
@@ -321,10 +322,9 @@
         [(32, 16, LANES), (RANK, RANK), (RANK, 64), (RANK, LANES)],
         *z,
         scratch=[pltpu.VMEM((RANK, LANES), F32)],
-        cost=LONG,
     )
     v = exchange(u, ("ja", "ka"), same_core)
-    (m,) = call(turn_kernel, [(RANK, 256)], v)
+    (m,) = call(turn_kernel, [(RANK, 256)], v, cost=LONG)
     inv_a, gram_c = call(invert_a_kernel, [(RANK, RANK), (RANK, RANK)], gram_b, c_all)
     *p, a = call(
         second_kernel,

time: 87.4 us -> 87.1 us (level)
  no operation moved by 1% of the time
where the time goes in v8:
time: 87.1 us; the launch traced here: 86.9 us
  blocking collectives  59.9 us (69%)
  starting transfers between devices  14.4 us (17%)
  Pallas kernels  6.92 us (8%)
  waiting for transfers between devices  4.83 us (6%)
    all_to_all x4, blocking collectives, exchange(): return lax.all_to_all(x, axes, 0, 0, tiled=True, axis_index_groups=groups)  59.9 us
    ppermute x6, starting transfers between devices, turned(): return lax.ppermute(x, axis, [(n, (n + step) % size) for n in range(size)])  8.18 us
    pallas_call x10, Pallas kernels, call(): pl.pallas_call(kernel, out_shape=[jax.ShapeDtypeStruct(s, F32) for s in o...  6.92 us
    ppermute x2, starting transfers between devices, other_core(): return lax.ppermute(x, 'ja', [(n, n ^ 1) for n in range(8)])  6.24 us
    ppermute x6, waiting for transfers between devices, turned(): return lax.ppermute(x, axis, [(n, (n + step) % size) for n in range(size)])  4.37 us
  transfers between devices with their start and end apart: 8, of which 7 were waited for; matrix products, arithmetic and copies ran while one was open for 0% of the time, Pallas kernels for 2%

profile of v8, /device:TPU:1, one launch (start us, length us, event | category | flops | bytes accessed | tf_op | source)
XLA Modules:
  0.0 86.9 jit_solution(12759038924662679228)
XLA Ops:
  0.6 0.9 %shard_map.50 = f32[160,128]{1,0:T(8,128)S(1)} custom-call(f32[8,64]{1,0:T(8,128)} %b_hbm.1, f32[1,8]{1,0:T(1,128)} %c_hbm.1), custom_call_target="tpu_custom_call" | custom-call | flops 10000000000 | tf_op jit(solution)/shard_map/pallas_call | solution.py:267
  1.6 20.7 %all_to_all.20 = f32[32,1,640]{2,1,0:T(1,128)S(1)} all-to-all(f32[32,1,640]{2,1,0:T(1,128)S(1)} %bitcast.16), channel_id=1, replica_groups=mesh['ia'=4,'ja'=8,'ka'=8] {'ia','ka'}, dimensions={0} | all-to-all | bytes 163840 | tf_op jit(solution)/shard_map/all_to_all | solution.py:279
  22.3 0.8 shard_map.51
  23.2 2.2 %collective-permute-start = (f32[4,144,128]{2,1,0:T(8,128)S(1)}, f32[4,144,128]{2,1,0:T(8,128)S(1)}, u32[]{:S(2)}, u32[]{:S(2)}) collective-permute-start(f32[4,144,128]{2,1,0:T(8,128)S(1)} %get-tuple-element.20), channel_id=1, source_target_pairs={{0,8},{8,0},{16,24},{24,16},{32,40},{40,32},{48,56},{56,48},{1,9},... | collective-permute-start | bytes 884744 | tf_op jit(solution)/shard_map/ppermute | solution.py:283
  25.4 0.8 shard_map.52
  26.1 0.4 collective-permute-done
  26.6 1.4 %collective-permute-start.1 = (f32[144,128]{1,0:T(8,128)S(1)}, f32[144,128]{1,0:T(8,128)S(1)}, u32[]{:S(2)}, u32[]{:S(2)}) collective-permute-start(f32[144,128]{1,0:T(8,128)S(1)} %get-tuple-element.38), channel_id=1, source_target_pairs={{0,16},{8,24},{16,32},{24,40},{32,48},{40,56},{48,0},{56,8},{1,17}... | collective-permute-start | bytes 221192 | tf_op jit(solution)/shard_map/ppermute | solution.py:288
  28.0 2.6 %collective-permute-start.2 = (f32[144,128]{1,0:T(8,128)S(1)}, f32[144,128]{1,0:T(8,128)S(1)}, u32[]{:S(2)}, u32[]{:S(2)}) collective-permute-start(f32[144,128]{1,0:T(8,128)S(1)} %get-tuple-element.37), channel_id=1, source_target_pairs={{0,32},{8,40},{16,48},{24,56},{32,0},{40,8},{48,16},{56,24},{1,33}... | collective-permute-start | bytes 221192 | tf_op jit(solution)/shard_map/ppermute | solution.py:288
  30.6 1.1 %collective-permute-start.3 = (f32[144,128]{1,0:T(8,128)S(1)}, f32[144,128]{1,0:T(8,128)S(1)}, u32[]{:S(2)}, u32[]{:S(2)}) collective-permute-start(f32[144,128]{1,0:T(8,128)S(1)} %get-tuple-element.36), channel_id=1, source_target_pairs={{0,48},{8,56},{16,0},{24,8},{32,16},{40,24},{48,32},{56,40},{1,49}... | collective-permute-start | bytes 221192 | tf_op jit(solution)/shard_map/ppermute | solution.py:288
  31.7 2.2 %collective-permute-done.2.z2_ref = f32[144,128]{1,0:T(8,128)S(1)} collective-permute-done((f32[144,128]{1,0:T(8,128)S(1)}, f32[144,128]{1,0:T(8,128)S(1)}, u32[]{:S(2)}, u32[]{:S(2)}) %collective-permute-start.2) | collective-permute-done | bytes 73760 | tf_op jit(solution)/shard_map/ppermute | solution.py:288
  34.5 13.7 %all_to_all.21.v_ref = f32[32,16,128]{2,1,0:T(8,128)S(1)} all-to-all(f32[32,16,128]{2,1,0:T(8,128)S(1)} %get-tuple-element.21), channel_id=1, replica_groups={{0,1,2,3,4,5,6,7,16,17,18,19,20,21,22,23,32,33,34,35,36,37,38,39,48,49,..., dimensions={0} | all-to-all | bytes 524288 | tf_op jit(solution)/shard_map/all_to_all | solution.py:279
  48.3 4.1 %collective-permute-start.4 = (f32[32,256]{1,0:T(8,128)S(1)}, f32[32,256]{1,0:T(8,128)S(1)}, u32[]{:S(2)}, u32[]{:S(2)}) collective-permute-start(f32[32,256]{1,0:T(8,128)S(1)} %shard_map.54.mine_ref), channel_id=1, source_target_pairs={{0,8},{8,0},{16,24},{24,16},{32,40},{40,32},{48,56},{56,48},{1,9},... | collective-permute-start | bytes 98312 | tf_op jit(solution)/shard_map/ppermute | solution.py:283
  52.4 0.8 shard_map.55
  53.3 1.2 %shard_map.56 = (f32[40,128]{1,0:T(8,128)S(1)}, f32[40,128]{1,0:T(8,128)S(1)}, f32[40,128]{1,0:T(8,128)S(1)}, f32[40,128]{1,0:T(8,128)S(1)}, f32[32,128]{1,0:T(8,128)S(1)}) custom-call(f32[32,256]{1,0:T(8,128)S(1)} %shard_map.54.mine_ref, f32[32,256]{1,0:T(8,128)S(1)} %collective-permute-done.4.other_ref, f32[32,32]{1,0:T(8,128)S(1)} %get-tuple-element.24.inv_ref, ...), custom_call_target="tpu_custom_call" | custom-call | tf_op jit(solution)/shard_map/pallas_call | solution.py:267
  54.4 0.4 collective-permute-start.5
  54.8 1.7 %collective-permute-start.6 = (f32[40,128]{1,0:T(8,128)S(1)}, f32[40,128]{1,0:T(8,128)S(1)}, u32[]{:S(2)}, u32[]{:S(2)}) collective-permute-start(f32[40,128]{1,0:T(8,128)S(1)} %get-tuple-element.28), channel_id=1, source_target_pairs={{0,128},{64,192},{128,0},{192,64},{1,129},{65,193},{129,1},{193,65... | collective-permute-start | bytes 61448 | tf_op jit(solution)/shard_map/ppermute | solution.py:288
  56.6 1.0 %collective-permute-start.7 = (f32[40,128]{1,0:T(8,128)S(1)}, f32[40,128]{1,0:T(8,128)S(1)}, u32[]{:S(2)}, u32[]{:S(2)}) collective-permute-start(f32[40,128]{1,0:T(8,128)S(1)} %get-tuple-element.29), channel_id=1, source_target_pairs={{0,192},{64,0},{128,64},{192,128},{1,193},{65,1},{129,65},{193,129... | collective-permute-start | bytes 61448 | tf_op jit(solution)/shard_map/ppermute | solution.py:288
  57.6 0.8 collective-permute-done.5.p1_ref
  58.4 0.6 collective-permute-done.6.p2_ref
  59.0 0.5 collective-permute-done.7.p3_ref
  59.5 10.5 %all_to_all.22.refs_0_ = f32[8,32,128]{2,1,0:T(8,128)S(1)} all-to-all(f32[8,32,128]{2,1,0:T(8,128)S(1)} %get-tuple-element.30), channel_id=1, replica_groups=mesh['ia'=4,'ja'=8,'ka'=8] {'ka'}, dimensions={0} | all-to-all | bytes 262144 | tf_op jit(solution)/shard_map/all_to_all | solution.py:279
  70.1 1.1 %shard_map.58 = (f32[160,128]{1,0:T(8,128)S(1)}, f32[32,128]{1,0:T(8,128)S(1)}) custom-call(f32[8,32,128]{2,1,0:T(8,128)S(1)} %all_to_all.22.refs_0_, f32[8,128]{1,0:T(8,128)S(1)} %get-tuple-element.31.refs_1_, f32[32,32]{1,0:T(8,128)S(1)} %get-tuple-element.32.refs_2_), custom_call_target="tpu_custom_call" | custom-call | tf_op jit(solution)/shard_map/pallas_call | solution.py:267
  71.2 15.0 %all_to_all.23 = f32[32,1,640]{2,1,0:T(1,128)S(1)} all-to-all(f32[32,1,640]{2,1,0:T(1,128)S(1)} %bitcast.15), channel_id=1, replica_groups=mesh['ia'=4,'ja'=8,'ka'=8] {'ia','ja'}, dimensions={0} | all-to-all | bytes 163840 | tf_op jit(solution)/shard_map/all_to_all | solution.py:279
  86.2 0.7 shard_map.59
  (9 shorter events, 0.9 us)
Async XLA Ops:
  0.6 21.7 %copy-start = (bf16[8,512,512]{2,1,0:T(8,128)(2,1)S(1)}, bf16[8,512,512]{2,1,0:T(8,128)(2,1)}, u32[]{:S(2)}) copy-start(bf16[8,512,512]{2,1,0:T(8,128)(2,1)} %t_ref.1) | copy-start | bytes 12582916
  23.2 3.4 %collective-permute-start = (f32[4,144,128]{2,1,0:T(8,128)S(1)}, f32[4,144,128]{2,1,0:T(8,128)S(1)}, u32[]{:S(2)}, u32[]{:S(2)}) collective-permute-start(f32[4,144,128]{2,1,0:T(8,128)S(1)} %get-tuple-element.20), channel_id=1, source_target_pairs={{0,8},{8,0},{16,24},{24,16},{32,40},{40,32},{48,56},{56,48},{1,9},... | collective-permute-start | bytes 884744 | tf_op jit(solution)/shard_map/ppermute | solution.py:283
  26.6 5.1 %collective-permute-start.1 = (f32[144,128]{1,0:T(8,128)S(1)}, f32[144,128]{1,0:T(8,128)S(1)}, u32[]{:S(2)}, u32[]{:S(2)}) collective-permute-start(f32[144,128]{1,0:T(8,128)S(1)} %get-tuple-element.38), channel_id=1, source_target_pairs={{0,16},{8,24},{16,32},{24,40},{32,48},{40,56},{48,0},{56,8},{1,17}... | collective-permute-start | bytes 221192 | tf_op jit(solution)/shard_map/ppermute | solution.py:288
  28.0 5.9 %collective-permute-start.2 = (f32[144,128]{1,0:T(8,128)S(1)}, f32[144,128]{1,0:T(8,128)S(1)}, u32[]{:S(2)}, u32[]{:S(2)}) collective-permute-start(f32[144,128]{1,0:T(8,128)S(1)} %get-tuple-element.37), channel_id=1, source_target_pairs={{0,32},{8,40},{16,48},{24,56},{32,0},{40,8},{48,16},{56,24},{1,33}... | collective-permute-start | bytes 221192 | tf_op jit(solution)/shard_map/ppermute | solution.py:288
  30.6 3.5 %collective-permute-start.3 = (f32[144,128]{1,0:T(8,128)S(1)}, f32[144,128]{1,0:T(8,128)S(1)}, u32[]{:S(2)}, u32[]{:S(2)}) collective-permute-start(f32[144,128]{1,0:T(8,128)S(1)} %get-tuple-element.36), channel_id=1, source_target_pairs={{0,48},{8,56},{16,0},{24,8},{32,16},{40,24},{48,32},{56,40},{1,49}... | collective-permute-start | bytes 221192 | tf_op jit(solution)/shard_map/ppermute | solution.py:288
  48.3 4.9 %collective-permute-start.4 = (f32[32,256]{1,0:T(8,128)S(1)}, f32[32,256]{1,0:T(8,128)S(1)}, u32[]{:S(2)}, u32[]{:S(2)}) collective-permute-start(f32[32,256]{1,0:T(8,128)S(1)} %shard_map.54.mine_ref), channel_id=1, source_target_pairs={{0,8},{8,0},{16,24},{24,16},{32,40},{40,32},{48,56},{56,48},{1,9},... | collective-permute-start | bytes 98312 | tf_op jit(solution)/shard_map/ppermute | solution.py:283
  54.4 3.9 %collective-permute-start.5 = (f32[40,128]{1,0:T(8,128)S(1)}, f32[40,128]{1,0:T(8,128)S(1)}, u32[]{:S(2)}, u32[]{:S(2)}) collective-permute-start(f32[40,128]{1,0:T(8,128)S(1)} %get-tuple-element.27), channel_id=1, source_target_pairs={{0,64},{64,128},{128,192},{192,0},{1,65},{65,129},{129,193},{193,1... | collective-permute-start | bytes 61448 | tf_op jit(solution)/shard_map/ppermute | solution.py:288
  54.8 4.1 %collective-permute-start.6 = (f32[40,128]{1,0:T(8,128)S(1)}, f32[40,128]{1,0:T(8,128)S(1)}, u32[]{:S(2)}, u32[]{:S(2)}) collective-permute-start(f32[40,128]{1,0:T(8,128)S(1)} %get-tuple-element.28), channel_id=1, source_target_pairs={{0,128},{64,192},{128,0},{192,64},{1,129},{65,193},{129,1},{193,65... | collective-permute-start | bytes 61448 | tf_op jit(solution)/shard_map/ppermute | solution.py:288
  56.6 2.9 %collective-permute-start.7 = (f32[40,128]{1,0:T(8,128)S(1)}, f32[40,128]{1,0:T(8,128)S(1)}, u32[]{:S(2)}, u32[]{:S(2)}) collective-permute-start(f32[40,128]{1,0:T(8,128)S(1)} %get-tuple-element.29), channel_id=1, source_target_pairs={{0,192},{64,0},{128,64},{192,128},{1,193},{65,1},{129,65},{193,129... | collective-permute-start | bytes 61448 | tf_op jit(solution)/shard_map/ppermute | solution.py:288

commit v9 on v8

--- a/solution.py
+++ b/solution.py
@@ -117,27 +117,22 @@
     extra = extra_ref[...]
     high, low = split(b)
 
-    def placed(part, q):
-        zeros = jnp.zeros((RANK, 512), jnp.bfloat16)
-        return [part if n == q else zeros for n in range(4)]
-
-    weights = jnp.concatenate(
-        [jnp.concatenate(placed(high, q) + placed(low, q), axis=0) for q in range(4)], axis=1
-    )
+    left = jnp.concatenate([high, low], axis=0)
     core = 1 - ja % 2 if other else ja % 2
     starts = [pl.multiple_of(64 * (2 * ((ja // 2 + n) % 4) + core), 64) for n in range(4)]
-    for h in range(2):
-        left = jnp.concatenate(
-            [
-                jnp.concatenate([t_ref[4 * h + q, pl.ds(start, 64), :] for start in starts], axis=0)
-                for q in range(4)
-            ],
-            axis=1,
-        )
-        both = lax.dot_general(left, weights, NT, preferred_element_type=F32)
-        y = both[:, :LANES] + both[:, LANES:]
-        for n in range(4):
-            out_ref[n, 64 * h : 64 * h + 64, :] = y[64 * n : 64 * n + 64]
+    low_lanes = iota((RANK, LANES), 1) < 64
+    right = jnp.concatenate(
+        [t_ref[k, pl.ds(start, 64), :] for k in range(8) for start in starts], axis=0
+    )
+    both = lax.dot_general(left, right, NT, preferred_element_type=F32)
+    both = both[:RANK] + both[RANK:]
+    for pair in range(4):
+        products = [both[:, 512 * pair : 512 * pair + 256], both[:, 512 * pair + 256 : 512 * pair + 512]]
+        rows = slice(32 * pair, 32 * pair + 32)
+        for v in range(2):
+            one, two = (x[:, 128 * v : 128 * v + 128] for x in products)
+            out_ref[2 * v, rows, :] = jnp.where(low_lanes, one, pltpu.roll(two, 64, 1))
+            out_ref[2 * v + 1, rows, :] = jnp.where(low_lanes, pltpu.roll(one, 64, 1), two)
     for n in range(4):
         out_ref[n, 128:144, :] = extra
 
@@ -154,17 +149,14 @@
     c_all_ref[...] = pltpu.roll(extra, 64, 1)[:, :64]
     c_here = pltpu.roll(extra, 64 - 8 * ka, 1)
     c_ref[...] = c_here
-    c_t = c_here.T[:8]
-    c_tiled = jnp.concatenate([c_t] * 4, axis=1)
-    which = iota((8, LANES), 0) - iota((8, LANES), 1) // 32
-    acc = None
-    for h in range(2):
-        weight = jnp.sum(jnp.where(which == 4 * h, c_tiled, 0.0), axis=0, keepdims=True)
-        term = z[64 * h : 64 * h + 64] * weight
-        acc = term if acc is None else acc + term
-    acc = acc + pltpu.roll(acc, 64, 1)
-    acc = acc + pltpu.roll(acc, 32, 1)
-    u = fold(acc)
+    low_lanes = iota((RANK, LANES), 1) < 64
+    m = None
+    for pair in range(4):
+        first, second = c_here[:, 2 * pair : 2 * pair + 1], c_here[:, 2 * pair + 1 : 2 * pair + 2]
+        term = z[32 * pair : 32 * pair + 32] * jnp.where(low_lanes, first, second)
+        m = term if m is None else m + term
+    m = m + pltpu.roll(m, 64, 1)
+    u = jnp.where(low_lanes[:16], m[:16], m[16:])
     for n in range(32):
         u_ref[n] = u
 
@@ -176,13 +168,17 @@
 
 
 def turn_kernel(v_ref, m_ref):
+    low_lanes = iota((16, LANES), 1) < 64
     parts = []
     for y in range(4):
         part = v_ref[8 * y]
         for ka in range(1, 8):
             part = part + v_ref[8 * y + ka]
-        parts.append(unfold(part))
-    m_ref[...] = jnp.concatenate(parts, axis=0).T
+        parts.append(part)
+    for p in range(2):
+        one, two = parts[2 * p], parts[2 * p + 1]
+        m_ref[:16, 128 * p : 128 * p + 128] = jnp.where(low_lanes, one, pltpu.roll(two, 64, 1))
+        m_ref[16:, 128 * p : 128 * p + 128] = jnp.where(low_lanes, pltpu.roll(one, 64, 1), two)
 
 
 def second_kernel(
@@ -232,8 +228,8 @@
     half = lax.axis_index("ka") % 2
     gram = unfold(gram_ref[...])
     diag = jnp.where(iota(gram.shape, 0) == iota(gram.shape, 1), gram, 0.0)
-    scale_col = 1.0 / jnp.sqrt(jnp.sum(diag, axis=1, keepdims=True) / total_i + EPS)
-    scale_row = 1.0 / jnp.sqrt(jnp.sum(diag, axis=0, keepdims=True) / total_i + EPS)
+    scale_col = lax.rsqrt(jnp.sum(diag, axis=1, keepdims=True) / total_i + EPS)
+    scale_row = lax.rsqrt(jnp.sum(diag, axis=0, keepdims=True) / total_i + EPS)
     inv = inverse(gram * scale_col * scale_row * gram_c_ref[...])
     scale_ref[...] = jnp.broadcast_to(scale_col, (RANK, LANES))
     m = total(u_ref) * scale_col

time: 87.1 us -> 87 us (level)
  no operation moved by 1% of the time
where the time goes in v9:
time: 87 us; the launch traced here: 86.8 us
  blocking collectives  59.9 us (69%)
  starting transfers between devices  14.4 us (17%)
  Pallas kernels  6.86 us (8%)
  waiting for transfers between devices  4.76 us (5%)
    all_to_all x4, blocking collectives, exchange(): return lax.all_to_all(x, axes, 0, 0, tiled=True, axis_index_groups=groups)  59.9 us
    ppermute x6, starting transfers between devices, turned(): return lax.ppermute(x, axis, [(n, (n + step) % size) for n in range(size)])  8.18 us
    pallas_call x10, Pallas kernels, call(): pl.pallas_call(kernel, out_shape=[jax.ShapeDtypeStruct(s, F32) for s in o...  6.86 us
    ppermute x2, starting transfers between devices, other_core(): return lax.ppermute(x, 'ja', [(n, n ^ 1) for n in range(8)])  6.27 us
    ppermute x6, waiting for transfers between devices, turned(): return lax.ppermute(x, axis, [(n, (n + step) % size) for n in range(size)])  4.37 us
  transfers between devices with their start and end apart: 8, of which 7 were waited for; matrix products, arithmetic and copies ran while one was open for 0% of the time, Pallas kernels for 2%

profile of v9, /device:TPU:1, one launch (start us, length us, event | category | flops | bytes accessed | tf_op | source)
XLA Modules:
  0.0 86.8 jit_solution(6863444893953798817)
XLA Ops:
  0.6 0.9 %shard_map.50 = f32[160,128]{1,0:T(8,128)S(1)} custom-call(f32[8,64]{1,0:T(8,128)} %b_hbm.1, f32[1,8]{1,0:T(1,128)} %c_hbm.1), custom_call_target="tpu_custom_call" | custom-call | flops 10000000000 | tf_op jit(solution)/shard_map/pallas_call | solution.py:263
  1.6 20.7 %all_to_all.20 = f32[32,1,640]{2,1,0:T(1,128)S(1)} all-to-all(f32[32,1,640]{2,1,0:T(1,128)S(1)} %bitcast.16), channel_id=1, replica_groups=mesh['ia'=4,'ja'=8,'ka'=8] {'ia','ka'}, dimensions={0} | all-to-all | bytes 163840 | tf_op jit(solution)/shard_map/all_to_all | solution.py:275
  22.3 0.9 %shard_map.51 = (f32[4,144,128]{2,1,0:T(8,128)S(1)}, f32[16,128]{1,0:T(8,128)S(1)}) custom-call(f32[160,128]{1,0:T(8,128)S(1)} %bitcast.12, bf16[8,512,512]{2,1,0:T(8,128)(2,1)S(1)} %copy-done), custom_call_target="tpu_custom_call" | custom-call | tf_op jit(solution)/shard_map/pallas_call | solution.py:263
  23.2 2.2 %collective-permute-start = (f32[4,144,128]{2,1,0:T(8,128)S(1)}, f32[4,144,128]{2,1,0:T(8,128)S(1)}, u32[]{:S(2)}, u32[]{:S(2)}) collective-permute-start(f32[4,144,128]{2,1,0:T(8,128)S(1)} %get-tuple-element.20), channel_id=1, source_target_pairs={{0,8},{8,0},{16,24},{24,16},{32,40},{40,32},{48,56},{56,48},{1,9},... | collective-permute-start | bytes 884744 | tf_op jit(solution)/shard_map/ppermute | solution.py:279
  25.4 0.9 shard_map.52
  26.3 0.3 collective-permute-done
  26.7 1.4 %collective-permute-start.1 = (f32[144,128]{1,0:T(8,128)S(1)}, f32[144,128]{1,0:T(8,128)S(1)}, u32[]{:S(2)}, u32[]{:S(2)}) collective-permute-start(f32[144,128]{1,0:T(8,128)S(1)} %get-tuple-element.38), channel_id=1, source_target_pairs={{0,16},{8,24},{16,32},{24,40},{32,48},{40,56},{48,0},{56,8},{1,17}... | collective-permute-start | bytes 221192 | tf_op jit(solution)/shard_map/ppermute | solution.py:284
  28.0 2.6 %collective-permute-start.2 = (f32[144,128]{1,0:T(8,128)S(1)}, f32[144,128]{1,0:T(8,128)S(1)}, u32[]{:S(2)}, u32[]{:S(2)}) collective-permute-start(f32[144,128]{1,0:T(8,128)S(1)} %get-tuple-element.37), channel_id=1, source_target_pairs={{0,32},{8,40},{16,48},{24,56},{32,0},{40,8},{48,16},{56,24},{1,33}... | collective-permute-start | bytes 221192 | tf_op jit(solution)/shard_map/ppermute | solution.py:284
  30.7 1.1 %collective-permute-start.3 = (f32[144,128]{1,0:T(8,128)S(1)}, f32[144,128]{1,0:T(8,128)S(1)}, u32[]{:S(2)}, u32[]{:S(2)}) collective-permute-start(f32[144,128]{1,0:T(8,128)S(1)} %get-tuple-element.36), channel_id=1, source_target_pairs={{0,48},{8,56},{16,0},{24,8},{32,16},{40,24},{48,32},{56,40},{1,49}... | collective-permute-start | bytes 221192 | tf_op jit(solution)/shard_map/ppermute | solution.py:284
  31.7 2.2 %collective-permute-done.2.z2_ref = f32[144,128]{1,0:T(8,128)S(1)} collective-permute-done((f32[144,128]{1,0:T(8,128)S(1)}, f32[144,128]{1,0:T(8,128)S(1)}, u32[]{:S(2)}, u32[]{:S(2)}) %collective-permute-start.2) | collective-permute-done | bytes 73760 | tf_op jit(solution)/shard_map/ppermute | solution.py:284
  34.5 13.7 %all_to_all.21.v_ref = f32[32,16,128]{2,1,0:T(8,128)S(1)} all-to-all(f32[32,16,128]{2,1,0:T(8,128)S(1)} %get-tuple-element.21), channel_id=1, replica_groups={{0,1,2,3,4,5,6,7,16,17,18,19,20,21,22,23,32,33,34,35,36,37,38,39,48,49,..., dimensions={0} | all-to-all | bytes 524288 | tf_op jit(solution)/shard_map/all_to_all | solution.py:275
  48.2 4.1 %collective-permute-start.4 = (f32[32,256]{1,0:T(8,128)S(1)}, f32[32,256]{1,0:T(8,128)S(1)}, u32[]{:S(2)}, u32[]{:S(2)}) collective-permute-start(f32[32,256]{1,0:T(8,128)S(1)} %shard_map.54.mine_ref), channel_id=1, source_target_pairs={{0,8},{8,0},{16,24},{24,16},{32,40},{40,32},{48,56},{56,48},{1,9},... | collective-permute-start | bytes 98312 | tf_op jit(solution)/shard_map/ppermute | solution.py:279
  52.3 0.8 shard_map.55
  53.2 1.2 %shard_map.56 = (f32[40,128]{1,0:T(8,128)S(1)}, f32[40,128]{1,0:T(8,128)S(1)}, f32[40,128]{1,0:T(8,128)S(1)}, f32[40,128]{1,0:T(8,128)S(1)}, f32[32,128]{1,0:T(8,128)S(1)}) custom-call(f32[32,256]{1,0:T(8,128)S(1)} %shard_map.54.mine_ref, f32[32,256]{1,0:T(8,128)S(1)} %collective-permute-done.4.other_ref, f32[32,32]{1,0:T(8,128)S(1)} %get-tuple-element.24.inv_ref, ...), custom_call_target="tpu_custom_call" | custom-call | tf_op jit(solution)/shard_map/pallas_call | solution.py:263
  54.3 0.4 collective-permute-start.5
  54.8 1.7 %collective-permute-start.6 = (f32[40,128]{1,0:T(8,128)S(1)}, f32[40,128]{1,0:T(8,128)S(1)}, u32[]{:S(2)}, u32[]{:S(2)}) collective-permute-start(f32[40,128]{1,0:T(8,128)S(1)} %get-tuple-element.28), channel_id=1, source_target_pairs={{0,128},{64,192},{128,0},{192,64},{1,129},{65,193},{129,1},{193,65... | collective-permute-start | bytes 61448 | tf_op jit(solution)/shard_map/ppermute | solution.py:284
  56.5 1.0 %collective-permute-start.7 = (f32[40,128]{1,0:T(8,128)S(1)}, f32[40,128]{1,0:T(8,128)S(1)}, u32[]{:S(2)}, u32[]{:S(2)}) collective-permute-start(f32[40,128]{1,0:T(8,128)S(1)} %get-tuple-element.29), channel_id=1, source_target_pairs={{0,192},{64,0},{128,64},{192,128},{1,193},{65,1},{129,65},{193,129... | collective-permute-start | bytes 61448 | tf_op jit(solution)/shard_map/ppermute | solution.py:284
  57.5 0.8 collective-permute-done.5.p1_ref
  58.3 0.6 collective-permute-done.6.p2_ref
  58.9 0.5 collective-permute-done.7.p3_ref
  59.4 10.5 %all_to_all.22.refs_0_ = f32[8,32,128]{2,1,0:T(8,128)S(1)} all-to-all(f32[8,32,128]{2,1,0:T(8,128)S(1)} %get-tuple-element.30), channel_id=1, replica_groups=mesh['ia'=4,'ja'=8,'ka'=8] {'ka'}, dimensions={0} | all-to-all | bytes 262144 | tf_op jit(solution)/shard_map/all_to_all | solution.py:275
  70.0 1.1 %shard_map.58 = (f32[160,128]{1,0:T(8,128)S(1)}, f32[32,128]{1,0:T(8,128)S(1)}) custom-call(f32[8,32,128]{2,1,0:T(8,128)S(1)} %all_to_all.22.refs_0_, f32[8,128]{1,0:T(8,128)S(1)} %get-tuple-element.31.refs_1_, f32[32,32]{1,0:T(8,128)S(1)} %get-tuple-element.32.refs_2_), custom_call_target="tpu_custom_call" | custom-call | tf_op jit(solution)/shard_map/pallas_call | solution.py:263
  71.1 15.0 %all_to_all.23 = f32[32,1,640]{2,1,0:T(1,128)S(1)} all-to-all(f32[32,1,640]{2,1,0:T(1,128)S(1)} %bitcast.15), channel_id=1, replica_groups=mesh['ia'=4,'ja'=8,'ka'=8] {'ia','ja'}, dimensions={0} | all-to-all | bytes 163840 | tf_op jit(solution)/shard_map/all_to_all | solution.py:275
  86.1 0.7 shard_map.59
  (9 shorter events, 0.7 us)
Async XLA Ops:
  0.6 21.7 %copy-start = (bf16[8,512,512]{2,1,0:T(8,128)(2,1)S(1)}, bf16[8,512,512]{2,1,0:T(8,128)(2,1)}, u32[]{:S(2)}) copy-start(bf16[8,512,512]{2,1,0:T(8,128)(2,1)} %t_ref.1) | copy-start | bytes 12582916
  23.2 3.4 %collective-permute-start = (f32[4,144,128]{2,1,0:T(8,128)S(1)}, f32[4,144,128]{2,1,0:T(8,128)S(1)}, u32[]{:S(2)}, u32[]{:S(2)}) collective-permute-start(f32[4,144,128]{2,1,0:T(8,128)S(1)} %get-tuple-element.20), channel_id=1, source_target_pairs={{0,8},{8,0},{16,24},{24,16},{32,40},{40,32},{48,56},{56,48},{1,9},... | collective-permute-start | bytes 884744 | tf_op jit(solution)/shard_map/ppermute | solution.py:279
  26.7 5.1 %collective-permute-start.1 = (f32[144,128]{1,0:T(8,128)S(1)}, f32[144,128]{1,0:T(8,128)S(1)}, u32[]{:S(2)}, u32[]{:S(2)}) collective-permute-start(f32[144,128]{1,0:T(8,128)S(1)} %get-tuple-element.38), channel_id=1, source_target_pairs={{0,16},{8,24},{16,32},{24,40},{32,48},{40,56},{48,0},{56,8},{1,17}... | collective-permute-start | bytes 221192 | tf_op jit(solution)/shard_map/ppermute | solution.py:284
  28.0 5.9 %collective-permute-start.2 = (f32[144,128]{1,0:T(8,128)S(1)}, f32[144,128]{1,0:T(8,128)S(1)}, u32[]{:S(2)}, u32[]{:S(2)}) collective-permute-start(f32[144,128]{1,0:T(8,128)S(1)} %get-tuple-element.37), channel_id=1, source_target_pairs={{0,32},{8,40},{16,48},{24,56},{32,0},{40,8},{48,16},{56,24},{1,33}... | collective-permute-start | bytes 221192 | tf_op jit(solution)/shard_map/ppermute | solution.py:284
  30.7 3.5 %collective-permute-start.3 = (f32[144,128]{1,0:T(8,128)S(1)}, f32[144,128]{1,0:T(8,128)S(1)}, u32[]{:S(2)}, u32[]{:S(2)}) collective-permute-start(f32[144,128]{1,0:T(8,128)S(1)} %get-tuple-element.36), channel_id=1, source_target_pairs={{0,48},{8,56},{16,0},{24,8},{32,16},{40,24},{48,32},{56,40},{1,49}... | collective-permute-start | bytes 221192 | tf_op jit(solution)/shard_map/ppermute | solution.py:284
  48.2 4.9 %collective-permute-start.4 = (f32[32,256]{1,0:T(8,128)S(1)}, f32[32,256]{1,0:T(8,128)S(1)}, u32[]{:S(2)}, u32[]{:S(2)}) collective-permute-start(f32[32,256]{1,0:T(8,128)S(1)} %shard_map.54.mine_ref), channel_id=1, source_target_pairs={{0,8},{8,0},{16,24},{24,16},{32,40},{40,32},{48,56},{56,48},{1,9},... | collective-permute-start | bytes 98312 | tf_op jit(solution)/shard_map/ppermute | solution.py:279
  54.3 3.9 %collective-permute-start.5 = (f32[40,128]{1,0:T(8,128)S(1)}, f32[40,128]{1,0:T(8,128)S(1)}, u32[]{:S(2)}, u32[]{:S(2)}) collective-permute-start(f32[40,128]{1,0:T(8,128)S(1)} %get-tuple-element.27), channel_id=1, source_target_pairs={{0,64},{64,128},{128,192},{192,0},{1,65},{65,129},{129,193},{193,1... | collective-permute-start | bytes 61448 | tf_op jit(solution)/shard_map/ppermute | solution.py:284
  54.8 4.1 %collective-permute-start.6 = (f32[40,128]{1,0:T(8,128)S(1)}, f32[40,128]{1,0:T(8,128)S(1)}, u32[]{:S(2)}, u32[]{:S(2)}) collective-permute-start(f32[40,128]{1,0:T(8,128)S(1)} %get-tuple-element.28), channel_id=1, source_target_pairs={{0,128},{64,192},{128,0},{192,64},{1,129},{65,193},{129,1},{193,65... | collective-permute-start | bytes 61448 | tf_op jit(solution)/shard_map/ppermute | solution.py:284
  56.5 2.9 %collective-permute-start.7 = (f32[40,128]{1,0:T(8,128)S(1)}, f32[40,128]{1,0:T(8,128)S(1)}, u32[]{:S(2)}, u32[]{:S(2)}) collective-permute-start(f32[40,128]{1,0:T(8,128)S(1)} %get-tuple-element.29), channel_id=1, source_target_pairs={{0,192},{64,0},{128,64},{192,128},{1,193},{65,1},{129,65},{193,129... | collective-permute-start | bytes 61448 | tf_op jit(solution)/shard_map/ppermute | solution.py:284

commit v10 on v8

--- a/solution.py
+++ b/solution.py
@@ -109,9 +109,9 @@
         extra_ref[:8] = folded_gram(b)
         row = iota((8, LANES), 0)
         c_rows = jnp.zeros((8, LANES), F32)
+        c_parts = y_ref[pl.ds(4, 32, stride=5), :]
         for ia in range(4):
-            starts = [5 * (8 * ia + ka) + 4 for ka in range(8)]
-            c_row = sum(y_ref[start : start + 1] for start in starts)
+            c_row = jnp.sum(c_parts[8 * ia : 8 * ia + 8], axis=0, keepdims=True)
             c_rows = jnp.where(row == 4 * (ja % 2) + ia, c_row, c_rows)
         extra_ref[8:] = c_rows
     extra = extra_ref[...]
@@ -232,8 +232,8 @@
     half = lax.axis_index("ka") % 2
     gram = unfold(gram_ref[...])
     diag = jnp.where(iota(gram.shape, 0) == iota(gram.shape, 1), gram, 0.0)
-    scale_col = 1.0 / jnp.sqrt(jnp.sum(diag, axis=1, keepdims=True) / total_i + EPS)
-    scale_row = 1.0 / jnp.sqrt(jnp.sum(diag, axis=0, keepdims=True) / total_i + EPS)
+    scale_col = lax.rsqrt(jnp.sum(diag, axis=1, keepdims=True) / total_i + EPS)
+    scale_row = lax.rsqrt(jnp.sum(diag, axis=0, keepdims=True) / total_i + EPS)
     inv = inverse(gram * scale_col * scale_row * gram_c_ref[...])
     scale_ref[...] = jnp.broadcast_to(scale_col, (RANK, LANES))
     m = total(u_ref) * scale_col

time: 87.1 us -> 87.1 us (level)
  no operation moved by 1% of the time
where the time goes in v10:
time: 87.1 us; the launch traced here: 86.8 us
  blocking collectives  59.9 us (69%)
  starting transfers between devices  14.4 us (17%)
  Pallas kernels  6.9 us (8%)
  waiting for transfers between devices  4.83 us (6%)
    all_to_all x4, blocking collectives, exchange(): return lax.all_to_all(x, axes, 0, 0, tiled=True, axis_index_groups=groups)  59.9 us
    ppermute x6, starting transfers between devices, turned(): return lax.ppermute(x, axis, [(n, (n + step) % size) for n in range(size)])  8.18 us
    pallas_call x10, Pallas kernels, call(): pl.pallas_call(kernel, out_shape=[jax.ShapeDtypeStruct(s, F32) for s in o...  6.9 us
    ppermute x2, starting transfers between devices, other_core(): return lax.ppermute(x, 'ja', [(n, n ^ 1) for n in range(8)])  6.24 us
    ppermute x6, waiting for transfers between devices, turned(): return lax.ppermute(x, axis, [(n, (n + step) % size) for n in range(size)])  4.37 us
  transfers between devices with their start and end apart: 8, of which 7 were waited for; matrix products, arithmetic and copies ran while one was open for 0% of the time, Pallas kernels for 2%

profile of v10, /device:TPU:1, one launch (start us, length us, event | category | flops | bytes accessed | tf_op | source)
XLA Modules:
  0.0 86.8 jit_solution(17879055914468868992)
XLA Ops:
  0.6 0.9 %shard_map.50 = f32[160,128]{1,0:T(8,128)S(1)} custom-call(f32[8,64]{1,0:T(8,128)} %b_hbm.1, f32[1,8]{1,0:T(1,128)} %c_hbm.1), custom_call_target="tpu_custom_call" | custom-call | flops 10000000000 | tf_op jit(solution)/shard_map/pallas_call | solution.py:267
  1.6 20.7 %all_to_all.20 = f32[32,1,640]{2,1,0:T(1,128)S(1)} all-to-all(f32[32,1,640]{2,1,0:T(1,128)S(1)} %bitcast.16), channel_id=1, replica_groups=mesh['ia'=4,'ja'=8,'ka'=8] {'ia','ka'}, dimensions={0} | all-to-all | bytes 163840 | tf_op jit(solution)/shard_map/all_to_all | solution.py:279
  22.3 0.8 shard_map.51
  23.2 2.2 %collective-permute-start = (f32[4,144,128]{2,1,0:T(8,128)S(1)}, f32[4,144,128]{2,1,0:T(8,128)S(1)}, u32[]{:S(2)}, u32[]{:S(2)}) collective-permute-start(f32[4,144,128]{2,1,0:T(8,128)S(1)} %get-tuple-element.20), channel_id=1, source_target_pairs={{0,8},{8,0},{16,24},{24,16},{32,40},{40,32},{48,56},{56,48},{1,9},... | collective-permute-start | bytes 884744 | tf_op jit(solution)/shard_map/ppermute | solution.py:283
  25.4 0.8 shard_map.52
  26.1 0.4 collective-permute-done
  26.6 1.4 %collective-permute-start.1 = (f32[144,128]{1,0:T(8,128)S(1)}, f32[144,128]{1,0:T(8,128)S(1)}, u32[]{:S(2)}, u32[]{:S(2)}) collective-permute-start(f32[144,128]{1,0:T(8,128)S(1)} %get-tuple-element.38), channel_id=1, source_target_pairs={{0,16},{8,24},{16,32},{24,40},{32,48},{40,56},{48,0},{56,8},{1,17}... | collective-permute-start | bytes 221192 | tf_op jit(solution)/shard_map/ppermute | solution.py:288
  28.0 2.6 %collective-permute-start.2 = (f32[144,128]{1,0:T(8,128)S(1)}, f32[144,128]{1,0:T(8,128)S(1)}, u32[]{:S(2)}, u32[]{:S(2)}) collective-permute-start(f32[144,128]{1,0:T(8,128)S(1)} %get-tuple-element.37), channel_id=1, source_target_pairs={{0,32},{8,40},{16,48},{24,56},{32,0},{40,8},{48,16},{56,24},{1,33}... | collective-permute-start | bytes 221192 | tf_op jit(solution)/shard_map/ppermute | solution.py:288
  30.6 1.1 %collective-permute-start.3 = (f32[144,128]{1,0:T(8,128)S(1)}, f32[144,128]{1,0:T(8,128)S(1)}, u32[]{:S(2)}, u32[]{:S(2)}) collective-permute-start(f32[144,128]{1,0:T(8,128)S(1)} %get-tuple-element.36), channel_id=1, source_target_pairs={{0,48},{8,56},{16,0},{24,8},{32,16},{40,24},{48,32},{56,40},{1,49}... | collective-permute-start | bytes 221192 | tf_op jit(solution)/shard_map/ppermute | solution.py:288
  31.7 2.2 %collective-permute-done.2.z2_ref = f32[144,128]{1,0:T(8,128)S(1)} collective-permute-done((f32[144,128]{1,0:T(8,128)S(1)}, f32[144,128]{1,0:T(8,128)S(1)}, u32[]{:S(2)}, u32[]{:S(2)}) %collective-permute-start.2) | collective-permute-done | bytes 73760 | tf_op jit(solution)/shard_map/ppermute | solution.py:288
  34.5 13.7 %all_to_all.21.v_ref = f32[32,16,128]{2,1,0:T(8,128)S(1)} all-to-all(f32[32,16,128]{2,1,0:T(8,128)S(1)} %get-tuple-element.21), channel_id=1, replica_groups={{0,1,2,3,4,5,6,7,16,17,18,19,20,21,22,23,32,33,34,35,36,37,38,39,48,49,..., dimensions={0} | all-to-all | bytes 524288 | tf_op jit(solution)/shard_map/all_to_all | solution.py:279
  48.3 4.1 %collective-permute-start.4 = (f32[32,256]{1,0:T(8,128)S(1)}, f32[32,256]{1,0:T(8,128)S(1)}, u32[]{:S(2)}, u32[]{:S(2)}) collective-permute-start(f32[32,256]{1,0:T(8,128)S(1)} %shard_map.54.mine_ref), channel_id=1, source_target_pairs={{0,8},{8,0},{16,24},{24,16},{32,40},{40,32},{48,56},{56,48},{1,9},... | collective-permute-start | bytes 98312 | tf_op jit(solution)/shard_map/ppermute | solution.py:283
  52.4 0.8 shard_map.55
  53.3 1.2 %shard_map.56 = (f32[40,128]{1,0:T(8,128)S(1)}, f32[40,128]{1,0:T(8,128)S(1)}, f32[40,128]{1,0:T(8,128)S(1)}, f32[40,128]{1,0:T(8,128)S(1)}, f32[32,128]{1,0:T(8,128)S(1)}) custom-call(f32[32,256]{1,0:T(8,128)S(1)} %shard_map.54.mine_ref, f32[32,256]{1,0:T(8,128)S(1)} %collective-permute-done.4.other_ref, f32[32,32]{1,0:T(8,128)S(1)} %get-tuple-element.24.inv_ref, ...), custom_call_target="tpu_custom_call" | custom-call | tf_op jit(solution)/shard_map/pallas_call | solution.py:267
  54.4 0.4 collective-permute-start.5
  54.8 1.7 %collective-permute-start.6 = (f32[40,128]{1,0:T(8,128)S(1)}, f32[40,128]{1,0:T(8,128)S(1)}, u32[]{:S(2)}, u32[]{:S(2)}) collective-permute-start(f32[40,128]{1,0:T(8,128)S(1)} %get-tuple-element.28), channel_id=1, source_target_pairs={{0,128},{64,192},{128,0},{192,64},{1,129},{65,193},{129,1},{193,65... | collective-permute-start | bytes 61448 | tf_op jit(solution)/shard_map/ppermute | solution.py:288
  56.6 1.0 %collective-permute-start.7 = (f32[40,128]{1,0:T(8,128)S(1)}, f32[40,128]{1,0:T(8,128)S(1)}, u32[]{:S(2)}, u32[]{:S(2)}) collective-permute-start(f32[40,128]{1,0:T(8,128)S(1)} %get-tuple-element.29), channel_id=1, source_target_pairs={{0,192},{64,0},{128,64},{192,128},{1,193},{65,1},{129,65},{193,129... | collective-permute-start | bytes 61448 | tf_op jit(solution)/shard_map/ppermute | solution.py:288
  57.6 0.8 collective-permute-done.5.p1_ref
  58.4 0.6 collective-permute-done.6.p2_ref
  59.0 0.5 collective-permute-done.7.p3_ref
  59.5 10.5 %all_to_all.22.refs_0_ = f32[8,32,128]{2,1,0:T(8,128)S(1)} all-to-all(f32[8,32,128]{2,1,0:T(8,128)S(1)} %get-tuple-element.30), channel_id=1, replica_groups=mesh['ia'=4,'ja'=8,'ka'=8] {'ka'}, dimensions={0} | all-to-all | bytes 262144 | tf_op jit(solution)/shard_map/all_to_all | solution.py:279
  70.1 1.1 %shard_map.58 = (f32[160,128]{1,0:T(8,128)S(1)}, f32[32,128]{1,0:T(8,128)S(1)}) custom-call(f32[8,32,128]{2,1,0:T(8,128)S(1)} %all_to_all.22.refs_0_, f32[8,128]{1,0:T(8,128)S(1)} %get-tuple-element.31.refs_1_, f32[32,32]{1,0:T(8,128)S(1)} %get-tuple-element.32.refs_2_), custom_call_target="tpu_custom_call" | custom-call | tf_op jit(solution)/shard_map/pallas_call | solution.py:267
  71.2 15.0 %all_to_all.23 = f32[32,1,640]{2,1,0:T(1,128)S(1)} all-to-all(f32[32,1,640]{2,1,0:T(1,128)S(1)} %bitcast.15), channel_id=1, replica_groups=mesh['ia'=4,'ja'=8,'ka'=8] {'ia','ja'}, dimensions={0} | all-to-all | bytes 163840 | tf_op jit(solution)/shard_map/all_to_all | solution.py:279
  86.2 0.7 shard_map.59
  (9 shorter events, 0.9 us)
Async XLA Ops:
  0.6 21.7 %copy-start = (bf16[8,512,512]{2,1,0:T(8,128)(2,1)S(1)}, bf16[8,512,512]{2,1,0:T(8,128)(2,1)}, u32[]{:S(2)}) copy-start(bf16[8,512,512]{2,1,0:T(8,128)(2,1)} %t_ref.1) | copy-start | bytes 12582916
  23.2 3.4 %collective-permute-start = (f32[4,144,128]{2,1,0:T(8,128)S(1)}, f32[4,144,128]{2,1,0:T(8,128)S(1)}, u32[]{:S(2)}, u32[]{:S(2)}) collective-permute-start(f32[4,144,128]{2,1,0:T(8,128)S(1)} %get-tuple-element.20), channel_id=1, source_target_pairs={{0,8},{8,0},{16,24},{24,16},{32,40},{40,32},{48,56},{56,48},{1,9},... | collective-permute-start | bytes 884744 | tf_op jit(solution)/shard_map/ppermute | solution.py:283
  26.6 5.1 %collective-permute-start.1 = (f32[144,128]{1,0:T(8,128)S(1)}, f32[144,128]{1,0:T(8,128)S(1)}, u32[]{:S(2)}, u32[]{:S(2)}) collective-permute-start(f32[144,128]{1,0:T(8,128)S(1)} %get-tuple-element.38), channel_id=1, source_target_pairs={{0,16},{8,24},{16,32},{24,40},{32,48},{40,56},{48,0},{56,8},{1,17}... | collective-permute-start | bytes 221192 | tf_op jit(solution)/shard_map/ppermute | solution.py:288
  28.0 5.9 %collective-permute-start.2 = (f32[144,128]{1,0:T(8,128)S(1)}, f32[144,128]{1,0:T(8,128)S(1)}, u32[]{:S(2)}, u32[]{:S(2)}) collective-permute-start(f32[144,128]{1,0:T(8,128)S(1)} %get-tuple-element.37), channel_id=1, source_target_pairs={{0,32},{8,40},{16,48},{24,56},{32,0},{40,8},{48,16},{56,24},{1,33}... | collective-permute-start | bytes 221192 | tf_op jit(solution)/shard_map/ppermute | solution.py:288
  30.6 3.5 %collective-permute-start.3 = (f32[144,128]{1,0:T(8,128)S(1)}, f32[144,128]{1,0:T(8,128)S(1)}, u32[]{:S(2)}, u32[]{:S(2)}) collective-permute-start(f32[144,128]{1,0:T(8,128)S(1)} %get-tuple-element.36), channel_id=1, source_target_pairs={{0,48},{8,56},{16,0},{24,8},{32,16},{40,24},{48,32},{56,40},{1,49}... | collective-permute-start | bytes 221192 | tf_op jit(solution)/shard_map/ppermute | solution.py:288
  48.3 4.9 %collective-permute-start.4 = (f32[32,256]{1,0:T(8,128)S(1)}, f32[32,256]{1,0:T(8,128)S(1)}, u32[]{:S(2)}, u32[]{:S(2)}) collective-permute-start(f32[32,256]{1,0:T(8,128)S(1)} %shard_map.54.mine_ref), channel_id=1, source_target_pairs={{0,8},{8,0},{16,24},{24,16},{32,40},{40,32},{48,56},{56,48},{1,9},... | collective-permute-start | bytes 98312 | tf_op jit(solution)/shard_map/ppermute | solution.py:283
  54.4 3.9 %collective-permute-start.5 = (f32[40,128]{1,0:T(8,128)S(1)}, f32[40,128]{1,0:T(8,128)S(1)}, u32[]{:S(2)}, u32[]{:S(2)}) collective-permute-start(f32[40,128]{1,0:T(8,128)S(1)} %get-tuple-element.27), channel_id=1, source_target_pairs={{0,64},{64,128},{128,192},{192,0},{1,65},{65,129},{129,193},{193,1... | collective-permute-start | bytes 61448 | tf_op jit(solution)/shard_map/ppermute | solution.py:288
  54.8 4.1 %collective-permute-start.6 = (f32[40,128]{1,0:T(8,128)S(1)}, f32[40,128]{1,0:T(8,128)S(1)}, u32[]{:S(2)}, u32[]{:S(2)}) collective-permute-start(f32[40,128]{1,0:T(8,128)S(1)} %get-tuple-element.28), channel_id=1, source_target_pairs={{0,128},{64,192},{128,0},{192,64},{1,129},{65,193},{129,1},{193,65... | collective-permute-start | bytes 61448 | tf_op jit(solution)/shard_map/ppermute | solution.py:288
  56.6 2.9 %collective-permute-start.7 = (f32[40,128]{1,0:T(8,128)S(1)}, f32[40,128]{1,0:T(8,128)S(1)}, u32[]{:S(2)}, u32[]{:S(2)}) collective-permute-start(f32[40,128]{1,0:T(8,128)S(1)} %get-tuple-element.29), channel_id=1, source_target_pairs={{0,192},{64,0},{128,64},{192,128},{1,193},{65,1},{129,65},{193,129... | collective-permute-start | bytes 61448 | tf_op jit(solution)/shard_map/ppermute | solution.py:288

commit v11 on v10

--- a/solution.py
+++ b/solution.py
@@ -86,8 +86,9 @@
     c_row = jnp.where(lane // 8 == 8 + lax.axis_index("ka"), c_tiled, 0.0)
     b_pairs = jnp.concatenate([b_ref[:4], b_ref[4:]], axis=1)
     tile = jnp.concatenate([b_pairs, c_row], axis=0)
-    for n in range(32):
-        y_ref[5 * n : 5 * n + 5] = tile
+    block = jnp.concatenate([tile] * 8, axis=0)
+    for n in range(4):
+        y_ref[40 * n : 40 * n + 40] = block
 
 
 def first_kernel(other, y_ref, t_ref, *refs):
@@ -258,7 +259,7 @@
     ss_row = jnp.sum(ss_ref[pl.ds(4, 32, stride=5), :], axis=0, keepdims=True)
     ss = jnp.sum(jnp.where(place, ss_row, 0.0), axis=1, keepdims=True)
     data = ss_ref[pl.ds(5 * (8 * (ka // 2) + ja), 4), :]
-    b = jnp.concatenate([data, pltpu.roll(data, 64, 1)], axis=0) / jnp.sqrt(ss / total_j + EPS)
+    b = jnp.concatenate([data, pltpu.roll(data, 64, 1)], axis=0) * lax.rsqrt(ss / total_j + EPS)
     out_b_ref[...] = b[:, :64]
     out_a_ref[...] = pltpu.roll(a_ref[...] * scale_ref[...], (32 - 4 * ja) % 32, 0)[:4, :64]
 

time: 87.1 us -> 87.1 us (level)
  no operation moved by 1% of the time
where the time goes in v11:
time: 87.1 us; the launch traced here: 86.8 us
  blocking collectives  59.9 us (69%)
  starting transfers between devices  14.4 us (17%)
  Pallas kernels  6.89 us (8%)
  waiting for transfers between devices  4.83 us (6%)
    all_to_all x4, blocking collectives, exchange(): return lax.all_to_all(x, axes, 0, 0, tiled=True, axis_index_groups=groups)  59.9 us
    ppermute x6, starting transfers between devices, turned(): return lax.ppermute(x, axis, [(n, (n + step) % size) for n in range(size)])  8.18 us
    pallas_call x10, Pallas kernels, call(): pl.pallas_call(kernel, out_shape=[jax.ShapeDtypeStruct(s, F32) for s in o...  6.89 us
    ppermute x2, starting transfers between devices, other_core(): return lax.ppermute(x, 'ja', [(n, n ^ 1) for n in range(8)])  6.24 us
    ppermute x6, waiting for transfers between devices, turned(): return lax.ppermute(x, axis, [(n, (n + step) % size) for n in range(size)])  4.37 us
  transfers between devices with their start and end apart: 8, of which 7 were waited for; matrix products, arithmetic and copies ran while one was open for 0% of the time, Pallas kernels for 2%

profile of v11, /device:TPU:1, one launch (start us, length us, event | category | flops | bytes accessed | tf_op | source)
XLA Modules:
  0.0 86.8 jit_solution(17235117711162877299)
XLA Ops:
  0.6 0.9 %shard_map.50 = f32[160,128]{1,0:T(8,128)S(1)} custom-call(f32[8,64]{1,0:T(8,128)} %b_hbm.1, f32[1,8]{1,0:T(1,128)} %c_hbm.1), custom_call_target="tpu_custom_call" | custom-call | flops 10000000000 | tf_op jit(solution)/shard_map/pallas_call | solution.py:268
  1.6 20.7 %all_to_all.20 = f32[32,1,640]{2,1,0:T(1,128)S(1)} all-to-all(f32[32,1,640]{2,1,0:T(1,128)S(1)} %bitcast.16), channel_id=1, replica_groups=mesh['ia'=4,'ja'=8,'ka'=8] {'ia','ka'}, dimensions={0} | all-to-all | bytes 163840 | tf_op jit(solution)/shard_map/all_to_all | solution.py:280
  22.3 0.8 shard_map.51
  23.2 2.2 %collective-permute-start = (f32[4,144,128]{2,1,0:T(8,128)S(1)}, f32[4,144,128]{2,1,0:T(8,128)S(1)}, u32[]{:S(2)}, u32[]{:S(2)}) collective-permute-start(f32[4,144,128]{2,1,0:T(8,128)S(1)} %get-tuple-element.20), channel_id=1, source_target_pairs={{0,8},{8,0},{16,24},{24,16},{32,40},{40,32},{48,56},{56,48},{1,9},... | collective-permute-start | bytes 884744 | tf_op jit(solution)/shard_map/ppermute | solution.py:284
  25.4 0.8 shard_map.52
  26.1 0.4 collective-permute-done
  26.6 1.4 %collective-permute-start.1 = (f32[144,128]{1,0:T(8,128)S(1)}, f32[144,128]{1,0:T(8,128)S(1)}, u32[]{:S(2)}, u32[]{:S(2)}) collective-permute-start(f32[144,128]{1,0:T(8,128)S(1)} %get-tuple-element.38), channel_id=1, source_target_pairs={{0,16},{8,24},{16,32},{24,40},{32,48},{40,56},{48,0},{56,8},{1,17}... | collective-permute-start | bytes 221192 | tf_op jit(solution)/shard_map/ppermute | solution.py:289
  28.0 2.6 %collective-permute-start.2 = (f32[144,128]{1,0:T(8,128)S(1)}, f32[144,128]{1,0:T(8,128)S(1)}, u32[]{:S(2)}, u32[]{:S(2)}) collective-permute-start(f32[144,128]{1,0:T(8,128)S(1)} %get-tuple-element.37), channel_id=1, source_target_pairs={{0,32},{8,40},{16,48},{24,56},{32,0},{40,8},{48,16},{56,24},{1,33}... | collective-permute-start | bytes 221192 | tf_op jit(solution)/shard_map/ppermute | solution.py:289
  30.6 1.1 %collective-permute-start.3 = (f32[144,128]{1,0:T(8,128)S(1)}, f32[144,128]{1,0:T(8,128)S(1)}, u32[]{:S(2)}, u32[]{:S(2)}) collective-permute-start(f32[144,128]{1,0:T(8,128)S(1)} %get-tuple-element.36), channel_id=1, source_target_pairs={{0,48},{8,56},{16,0},{24,8},{32,16},{40,24},{48,32},{56,40},{1,49}... | collective-permute-start | bytes 221192 | tf_op jit(solution)/shard_map/ppermute | solution.py:289
  31.7 2.2 %collective-permute-done.2.z2_ref = f32[144,128]{1,0:T(8,128)S(1)} collective-permute-done((f32[144,128]{1,0:T(8,128)S(1)}, f32[144,128]{1,0:T(8,128)S(1)}, u32[]{:S(2)}, u32[]{:S(2)}) %collective-permute-start.2) | collective-permute-done | bytes 73760 | tf_op jit(solution)/shard_map/ppermute | solution.py:289
  34.5 13.7 %all_to_all.21.v_ref = f32[32,16,128]{2,1,0:T(8,128)S(1)} all-to-all(f32[32,16,128]{2,1,0:T(8,128)S(1)} %get-tuple-element.21), channel_id=1, replica_groups={{0,1,2,3,4,5,6,7,16,17,18,19,20,21,22,23,32,33,34,35,36,37,38,39,48,49,..., dimensions={0} | all-to-all | bytes 524288 | tf_op jit(solution)/shard_map/all_to_all | solution.py:280
  48.3 4.1 %collective-permute-start.4 = (f32[32,256]{1,0:T(8,128)S(1)}, f32[32,256]{1,0:T(8,128)S(1)}, u32[]{:S(2)}, u32[]{:S(2)}) collective-permute-start(f32[32,256]{1,0:T(8,128)S(1)} %shard_map.54.mine_ref), channel_id=1, source_target_pairs={{0,8},{8,0},{16,24},{24,16},{32,40},{40,32},{48,56},{56,48},{1,9},... | collective-permute-start | bytes 98312 | tf_op jit(solution)/shard_map/ppermute | solution.py:284
  52.4 0.8 shard_map.55
  53.3 1.2 %shard_map.56 = (f32[40,128]{1,0:T(8,128)S(1)}, f32[40,128]{1,0:T(8,128)S(1)}, f32[40,128]{1,0:T(8,128)S(1)}, f32[40,128]{1,0:T(8,128)S(1)}, f32[32,128]{1,0:T(8,128)S(1)}) custom-call(f32[32,256]{1,0:T(8,128)S(1)} %shard_map.54.mine_ref, f32[32,256]{1,0:T(8,128)S(1)} %collective-permute-done.4.other_ref, f32[32,32]{1,0:T(8,128)S(1)} %get-tuple-element.24.inv_ref, ...), custom_call_target="tpu_custom_call" | custom-call | tf_op jit(solution)/shard_map/pallas_call | solution.py:268
  54.4 0.4 collective-permute-start.5
  54.8 1.7 %collective-permute-start.6 = (f32[40,128]{1,0:T(8,128)S(1)}, f32[40,128]{1,0:T(8,128)S(1)}, u32[]{:S(2)}, u32[]{:S(2)}) collective-permute-start(f32[40,128]{1,0:T(8,128)S(1)} %get-tuple-element.28), channel_id=1, source_target_pairs={{0,128},{64,192},{128,0},{192,64},{1,129},{65,193},{129,1},{193,65... | collective-permute-start | bytes 61448 | tf_op jit(solution)/shard_map/ppermute | solution.py:289
  56.6 1.0 %collective-permute-start.7 = (f32[40,128]{1,0:T(8,128)S(1)}, f32[40,128]{1,0:T(8,128)S(1)}, u32[]{:S(2)}, u32[]{:S(2)}) collective-permute-start(f32[40,128]{1,0:T(8,128)S(1)} %get-tuple-element.29), channel_id=1, source_target_pairs={{0,192},{64,0},{128,64},{192,128},{1,193},{65,1},{129,65},{193,129... | collective-permute-start | bytes 61448 | tf_op jit(solution)/shard_map/ppermute | solution.py:289
  57.5 0.8 collective-permute-done.5.p1_ref
  58.4 0.6 collective-permute-done.6.p2_ref
  59.0 0.5 collective-permute-done.7.p3_ref
  59.5 10.5 %all_to_all.22.refs_0_ = f32[8,32,128]{2,1,0:T(8,128)S(1)} all-to-all(f32[8,32,128]{2,1,0:T(8,128)S(1)} %get-tuple-element.30), channel_id=1, replica_groups=mesh['ia'=4,'ja'=8,'ka'=8] {'ka'}, dimensions={0} | all-to-all | bytes 262144 | tf_op jit(solution)/shard_map/all_to_all | solution.py:280
  70.1 1.1 %shard_map.58 = (f32[160,128]{1,0:T(8,128)S(1)}, f32[32,128]{1,0:T(8,128)S(1)}) custom-call(f32[8,32,128]{2,1,0:T(8,128)S(1)} %all_to_all.22.refs_0_, f32[8,128]{1,0:T(8,128)S(1)} %get-tuple-element.31.refs_1_, f32[32,32]{1,0:T(8,128)S(1)} %get-tuple-element.32.refs_2_), custom_call_target="tpu_custom_call" | custom-call | tf_op jit(solution)/shard_map/pallas_call | solution.py:268
  71.2 15.0 %all_to_all.23 = f32[32,1,640]{2,1,0:T(1,128)S(1)} all-to-all(f32[32,1,640]{2,1,0:T(1,128)S(1)} %bitcast.15), channel_id=1, replica_groups=mesh['ia'=4,'ja'=8,'ka'=8] {'ia','ja'}, dimensions={0} | all-to-all | bytes 163840 | tf_op jit(solution)/shard_map/all_to_all | solution.py:280
  86.2 0.7 shard_map.59
  (9 shorter events, 0.9 us)
Async XLA Ops:
  0.6 21.7 %copy-start = (bf16[8,512,512]{2,1,0:T(8,128)(2,1)S(1)}, bf16[8,512,512]{2,1,0:T(8,128)(2,1)}, u32[]{:S(2)}) copy-start(bf16[8,512,512]{2,1,0:T(8,128)(2,1)} %t_ref.1) | copy-start | bytes 12582916
  23.2 3.4 %collective-permute-start = (f32[4,144,128]{2,1,0:T(8,128)S(1)}, f32[4,144,128]{2,1,0:T(8,128)S(1)}, u32[]{:S(2)}, u32[]{:S(2)}) collective-permute-start(f32[4,144,128]{2,1,0:T(8,128)S(1)} %get-tuple-element.20), channel_id=1, source_target_pairs={{0,8},{8,0},{16,24},{24,16},{32,40},{40,32},{48,56},{56,48},{1,9},... | collective-permute-start | bytes 884744 | tf_op jit(solution)/shard_map/ppermute | solution.py:284
  26.6 5.1 %collective-permute-start.1 = (f32[144,128]{1,0:T(8,128)S(1)}, f32[144,128]{1,0:T(8,128)S(1)}, u32[]{:S(2)}, u32[]{:S(2)}) collective-permute-start(f32[144,128]{1,0:T(8,128)S(1)} %get-tuple-element.38), channel_id=1, source_target_pairs={{0,16},{8,24},{16,32},{24,40},{32,48},{40,56},{48,0},{56,8},{1,17}... | collective-permute-start | bytes 221192 | tf_op jit(solution)/shard_map/ppermute | solution.py:289
  28.0 5.9 %collective-permute-start.2 = (f32[144,128]{1,0:T(8,128)S(1)}, f32[144,128]{1,0:T(8,128)S(1)}, u32[]{:S(2)}, u32[]{:S(2)}) collective-permute-start(f32[144,128]{1,0:T(8,128)S(1)} %get-tuple-element.37), channel_id=1, source_target_pairs={{0,32},{8,40},{16,48},{24,56},{32,0},{40,8},{48,16},{56,24},{1,33}... | collective-permute-start | bytes 221192 | tf_op jit(solution)/shard_map/ppermute | solution.py:289
  30.6 3.5 %collective-permute-start.3 = (f32[144,128]{1,0:T(8,128)S(1)}, f32[144,128]{1,0:T(8,128)S(1)}, u32[]{:S(2)}, u32[]{:S(2)}) collective-permute-start(f32[144,128]{1,0:T(8,128)S(1)} %get-tuple-element.36), channel_id=1, source_target_pairs={{0,48},{8,56},{16,0},{24,8},{32,16},{40,24},{48,32},{56,40},{1,49}... | collective-permute-start | bytes 221192 | tf_op jit(solution)/shard_map/ppermute | solution.py:289
  48.3 4.9 %collective-permute-start.4 = (f32[32,256]{1,0:T(8,128)S(1)}, f32[32,256]{1,0:T(8,128)S(1)}, u32[]{:S(2)}, u32[]{:S(2)}) collective-permute-start(f32[32,256]{1,0:T(8,128)S(1)} %shard_map.54.mine_ref), channel_id=1, source_target_pairs={{0,8},{8,0},{16,24},{24,16},{32,40},{40,32},{48,56},{56,48},{1,9},... | collective-permute-start | bytes 98312 | tf_op jit(solution)/shard_map/ppermute | solution.py:284
  54.4 3.9 %collective-permute-start.5 = (f32[40,128]{1,0:T(8,128)S(1)}, f32[40,128]{1,0:T(8,128)S(1)}, u32[]{:S(2)}, u32[]{:S(2)}) collective-permute-start(f32[40,128]{1,0:T(8,128)S(1)} %get-tuple-element.27), channel_id=1, source_target_pairs={{0,64},{64,128},{128,192},{192,0},{1,65},{65,129},{129,193},{193,1... | collective-permute-start | bytes 61448 | tf_op jit(solution)/shard_map/ppermute | solution.py:289
  54.8 4.1 %collective-permute-start.6 = (f32[40,128]{1,0:T(8,128)S(1)}, f32[40,128]{1,0:T(8,128)S(1)}, u32[]{:S(2)}, u32[]{:S(2)}) collective-permute-start(f32[40,128]{1,0:T(8,128)S(1)} %get-tuple-element.28), channel_id=1, source_target_pairs={{0,128},{64,192},{128,0},{192,64},{1,129},{65,193},{129,1},{193,65... | collective-permute-start | bytes 61448 | tf_op jit(solution)/shard_map/ppermute | solution.py:289
  56.6 2.9 %collective-permute-start.7 = (f32[40,128]{1,0:T(8,128)S(1)}, f32[40,128]{1,0:T(8,128)S(1)}, u32[]{:S(2)}, u32[]{:S(2)}) collective-permute-start(f32[40,128]{1,0:T(8,128)S(1)} %get-tuple-element.29), channel_id=1, source_target_pairs={{0,192},{64,0},{128,64},{192,128},{1,193},{65,1},{129,65},{193,129... | collective-permute-start | bytes 61448 | tf_op jit(solution)/shard_map/ppermute | solution.py:289
